TPU v7x, 512 devices: a whole 4x8x8 slice. The times are simulated.
512 devices in a mesh: gx: 16 (over z_lo, y), gy: 8 (over x, core), gz: 4 (over z_hi).
Axes of the slice: x: 4, y: 8, z: 8 (z_hi: 4, z_lo: 2; z = z_hi * 2 + z_lo), core: 2. Of those that a mesh axis runs over, the one named last changes fastest.
Arguments:
- offsets: bfloat16 [3, 48, 4096], replicated, may hold values from -0.14941406 to 0.14941406
- displacement: float32 [384, 3, 256, 512], P('gx', None, 'gy', 'gz'), may hold values from -0.25 to 0.25
- adjoint: float32 [384, 3, 256, 512], P('gx', None, 'gy', 'gz'), may hold values from -1.5 to 1.5
- span_x: int32 [384], replicated, may hold values from 0 to 44, never falling along the last dimension, each value on 1 to 18 neighbouring positions
- span_y: int32 [256], replicated, may hold values from 0 to 60, never falling along the last dimension, each value on 1 to 9 neighbouring positions
- span_z: int32 [512], replicated, may hold values from 0 to 60, never falling along the last dimension, each value on 1 to 17 neighbouring positions
Outputs:
- control_gradient: float32 [3, 48, 4096], replicated
Inputs may be any that keep to these rules, and one draw needn't show every extreme that they name: span_x never falls along the node lines; each span 0 to 44 holds 1 to 18 node lines. span_y never falls; each span 0 to 60 holds 1 to 9 node lines. span_z never falls; each span 0 to 60 holds 1 to 17 node lines.
All inputs are finite; a program needn't handle non-finite values.
Results may differ from a plain program's by a relative error of at most 0.0003.
Values sent between devices are 32-bit elements; how exact they have to be, the bound alone decides.
No kernel may reach another device: no remote copies, remote signals or barrier semaphores. Data moves between devices by JAX's collectives and lax.ppermute only.
A program may use at most 128 MiB of HBM per device.

v0:
```python
import jax
import jax.numpy as jnp
from jax import lax
from jax.sharding import PartitionSpec as P

NCX = 48
NCY = 64
NCZ = 64


MU_SHEAR = 40.0
LAME_FIRST = 60.0
TAPER_RATE = 0.8
HIGHEST_PRECISION = lax.Precision.HIGHEST


def passed_along(value, axis, steps):
    count = lax.axis_size(axis)
    initial, last = (max(0, -steps), min(count, count - steps))
    return lax.ppermute(value, axis, [(source, source + steps) for source in range(initial, last)])


def basis_matrix(span_table, first_row, row_count, col_count):
    all_rows = jnp.arange(span_table.shape[0], dtype=jnp.int32)
    own_rows = first_row + jnp.arange(row_count, dtype=jnp.int32)
    own_spans = lax.dynamic_slice_in_dim(span_table, first_row, row_count)
    matches = span_table[None, :] == own_spans[:, None]
    counted = jnp.sum(matches.astype(jnp.float32), axis=1)
    earlier = jnp.sum(
        (matches & (all_rows[None, :] < own_rows[:, None])).astype(jnp.float32), axis=1
    )
    local_param = (earlier + 0.5) / counted
    complement = 1.0 - local_param
    square = local_param * local_param
    param_cube = square * local_param
    weights = [
        complement * complement * complement / 6.0,
        (3.0 * param_cube - 6.0 * square + 4.0) / 6.0,
        (-3.0 * param_cube + 3.0 * square + 3.0 * local_param + 1.0) / 6.0,
        param_cube / 6.0,
    ]
    columns = jnp.arange(col_count, dtype=jnp.int32)
    offset_table = columns[None, :] - own_spans[:, None]
    matrix = jnp.zeros((row_count, col_count), jnp.float32)
    for degree_term in range(4):
        matrix = matrix + jnp.where(offset_table == degree_term, weights[degree_term][:, None], 0.0)
    return matrix


def control_points(offsets, node_x, node_y, node_z):
    offset_grid = offsets.astype(jnp.float32).reshape(3, NCX, NCY, NCZ)
    along_x = jnp.arange(NCX, dtype=jnp.float32)[:, None, None]
    across_y = jnp.arange(NCY, dtype=jnp.float32)[None, :, None]
    through_z = jnp.arange(NCZ, dtype=jnp.float32)[None, None, :]
    step_x = 2.0 * node_x / (NCX - 3)
    step_y = 2.0 * node_y / (NCY - 3)
    step_z = 2.0 * node_z / (NCZ - 3)
    taper_scale = 1.0 + TAPER_RATE * along_x / (NCX - 1)
    coord_x = step_x * (along_x + offset_grid[0])
    coord_y = step_y * (taper_scale * (across_y - 0.5 * (NCY - 1)) + offset_grid[1])
    coord_z = step_z * (taper_scale * (through_z - 0.5 * (NCZ - 1)) + offset_grid[2])
    return jnp.stack([coord_x, coord_y, coord_z])


def node_positions(points, basis_x, basis_y, basis_z):
    partial_x = jnp.einsum("cabz,ia->icbz", points, basis_x, precision=HIGHEST_PRECISION)
    partial_y = jnp.einsum("icbz,jb->icjz", partial_x, basis_y, precision=HIGHEST_PRECISION)
    return jnp.einsum("icjz,kz->icjk", partial_y, basis_z, precision=HIGHEST_PRECISION)


def control_terms(node_grad, basis_x, basis_y, basis_z):
    along_z = jnp.einsum("icjk,kz->icjz", node_grad, basis_z, precision=HIGHEST_PRECISION)
    along_y = jnp.einsum("icjz,jb->icbz", along_z, basis_y, precision=HIGHEST_PRECISION)
    return jnp.einsum("icbz,ia->cabz", along_y, basis_x, precision=HIGHEST_PRECISION)


def derivatives(lower_values, upper_values):
    y_count = lower_values.shape[1] - 1
    z_count = lower_values.shape[2] - 1

    def corner(values, shift_y, shift_z):
        return values[shift_y : shift_y + y_count, shift_z : shift_z + z_count]

    result = []
    for component in range(lower_values.shape[0]):
        lower_field = lower_values[component]
        upper_field = upper_values[component]
        d_first = (
            corner(upper_field, 0, 0)
            + corner(upper_field, 0, 1)
            + corner(upper_field, 1, 0)
            + corner(upper_field, 1, 1)
            - corner(lower_field, 0, 0)
            - corner(lower_field, 0, 1)
            - corner(lower_field, 1, 0)
            - corner(lower_field, 1, 1)
        ) * 0.125
        d_second = (
            corner(lower_field, 1, 0)
            + corner(lower_field, 1, 1)
            + corner(upper_field, 1, 0)
            + corner(upper_field, 1, 1)
            - corner(lower_field, 0, 0)
            - corner(lower_field, 0, 1)
            - corner(upper_field, 0, 0)
            - corner(upper_field, 0, 1)
        ) * 0.125
        d_third = (
            corner(lower_field, 0, 1)
            + corner(lower_field, 1, 1)
            + corner(upper_field, 0, 1)
            + corner(upper_field, 1, 1)
            - corner(lower_field, 0, 0)
            - corner(lower_field, 1, 0)
            - corner(upper_field, 0, 0)
            - corner(upper_field, 1, 0)
        ) * 0.125
        result.append([d_first, d_second, d_third])
    return result


def invert(matrix):

    def cofactor(row_index, col_index):
        keep_rows = [other for other in range(3) if other != row_index]
        keep_cols = [other for other in range(3) if other != col_index]
        minor_value = (
            matrix[keep_rows[0]][keep_cols[0]] * matrix[keep_rows[1]][keep_cols[1]]
            - matrix[keep_rows[0]][keep_cols[1]] * matrix[keep_rows[1]][keep_cols[0]]
        )
        return minor_value if (row_index + col_index) % 2 == 0 else -minor_value

    cofactors = [
        [cofactor(row_index, col_index) for col_index in range(3)] for row_index in range(3)
    ]
    determinant = (
        matrix[0][0] * cofactors[0][0]
        + matrix[0][1] * cofactors[0][1]
        + matrix[0][2] * cofactors[0][2]
    )
    inverse = [
        [cofactors[col_index][row_index] / determinant for col_index in range(3)]
        for row_index in range(3)
    ]
    return (determinant, inverse)


def product(left_matrix, right_matrix):
    return [
        [
            left_matrix[row_index][0] * right_matrix[0][col_index]
            + left_matrix[row_index][1] * right_matrix[1][col_index]
            + left_matrix[row_index][2] * right_matrix[2][col_index]
            for col_index in range(3)
        ]
        for row_index in range(3)
    ]


def layer_terms(lower_pos, upper_pos, lower_rest, upper_rest, live_mask, counted):
    jacobian = derivatives(lower_pos, upper_pos)
    disp_grad = derivatives(lower_rest[:3], upper_rest[:3])
    adj_grad = derivatives(lower_rest[3:], upper_rest[3:])
    jacobian = [
        [
            jnp.where(
                live_mask, jacobian[row_index][col_index], 1.0 if row_index == col_index else 0.0
            )
            for col_index in range(3)
        ]
        for row_index in range(3)
    ]
    disp_grad = [
        [jnp.where(live_mask, disp_grad[row_index][col_index], 0.0) for col_index in range(3)]
        for row_index in range(3)
    ]
    adj_grad = [
        [jnp.where(live_mask, adj_grad[row_index][col_index], 0.0) for col_index in range(3)]
        for row_index in range(3)
    ]
    det_ref, inv_ref = invert(jacobian)
    strain = product(disp_grad, inv_ref)
    virtual = product(adj_grad, inv_ref)
    deform = [
        [
            strain[row_index][col_index] + (1.0 if row_index == col_index else 0.0)
            for col_index in range(3)
        ]
        for row_index in range(3)
    ]
    det_def, inv_def = invert(deform)
    log_det = jnp.log(det_def)
    stretch = 0.0
    virtual_work = 0.0
    for row_index in range(3):
        for col_index in range(3):
            stretch = stretch + deform[row_index][col_index] * deform[row_index][col_index]
            stress = (
                MU_SHEAR * (deform[row_index][col_index] - inv_def[col_index][row_index])
                + LAME_FIRST * log_det * inv_def[col_index][row_index]
            )
            virtual_work = virtual_work + stress * virtual[row_index][col_index]
    energy = 0.5 * MU_SHEAR * (stretch - 3.0 - 2.0 * log_det) + 0.5 * LAME_FIRST * log_det * log_det
    volume = 8.0 * det_ref
    lagrangian = jnp.sum(jnp.where(live_mask, volume * (energy - virtual_work), 0.0))
    total_volume = jnp.sum(jnp.where(counted, volume, 0.0))
    return (lagrangian, total_volume)


def layer_gradient(lower_nodes, upper_nodes, live_mask, counted):

    def lagrange(lower_pos, upper_pos):
        return layer_terms(
            lower_pos, upper_pos, lower_nodes[3:], upper_nodes[3:], live_mask, counted
        )

    lagrangian, pullback, volume = jax.vjp(lagrange, lower_nodes[:3], upper_nodes[:3], has_aux=True)
    grad_lower, grad_upper = pullback(jnp.ones_like(lagrangian))
    return (grad_lower, grad_upper, volume)


def on_device(offsets, displacement, adjoint, span_x, span_y, span_z):
    count_x = displacement.shape[0]
    count_y = displacement.shape[2]
    count_z = displacement.shape[3]
    nodes_x = span_x.shape[0]
    nodes_y = span_y.shape[0]
    nodes_z = span_z.shape[0]
    start_x = lax.axis_index("gx") * count_x
    start_y = lax.axis_index("gy") * count_y
    start_z = lax.axis_index("gz") * count_z
    points = control_points(offsets, nodes_x, nodes_y, nodes_z)
    basis_x = basis_matrix(span_x, start_x, count_x, NCX)
    basis_y = basis_matrix(span_y, start_y, count_y, NCY)
    basis_z = basis_matrix(span_z, start_z, count_z, NCZ)
    positions = node_positions(points, basis_x, basis_y, basis_z)
    fields = jnp.concatenate([positions, displacement, adjoint], axis=1)
    upper_x = passed_along(fields[:1], "gx", -1)
    extended = jnp.concatenate([fields, upper_x], axis=0)
    upper_y = passed_along(extended[:, :, :1], "gy", -1)
    extended = jnp.concatenate([extended, upper_y], axis=2)
    upper_z = passed_along(extended[:, :, :, :1], "gz", -1)
    extended = jnp.concatenate([extended, upper_z], axis=3)
    margin = 0
    layers = extended.shape[0] - 1
    local_y = jnp.arange(extended.shape[2] - 1, dtype=jnp.int32)
    local_z = jnp.arange(extended.shape[3] - 1, dtype=jnp.int32)
    global_y = start_y - margin + local_y
    global_z = start_z - margin + local_z
    live_y = (global_y >= 0) & (global_y < nodes_y - 1)
    live_z = (global_z >= 0) & (global_z < nodes_z - 1)
    live_plane = live_y[:, None] & live_z[None, :]
    owned_plane = live_plane & (local_y >= margin)[:, None] & (local_z >= margin)[None, :]

    def one_layer(inputs):
        lower_nodes, upper_nodes, layer_index = inputs
        global_x = start_x - margin + layer_index
        live_x = (global_x >= 0) & (global_x < nodes_x - 1)
        live_mask = live_plane & live_x
        counted = owned_plane & live_x & (layer_index >= margin)
        return layer_gradient(lower_nodes, upper_nodes, live_mask, counted)

    grad_lower, grad_upper, volumes = lax.map(
        one_layer, (extended[:-1], extended[1:], jnp.arange(layers, dtype=jnp.int32))
    )
    padding = jnp.zeros_like(grad_lower[:1])
    node_grad = jnp.concatenate([grad_lower, padding], axis=0) + jnp.concatenate(
        [padding, grad_upper], axis=0
    )
    received = passed_along(node_grad[:, :, :, count_z:], "gz", 1)
    node_grad = jnp.concatenate(
        [node_grad[:, :, :, :1] + received, node_grad[:, :, :, 1:count_z]], axis=3
    )
    received = passed_along(node_grad[:, :, count_y:], "gy", 1)
    node_grad = jnp.concatenate(
        [node_grad[:, :, :1] + received, node_grad[:, :, 1:count_y]], axis=2
    )
    received = passed_along(node_grad[count_x:], "gx", 1)
    own_grad = jnp.concatenate([node_grad[:1] + received, node_grad[1:count_x]], axis=0)
    volume = lax.psum(jnp.sum(volumes), ("gx", "gy", "gz"))
    elements = (nodes_x - 1) * (nodes_y - 1) * (nodes_z - 1)
    scaled = own_grad * (elements / volume)
    control = control_terms(scaled, basis_x, basis_y, basis_z)
    summed = lax.psum(control, ("gx", "gy", "gz"))
    return summed.reshape(3, NCX, NCY * NCZ)


def solution(mesh):
    placed = (P(), P("gx", None, "gy", "gz"), P("gx", None, "gy", "gz"), P(), P(), P())
    return jax.shard_map(on_device, mesh=mesh, in_specs=placed, out_specs=P(), check_vma=False)
```

profile of v0, /device:TPU:1, one launch (start us, length us, event | category | flops | bytes accessed | tf_op | source)
XLA Modules:
  0.0 781.1 jit_solution(13405371795327939920)
XLA Ops:
  14.1 2.2 fusion.93
  17.0 4.1 fusion.91
  21.2 2.5 fusion.78
  28.3 5.3 collective-permute-done
  33.7 9.4 %collective-permute-start.1 = (f32[25,9,1,128]{3,2,1,0:T(1,128)S(1)}, f32[25,9,1,128]{3,2,1,0:T(1,128)S(1)}, u32[]{:S(2)}, u32[]{:S(2)}) collective-permute-start(f32[25,9,1,128]{3,2,1,0:T(1,128)S(1)} %pad_maximum_fusion.7), channel_id=1, source_target_pairs={{4,0},{8,4},{12,8},{16,12},{20,16},{24,20},{28,24},{5,1},{9,5},{13... | collective-permute-start | bytes 345608 | tf_op jit(solution)/shard_map/ppermute | solution.py:20
  43.9 2.5 pad_maximum_fusion.1
  46.4 3.7 copy.32
  51.4 7.4 collective-permute-done.2
  58.8 3.4 copy.33
  62.2 3.7 pad_maximum_fusion
  66.0 6.8 fusion.249
  73.4 276.5 %while.18 = (s32[]{:T(128)}, f32[24,3,33,129]{3,2,1,0:T(8,128)S(1)}, f32[24,3,33,129]{3,2,1,0:T(8,128)}, f32[24]{0:T(128)}, s32[24]{0:T(128)}, /*index=5*/s32[]{...) while((s32[]{:T(128)}, ...), condition=%wide.region_8.9_spmd.clone, body=%wide.region_6.8_spmd.clone.sunk | while | flops 5689628 | bytes 8451959 | solution.py:263
  78.9 1.8 select_reduce_fusion.2
  90.4 1.8 select_reduce_fusion.2
  101.9 1.8 select_reduce_fusion.2
  113.4 1.8 select_reduce_fusion.2
  125.0 1.8 select_reduce_fusion.2
  136.5 1.8 select_reduce_fusion.2
  148.0 1.8 select_reduce_fusion.2
  159.5 1.8 select_reduce_fusion.2
  171.0 1.8 select_reduce_fusion.2
  182.6 1.8 select_reduce_fusion.2
  194.1 1.8 select_reduce_fusion.2
  205.6 1.8 select_reduce_fusion.2
  217.1 1.8 select_reduce_fusion.2
  228.6 1.8 select_reduce_fusion.2
  240.2 1.8 select_reduce_fusion.2
  251.7 1.8 select_reduce_fusion.2
  286.3 1.8 select_reduce_fusion.2
  297.8 1.8 select_reduce_fusion.2
  320.8 1.8 select_reduce_fusion.2
  332.3 1.8 select_reduce_fusion.2
  343.8 1.8 select_reduce_fusion.2
  349.8 2.7 fusion.94
  352.5 2.0 copy.34
  354.5 4.4 collective-permute-start.3
  358.9 3.8 pad_add_fusion.3
  362.7 1.8 copy.35
  364.5 2.2 fusion.96
  367.0 2.8 collective-permute-start.4
  371.4 4.7 collective-permute-start.5
  376.8 98.4 %psum.14 = f32[]{:T(128)} all-reduce(f32[]{:T(128)} %reduce_sum.82), channel_id=1, replica_groups=mesh['gx'=16,'gy'=8,'gz'=4] {'gx','gy','gz'}, use_global_device_ids=true, to_apply=%region_10.11 | all-reduce | flops 1 | bytes 8 | tf_op jit(solution)/shard_map/psum | solution.py:280
  477.3 2.1 convolution_bitcast_fusion
  479.4 5.3 fusion.88
  484.7 3.6 copy.37
  488.3 5.3 reshape.317
  493.6 277.4 %all-reduce.58.cloned.1.call-done = f32[3,48,4096]{2,1,0:T(8,128)} async-done(((f32[3,48,4096]{2,1,0:T(8,128)}), f32[3,48,4096]{2,1,0:T(8,128)}) %all-reduce.58.cloned.1.call-update) | async-done | bytes 2359312 | tf_op jit(solution)/shard_map/psum | solution.py:284
  771.0 3.3 copy.74
  (744 shorter events, 229.0 us)
Async XLA Ops:
  6.5 764.5 %all-reduce.58.cloned.1.call-start = ((), (), s32[]{:S(2)}) async-start(), calls=%async_computation | async-start | bytes 4718592 | tf_op jit(solution)/shard_map/psum | solution.py:284
  7.4 13.8 %copy-start.27 = (s32[24]{0:T(128)}, s32[24]{0:T(128)S(1)}, u32[]{:S(2)}) copy-start(s32[24]{0:T(128)S(1)} %dynamic_slice.32) | copy-start | bytes 292
  8.3 12.9 %copy-start.5 = (f32[24]{0:T(128)}, f32[24]{0:T(128)S(1)}, u32[]{:S(2)}) copy-start(f32[24]{0:T(128)S(1)} %get-tuple-element.379) | copy-start | bytes 292
  8.3 12.9 %copy-start.7 = (f32[24]{0:T(128)}, f32[24]{0:T(128)S(1)}, u32[]{:S(2)}) copy-start(f32[24]{0:T(128)S(1)} %get-tuple-element.380) | copy-start | bytes 292
  14.1 2.2 copy-start.32
  14.1 2.5 copy-start.31
  16.4 7.3 copy-start.9
  16.6 7.1 copy-start.11
  16.6 7.1 copy-start.13
  16.6 7.1 copy-start.15
  16.7 7.1 copy-start.17
  16.8 8.6 %copy-start.29 = (s32[128]{0:T(128)}, s32[128]{0:T(128)S(1)}, u32[]{:S(2)}) copy-start(s32[128]{0:T(128)S(1)} %dynamic_slice.34) | copy-start | bytes 1540
  17.0 8.4 %copy-start.19 = (f32[128]{0:T(128)}, f32[128]{0:T(128)S(1)}, u32[]{:S(2)}) copy-start(f32[128]{0:T(128)S(1)} %get-tuple-element.312) | copy-start | bytes 1540
  17.0 8.4 %copy-start.21 = (f32[128]{0:T(128)}, f32[128]{0:T(128)S(1)}, u32[]{:S(2)}) copy-start(f32[128]{0:T(128)S(1)} %get-tuple-element.372) | copy-start | bytes 1540
  17.0 8.4 %copy-start.23 = (f32[128]{0:T(128)}, f32[128]{0:T(128)S(1)}, u32[]{:S(2)}) copy-start(f32[128]{0:T(128)S(1)} %get-tuple-element.373) | copy-start | bytes 1540
  17.0 8.4 %copy-start.25 = (f32[128]{0:T(128)}, f32[128]{0:T(128)S(1)}, u32[]{:S(2)}) copy-start(f32[128]{0:T(128)S(1)} %get-tuple-element.374) | copy-start | bytes 1540
  17.0 4.1 copy-start.4
  27.0 6.6 collective-permute-start
  33.7 10.2 %collective-permute-start.1 = (f32[25,9,1,128]{3,2,1,0:T(1,128)S(1)}, f32[25,9,1,128]{3,2,1,0:T(1,128)S(1)}, u32[]{:S(2)}, u32[]{:S(2)}) collective-permute-start(f32[25,9,1,128]{3,2,1,0:T(1,128)S(1)} %pad_maximum_fusion.7), channel_id=1, source_target_pairs={{4,0},{8,4},{12,8},{16,12},{20,16},{24,20},{28,24},{5,1},{9,5},{13... | collective-permute-start | bytes 345608 | tf_op jit(solution)/shard_map/ppermute | solution.py:20
  50.1 8.7 %collective-permute-start.2 = (f32[25,9,33,1]{2,3,1,0:T(1,128)S(1)}, f32[25,9,33,1]{2,3,1,0:T(1,128)S(1)}, u32[]{:S(2)}, u32[]{:S(2)}) collective-permute-start(f32[25,9,33,1]{2,3,1,0:T(1,128)S(1)} %copy.32), channel_id=1, source_target_pairs={{1,0},{2,1},{3,2},{5,4},{6,5},{7,6},{9,8},{10,9},{11,10},{13,12},{... | collective-permute-start | bytes 89108 | tf_op jit(solution)/shard_map/ppermute | solution.py:20
  66.0 7.4 copy-start
  81.9 1.8 copy-start.33
  128.0 1.8 copy-start.33
  139.5 1.8 copy-start.33
  162.5 1.8 copy-start.33
  185.6 1.8 copy-start.33
  208.6 1.8 copy-start.33
  220.1 1.8 copy-start.33
  231.7 1.8 copy-start.33
  243.2 1.8 copy-start.33
  254.7 1.8 copy-start.33
  266.2 1.8 copy-start.33
  277.8 1.8 copy-start.33
  323.8 1.8 copy-start.33
  335.3 1.8 copy-start.33
  354.5 8.2 %collective-permute-start.3 = (f32[25,3,33,1]{2,3,1,0:T(1,128)S(1)}, f32[25,3,33,1]{2,3,1,0:T(1,128)S(1)}, u32[]{:S(2)}, u32[]{:S(2)}) collective-permute-start(f32[25,3,33,1]{2,3,1,0:T(1,128)S(1)} %copy.34), channel_id=1, source_target_pairs={{0,1},{1,2},{2,3},{4,5},{5,6},{6,7},{8,9},{9,10},{10,11},{12,13},{... | collective-permute-start | bytes 29708 | tf_op jit(solution)/shard_map/ppermute | solution.py:20
  364.5 2.3 copy-start.1
  367.0 3.9 collective-permute-start.4
  371.0 5.2 copy-start.35
  371.4 104.7 %copy-start.20 = (f32[128]{0:T(128)S(1)}, f32[128]{0:T(128)}, u32[]{:S(2)}) copy-start(f32[128]{0:T(128)} %copy-done.19) | copy-start | bytes 1540
  371.4 104.7 %copy-start.22 = (f32[128]{0:T(128)S(1)}, f32[128]{0:T(128)}, u32[]{:S(2)}) copy-start(f32[128]{0:T(128)} %copy-done.21) | copy-start | bytes 1540
  371.4 104.7 %copy-start.24 = (f32[128]{0:T(128)S(1)}, f32[128]{0:T(128)}, u32[]{:S(2)}) copy-start(f32[128]{0:T(128)} %copy-done.23) | copy-start | bytes 1540
  371.4 104.7 %copy-start.26 = (f32[128]{0:T(128)S(1)}, f32[128]{0:T(128)}, u32[]{:S(2)}) copy-start(f32[128]{0:T(128)} %copy-done.25) | copy-start | bytes 1540
  371.4 104.7 %copy-start.30 = (s32[128]{0:T(128)S(1)}, s32[128]{0:T(128)}, u32[]{:S(2)}) copy-start(s32[128]{0:T(128)} %copy-done.29) | copy-start | bytes 1540
  371.4 104.6 %collective-permute-start.5 = (f32[1,3,32,128]{3,2,1,0:T(8,128)S(1)}, f32[1,3,32,128]{3,2,1,0:T(8,128)S(1)}, u32[]{:S(2)}, u32[]{:S(2)}) collective-permute-start(f32[1,3,32,128]{3,2,1,0:T(8,128)S(1)} %slice.1073), channel_id=1, source_target_pairs={{0,32},{32,64},{64,96},{96,128},{128,160},{160,192},{192,224},{224... | collective-permute-start | bytes 147464 | tf_op jit(solution)/shard_map/ppermute | solution.py:20
  477.2 2.2 copy-start.6
  477.2 2.2 copy-start.8
  477.3 2.2 copy-start.28
  (41 other events, 38.9 us)
Sparse Core Ops, SparseCore 0:
  493.7 277.2 all-reduce.57
where the time goes:
time: 788 us; the launch traced here: 781 us
  waiting for transfers between devices  292 us (37%)
  local copies, waits for them, and re-layouts  172 us (22%)
  other arithmetic  138 us (18%)
  blocking collectives  98.4 us (12%)
  loops' own time  28.5 us (4%)
  starting transfers between devices  23.9 us (3%)
  between operations  14.9 us (2%)
  matrix products  13.7 us (2%)
    psum x1, waiting for transfers between devices, on_device(): summed = lax.psum(control, ('gx', 'gy', 'gz'))  277 us
    psum x1, blocking collectives, on_device(): volume = lax.psum(jnp.sum(volumes), ('gx', 'gy', 'gz'))  98.4 us
    reduce_sum x24, other arithmetic, layer_terms(): total_volume = jnp.sum(jnp.where(counted, volume, 0.0))  43.6 us
    squeeze x24, local copies, waits for them, and re-layouts, derivatives(): lower_field = lower_values[component]  38.6 us
    squeeze x24, local copies, waits for them, and re-layouts, derivatives(): upper_field = upper_values[component]  38.4 us
    dynamic_slice x24, local copies, waits for them, and re-layouts, on_device(): lax.map(one_layer, (extended[:-1], extended[1:], jnp.arange(layers, dtype...  29.3 us
    another operation x1, loops' own time, on_device(): lax.map(one_layer, (extended[:-1], extended[1:], jnp.arange(layers, dtype...  28.5 us
    ppermute x6, starting transfers between devices, passed_along(): lax.ppermute(value, axis, [(source, source + steps) for source in range(i...  23.9 us
  transfers between devices with their start and end apart: 7, of which 5 were waited for; matrix products, arithmetic and copies ran while one was open for 1% of the time, Pallas kernels for 0%

commit v1 on v0

v1 whole, which is shorter than its diff:
```python
import functools

import jax
import jax.numpy as jnp
from jax import lax
from jax.experimental import pallas as pl
from jax.experimental.pallas import tpu as pltpu
from jax.sharding import Mesh
from jax.sharding import PartitionSpec as P

NCX = 48
NCY = 64
NCZ = 64
MU_SHEAR = 40.0
LAME_RATIO = 60.0 / 40.0
TAPER_RATE = 0.8

LENGTH = ("zl", "y")
WIDTH = ("x", "c")
DEPTH = ("zh",)
F32 = jnp.float32
BF16 = jnp.bfloat16
MIB = 1 << 20


def spline_weights(t):
    c = 1.0 - t
    t2 = t * t
    t3 = t2 * t
    return [
        c * c * c / 6.0,
        (3.0 * t3 - 6.0 * t2 + 4.0) / 6.0,
        (-3.0 * t3 + 3.0 * t2 + 3.0 * t + 1.0) / 6.0,
        t3 / 6.0,
    ]


def node_params(span_ref, first, count):
    total = span_ref.shape[1]
    table = jnp.broadcast_to(span_ref[...].astype(F32), (count, total))
    place = lax.broadcasted_iota(jnp.int32, (count, total), 1)
    node = jnp.minimum(first + lax.broadcasted_iota(jnp.int32, (count, total), 0), total - 1)
    own = jnp.sum(jnp.where(place == node, table, 0.0), axis=1, keepdims=True)
    matches = table == own
    counted = jnp.sum(jnp.where(matches, 1.0, 0.0), axis=1, keepdims=True)
    earlier = jnp.sum(jnp.where(matches & (place < node), 1.0, 0.0), axis=1, keepdims=True)
    return own, (earlier + 0.5) / counted


def node_rows(own, t, columns):
    offset = columns - own
    out = jnp.zeros(columns.shape, F32)
    for k, weight in enumerate(spline_weights(t)):
        out = out + jnp.where(offset == float(k), weight, 0.0)
    return out


def element_rows(lower, upper, columns, live):
    low, high = node_rows(*lower, columns), node_rows(*upper, columns)
    return jnp.concatenate(
        [jnp.where(live, low + high, 0.0), jnp.where(live, high - low, 0.0)], axis=0
    )


def split(value):
    high = value.astype(BF16)
    return high, (value - high.astype(F32)).astype(BF16)


def dot(a, b):
    return lax.dot_general(a, b, (((1,), (0,)), ((), ())), preferred_element_type=F32)


def face_kernel(u_ref, w_ref, x_ref, y_ref, z_ref):
    layers = u_ref.shape[0]
    rows, lanes = u_ref.shape[2], u_ref.shape[3]
    lane = lax.broadcasted_iota(jnp.int32, (rows, lanes), 1)
    for f in range(6):
        source = (u_ref, w_ref)[f // 3]
        c = f % 3
        x_ref[f] = source[0, c]
        packed = jnp.zeros((rows, lanes), F32)
        for i in range(layers):
            y_ref[i, pl.ds(f, 1)] = source[i, c, pl.ds(0, 1)]
            value = source[i, c]
            packed = jnp.where(lane == i, value if i == 0 else pltpu.roll(value, i, 1), packed)
        z_ref[f] = packed
    for i in range(layers):
        y_ref[i, pl.ds(6, 2)] = jnp.zeros((2, lanes), F32)


def net_kernel(
    sx_smem, o_ref, sx_ref, sy_ref, sz_ref, q_ref, coef_ref, lin_ref, yb_ref, zb_ref, zf_ref, yf_ref
):
    window = q_ref.shape[0] - 1
    ny, nz = q_ref.shape[2:]
    nx = window - 4
    nodes_x, nodes_y, nodes_z = sx_ref.shape[1], sy_ref.shape[1], sz_ref.shape[1]
    step_x = 2.0 * nodes_x / (NCX - 3)
    step_y = 2.0 * nodes_y / (NCY - 3)
    step_z = 2.0 * nodes_z / (NCZ - 3)
    start_x = lax.axis_index(LENGTH) * nx
    start_y = lax.axis_index(WIDTH) * ny
    start_z = lax.axis_index(DEPTH) * nz
    lanes = 2 * NCZ

    rows = coef_ref.shape[1]
    own, t = node_params(sx_ref, start_x, rows)
    own_up, t_up = node_params(sx_ref, start_x + 1, rows)
    climbs = own_up > own
    low = spline_weights(t) + [jnp.zeros_like(t)]
    high = spline_weights(t_up)
    high = [
        jnp.where(climbs, high[k - 1] if k else 0.0, high[k] if k < 4 else 0.0) for k in range(5)
    ]
    dx = (own_up - own) + (t_up - t)
    rate = TAPER_RATE / (NCX - 1)
    both = (own_up + own) + (t_up + t) + 2.0
    columns = [low[k] + high[k] for k in range(5)] + [high[k] - low[k] for k in range(5)]
    columns += [4.0 * step_x * dx, 2.0 * rate * dx, 4.0 + 2.0 * rate * both]
    for k, column in enumerate(columns):
        coef_ref[k] = jnp.broadcast_to(column, (rows, lanes))

    lower = node_params(sy_ref, start_y, ny)
    upper = node_params(sy_ref, start_y + 1, ny)
    live_y = start_y + lax.broadcasted_iota(jnp.int32, (ny, lanes), 0) < nodes_y - 1
    lane = lax.broadcasted_iota(jnp.int32, (ny, lanes), 1)
    half = NCY // 2
    y_rows = element_rows(lower, upper, (lane % NCY).astype(F32), live_y)
    for r, step in enumerate((step_x, step_y, step_z)):
        hi, lo = split(step * y_rows)
        yf_ref[r] = jnp.concatenate([hi, lo[:, :NCY]], axis=1)
    paired = 2 * (lane % half) + (lane % NCY) // half
    y_rows = element_rows(lower, upper, paired.astype(F32), live_y)
    turned = jnp.transpose(jnp.concatenate([y_rows, y_rows], axis=0))[:NCY]
    hi, lo = split(turned)
    yb_ref[...] = jnp.concatenate([hi, lo[:, : 2 * ny]], axis=1)
    place = (upper[0] + lower[0]) + (upper[1] + lower[1]) + (2.0 - (NCY - 1))
    rise = (upper[0] - lower[0]) + (upper[1] - lower[1])
    live_z = start_z + lane < nodes_z - 1
    live = live_y & live_z
    lin_ref[0] = jnp.where(live, step_y * place, 0.0)
    lin_ref[1] = jnp.where(live, step_y * rise, 0.0)
    lin_ref[4] = jnp.where(live, 0.0, 1.0)
    lin_ref[5] = jnp.where(live, 1.0, 0.0)

    lower = node_params(sz_ref, start_z, nz)
    upper = node_params(sz_ref, start_z + 1, nz)
    live_z = start_z + lax.broadcasted_iota(jnp.int32, (nz, lanes), 0) < nodes_z - 1
    lane = lax.broadcasted_iota(jnp.int32, (nz, lanes), 1)
    z_rows = element_rows(lower, upper, (lane % NCZ).astype(F32), live_z)
    wide = lax.broadcasted_iota(jnp.int32, z_rows.shape, 1)
    hi, lo = split(
        jnp.concatenate(
            [jnp.where(wide < NCZ, z_rows, 0.0), jnp.where(wide < NCZ, 0.0, z_rows)], axis=0
        )
    )
    zb_ref[0] = hi
    zb_ref[1] = lo
    hi, lo = split(jnp.transpose(z_rows)[:NCZ])
    zf_ref[0] = hi
    zf_ref[1] = lo
    place = (upper[0] + lower[0]) + (upper[1] + lower[1]) + (2.0 - (NCZ - 1))
    rise = (upper[0] - lower[0]) + (upper[1] - lower[1])
    place = jnp.transpose(jnp.broadcast_to(step_z * place, (nz, lanes)))[:ny]
    rise = jnp.transpose(jnp.broadcast_to(step_z * rise, (nz, lanes)))[:ny]
    lin_ref[2] = jnp.where(live, place, 0.0)
    lin_ref[3] = jnp.where(live, rise, 0.0)

    start = jnp.minimum(sx_smem[start_x], NCX - window)

    def step(t, carry):
        for r in range(3):
            o = o_ref[r, start + t]
            along_z = dot(o, zf_ref[0]) + dot(o, zf_ref[1])
            high, low = split(along_z)
            full = dot(yf_ref[r], jnp.concatenate([high, low, high], axis=0))
            q_ref[t, 3 * r] = full[:ny, :nz]
            q_ref[t, 3 * r + 1] = full[ny:, :nz]
            q_ref[t, 3 * r + 2] = full[:ny, nz:]
        return carry

    lax.fori_loop(0, window, step, 0)
    q_ref[window] = jnp.zeros(q_ref.shape[1:], F32)


def cofactors(m):
    out = [[None] * 3 for _ in range(3)]
    for r in range(3):
        r1, r2 = (r + 1) % 3, (r + 2) % 3
        for c in range(3):
            c1, c2 = (c + 1) % 3, (c + 2) % 3
            out[r][c] = m[r1][c1] * m[r2][c2] - m[r1][c2] * m[r2][c1]
    return out


def dot3(a, b):
    return a[0] * b[0] + a[1] * b[1] + a[2] * b[2]


def column(m, c):
    return [m[0][c], m[1][c], m[2][c]]


def element_gradient(jac, grad_u, grad_w, dead):
    cof = cofactors(jac)
    det = dot3(jac[0], cof[0])
    scale = 1.0 / (det + dead)
    inv_t = [[cof[r][c] * scale for c in range(3)] for r in range(3)]
    strain = [[dot3(grad_u[r], inv_t[c]) for c in range(3)] for r in range(3)]
    virt = [[dot3(grad_w[r], inv_t[c]) for c in range(3)] for r in range(3)]
    deform = [[strain[r][c] + 1.0 if r == c else strain[r][c] for c in range(3)] for r in range(3)]
    reduced = [[deform[r][c] - virt[r][c] for c in range(3)] for r in range(3)]
    cof_d = cofactors(deform)
    det_d = dot3(deform[0], cof_d[0])
    log_d = jnp.log(det_d)
    scale_d = 1.0 / det_d
    flip = [[cof_d[r][c] * scale_d for c in range(3)] for r in range(3)]
    mixed = [[dot3(column(virt, a), column(flip, b)) for b in range(3)] for a in range(3)]
    trace = mixed[0][0] + mixed[1][1] + mixed[2][2]
    factor = 1.0 - LAME_RATIO * log_d
    shift = factor + LAME_RATIO * trace
    inner = [
        [factor * mixed[a][b] + shift if a == b else factor * mixed[a][b] for b in range(3)]
        for a in range(3)
    ]
    quad = [[None] * 3 for _ in range(3)]
    for a in range(3):
        for b in range(a, 3):
            quad[a][b] = dot3(column(reduced, a), column(reduced, b)) - dot3(
                column(virt, a), column(virt, b)
            )
            quad[b][a] = quad[a][b]
    level = (
        0.5 * (quad[0][0] + quad[1][1] + quad[2][2])
        + (0.5 * LAME_RATIO * log_d - 1.0) * log_d
        - 1.5
        + factor * (1.0 + trace)
        + LAME_RATIO * trace
    )
    tensor = [
        [reduced[a][b] - quad[a][b] - dot3(flip[a], column(inner, b)) for b in range(3)]
        for a in range(3)
    ]
    for a in range(3):
        tensor[a][a] = tensor[a][a] + level
    return det, [[dot3(tensor[r], column(cof, s)) for s in range(3)] for r in range(3)]


def element_kernel(
    sx_smem, coef_ref, u_ref, w_ref, xf_ref, yf_ref, yxf_ref, zf_ref, zxf_ref, zyf_ref, zxyf_ref,
    lin_ref, q_ref, yb_ref, zb_ref, out_ref, raw, side, sums, diffs, planes, acc, left_hi, left_lo,
):
    layers, _, ny, nz = u_ref.shape
    window = q_ref.shape[0] - 1
    start_x = lax.axis_index(LENGTH) * layers
    live_layers = jnp.minimum(layers, sx_smem.shape[0] - 1 - start_x)
    start = jnp.minimum(sx_smem[start_x], NCX - window)
    rows = ny + 8
    lane = lax.broadcasted_iota(jnp.int32, (rows, nz), 1)

    for f in range(6):
        far = pltpu.roll(zxf_ref[f], layers, 1)
        side[f, pl.ds(0, ny)] = jnp.where(lane[:ny] == layers, far, zf_ref[f])
        far = pltpu.roll(zxyf_ref[f], layers, 1)
        side[f, pl.ds(ny, 8)] = jnp.where(lane[:8] == layers, far, zyf_ref[f])
    acc[...] = jnp.zeros(acc.shape, F32)

    def make_planes(i):
        slot = lax.rem(i, 2)

        @pl.when(i < layers)
        def _():
            edge = yf_ref[i]
            for f in range(6):
                raw[f, pl.ds(0, ny)] = (u_ref, w_ref)[f // 3][i, f % 3]
                raw[f, pl.ds(ny, 1)] = edge[f : f + 1]

        @pl.when(i >= layers)
        def _():
            for f in range(6):
                raw[f, pl.ds(0, ny)] = xf_ref[f]
                raw[f, pl.ds(ny, 1)] = yxf_ref[pl.ds(f, 1)]

        for f in range(6):
            here = raw[f]
            beyond = pltpu.roll(side[f], nz - 1 - i, 1)
            there = jnp.where(lane == nz - 1, beyond, pltpu.roll(here, nz - 1, 1))
            sums[f] = here + there
            diffs[f] = there - here
        for f in range(6):
            low, high = sums[f, pl.ds(0, ny)], sums[f, pl.ds(1, ny)]
            planes[slot, 3 * f] = low + high
            planes[slot, 3 * f + 1] = high - low
            planes[slot, 3 * f + 2] = diffs[f, pl.ds(0, ny)] + diffs[f, pl.ds(1, ny)]

    raw[:, pl.ds(ny, 8)] = jnp.zeros((6, 8, nz), F32)
    make_planes(jnp.int32(0))

    def layer(i, volume):
        make_planes(i + 1)
        new, old = lax.rem(i + 1, 2), lax.rem(i, 2)
        first = sx_smem[start_x + i] - start
        coef = [coef_ref[k, pl.ds(i, 1)] for k in range(13)]
        total, delta = coef[:5], coef[5:10]
        for block in range(ny // 8):
            at = pl.ds(8 * block, 8)
            jac = [[None] * 3 for _ in range(3)]
            for r in range(3):
                for s in range(3):
                    weight = delta if s == 0 else total
                    value = weight[0] * q_ref[first, 3 * r + s, at]
                    for k in range(1, 5):
                        value = value + weight[k] * q_ref[first + k, 3 * r + s, at]
                    jac[r][s] = value
            jac[0][0] = jac[0][0] + coef[10] * lin_ref[5, at]
            jac[1][0] = jac[1][0] + coef[11] * lin_ref[0, at]
            jac[1][1] = jac[1][1] + coef[12] * lin_ref[1, at]
            jac[2][0] = jac[2][0] + coef[11] * lin_ref[2, at]
            jac[2][2] = jac[2][2] + coef[12] * lin_ref[3, at]
            grads = []
            for f in range(6):
                grads.append(
                    [
                        planes[new, 3 * f, at] - planes[old, 3 * f, at],
                        planes[new, 3 * f + 1, at] + planes[old, 3 * f + 1, at],
                        planes[new, 3 * f + 2, at] + planes[old, 3 * f + 2, at],
                    ]
                )
            det, gradient = element_gradient(jac, grads[:3], grads[3:], lin_ref[4, at])
            volume = volume + det
            for r in range(3):
                for s in range(3):
                    weight = delta if s == 0 else total
                    for k in range(5):
                        p = (first + k, 3 * r + s, at)
                        acc[p] = acc[p] + weight[k] * gradient[r][s]
        return volume

    volume = lax.fori_loop(0, live_layers, layer, jnp.zeros((8, nz), F32))

    blank = jnp.zeros((ny, nz), BF16)
    half = NCY // 2

    def along_width(t, carry):
        for r in range(3):
            hi, lo = [], []
            for s in range(3):
                h, l = split(acc[t, 3 * r + s])
                hi.append(h)
                lo.append(l)
            hi = jnp.concatenate(
                [jnp.concatenate([hi[0], hi[2]], axis=1), jnp.concatenate([hi[1], blank], axis=1)],
                axis=0,
            )
            lo = jnp.concatenate(
                [jnp.concatenate([lo[0], lo[2]], axis=1), jnp.concatenate([lo[1], blank], axis=1)],
                axis=0,
            )
            full = dot(yb_ref[...], jnp.concatenate([hi, lo, hi], axis=0))
            high, low = split(full)
            at = pl.ds(pl.multiple_of((t * 3 + r) * half, half), half)
            left_hi[at, pl.ds(0, 2 * nz)] = high[:half]
            left_hi[at, pl.ds(2 * nz, 2 * nz)] = high[half:]
            left_lo[at, pl.ds(0, 2 * nz)] = low[:half]
            left_lo[at, pl.ds(2 * nz, 2 * nz)] = low[half:]
        return carry

    lax.fori_loop(0, window, along_width, 0)

    stride = out_ref.shape[0] // half
    batch = 12

    def along_depth(step, carry):
        at = pl.ds(pl.multiple_of(step * batch * half, half), batch * half)
        hi, lo = left_hi[at], left_lo[at]
        full = dot(hi, zb_ref[0]) + dot(lo, zb_ref[0]) + dot(hi, zb_ref[1])
        for b in range(batch):
            out_ref[pl.ds(step * batch + b, half, stride=stride)] = full[b * half : (b + 1) * half]
        return carry

    lax.fori_loop(0, 3 * window // batch, along_depth, 0)

    total = jnp.sum(volume, axis=0, keepdims=True)
    out_ref[pl.ds(3 * window, half, stride=stride)] = jnp.broadcast_to(total, (half, nz))
    for spare in range(3 * window + 1, stride):
        out_ref[pl.ds(spare, half, stride=stride)] = jnp.zeros((half, nz), F32)


def shifted(value, axes, sizes):
    names = sum(axes, ())
    dims = [sizes[a] for a in axes]
    pairs = []
    count = 1
    for d in dims:
        count *= d
    for flat in range(count):
        rest, index = flat, []
        for d in reversed(dims):
            index.insert(0, rest % d)
            rest //= d
        if all(v > 0 for v in index):
            target = 0
            for v, d in zip(index, dims):
                target = target * d + v - 1
            pairs.append((flat, target))
    return lax.ppermute(value, names, pairs)


def on_device(sizes, offsets, displacement, adjoint, span_x, span_y, span_z):
    nx, _, ny, nz = displacement.shape
    nodes_x, nodes_y, nodes_z = span_x.shape[0], span_y.shape[0], span_z.shape[0]
    vmem = pl.BlockSpec(memory_space=pltpu.VMEM)
    smem = pl.BlockSpec(memory_space=pltpu.SMEM)

    x_face, y_face, z_face = pl.pallas_call(
        face_kernel,
        out_shape=(
            jax.ShapeDtypeStruct((6, ny, nz), F32),
            jax.ShapeDtypeStruct((nx, 8, nz), F32),
            jax.ShapeDtypeStruct((6, ny, nz), F32),
        ),
        in_specs=[vmem] * 2,
        out_specs=(vmem,) * 3,
        name="faces",
        compiler_params=pltpu.CompilerParams(vmem_limit_bytes=16 * MIB),
    )(displacement, adjoint)
    xf = shifted(x_face, (LENGTH,), sizes)
    yf = shifted(y_face, (WIDTH,), sizes)
    zf = shifted(z_face, (DEPTH,), sizes)
    yxf = shifted(y_face[0], (LENGTH, WIDTH), sizes)
    zxf = shifted(z_face, (LENGTH, DEPTH), sizes)
    zyf = shifted(z_face[:, :8], (WIDTH, DEPTH), sizes)
    zxyf = shifted(z_face[:, :8], (LENGTH, WIDTH, DEPTH), sizes)

    window = nx + 4
    spans = [s.reshape(1, s.shape[0]) for s in (span_x, span_y, span_z)]
    net, coef, linear, y_back, z_back = pl.pallas_call(
        net_kernel,
        out_shape=(
            jax.ShapeDtypeStruct((window + 1, 9, ny, nz), F32),
            jax.ShapeDtypeStruct((13, -(-nx // 8) * 8, nz), F32),
            jax.ShapeDtypeStruct((6, ny, nz), F32),
            jax.ShapeDtypeStruct((NCY, 6 * ny), BF16),
            jax.ShapeDtypeStruct((2, 4 * nz, 2 * NCZ), BF16),
        ),
        in_specs=[smem] + [vmem] * 4,
        out_specs=(vmem,) * 5,
        scratch_shapes=[
            pltpu.VMEM((2, NCZ, 2 * nz), BF16),
            pltpu.VMEM((3, 2 * ny, 3 * NCY), BF16),
        ],
        name="net",
        compiler_params=pltpu.CompilerParams(vmem_limit_bytes=24 * MIB),
        cost_estimate=pl.CostEstimate(flops=2 * 10**9, bytes_accessed=6 * MIB, transcendentals=0),
    )(span_x, offsets.reshape(3, NCX, NCY, NCZ), *spans)

    half = NCY // 2
    stride = -(-(3 * window + 1) // 8) * 8
    terms = pl.pallas_call(
        element_kernel,
        out_shape=jax.ShapeDtypeStruct((half * stride, 2 * NCZ), F32),
        in_specs=[smem] + [vmem] * 14,
        out_specs=vmem,
        scratch_shapes=[
            pltpu.VMEM((6, ny + 8, nz), F32),
            pltpu.VMEM((6, ny + 8, nz), F32),
            pltpu.VMEM((6, ny + 8, nz), F32),
            pltpu.VMEM((6, ny + 8, nz), F32),
            pltpu.VMEM((2, 18, ny, nz), F32),
            pltpu.VMEM((window + 1, 9, ny, nz), F32),
            pltpu.VMEM((3 * window * half, 4 * nz), BF16),
            pltpu.VMEM((3 * window * half, 4 * nz), BF16),
        ],
        name="elements",
        compiler_params=pltpu.CompilerParams(vmem_limit_bytes=48 * MIB),
        cost_estimate=pl.CostEstimate(flops=10**10, bytes_accessed=10 * MIB, transcendentals=0),
    )(
        span_x, coef, displacement, adjoint, xf, yf, yxf, zf, zxf, zyf, zxyf,
        linear, net, y_back, z_back,
    )

    size_w, size_d = sizes[WIDTH], sizes[DEPTH]
    terms = terms.reshape(size_w, size_d * stride, 2 * NCZ)
    terms = jnp.sum(lax.all_to_all(terms, WIDTH, 0, 0, tiled=True), axis=0)
    terms = terms.reshape(size_d, stride, 2 * NCZ)
    terms = jnp.sum(lax.all_to_all(terms, DEPTH, 0, 0, tiled=True), axis=0)
    size_l = sizes[LENGTH]
    part = 3 * NCX // size_l
    start = lax.dynamic_slice_in_dim(span_x, lax.axis_index(LENGTH) * nx, 1)[0]
    first_row = jnp.minimum(start, NCX - window)
    spread = lax.dynamic_update_slice(
        jnp.zeros((3 * NCX, 2 * NCZ), F32), terms[: 3 * window], (3 * first_row, 0)
    )
    spread = jnp.concatenate(
        [
            spread.reshape(size_l, part, 2 * NCZ),
            jnp.broadcast_to(terms[3 * window], (size_l, 1, 2 * NCZ)),
        ],
        axis=1,
    )
    summed = jnp.sum(lax.all_to_all(spread, LENGTH, 0, 0, tiled=True), axis=0)
    elements = (nodes_x - 1) * (nodes_y - 1) * (nodes_z - 1)
    owned = summed[:part] * (elements * MU_SHEAR / jnp.sum(summed[part]))
    size_x, size_c = size_w // 2, 2
    for axes, size in ((LENGTH, size_l), (DEPTH, size_d), (("x",), size_x)):
        owned = jnp.broadcast_to(owned[None], (size,) + owned.shape)
        owned = lax.all_to_all(owned, axes, 0, 0, tiled=True)
    other = lax.ppermute(owned, "c", [(0, 1), (1, 0)])
    core = lax.axis_index("c")
    both = jnp.stack([jnp.where(core == 0, owned, other), jnp.where(core == 0, other, owned)])
    both = both.reshape(size_c, size_x, size_d, size_l, part // 3, 3, 2 * NCZ)
    return both.transpose(5, 3, 4, 1, 0, 2, 6).reshape(3, NCX, NCY * NCZ)


def solution(mesh):
    count_x, count_y, count_z = mesh.devices.shape
    fine = Mesh(
        mesh.devices.reshape(2, count_x // 2, count_y // 2, 2, count_z), ("zl", "y", "x", "c", "zh")
    )
    sizes = {LENGTH: count_x, WIDTH: count_y, DEPTH: count_z}
    brick = P(LENGTH, None, WIDTH, DEPTH)
    return jax.shard_map(
        functools.partial(on_device, sizes),
        mesh=fine,
        in_specs=(P(), brick, brick, P(), P(), P()),
        out_specs=P(),
        check_vma=False,
    )
```

time: 788 us -> 176 us (0.22)
  waiting for transfers between devices: 292 us -> 8.79 us
  local copies, waits for them, and re-layouts: 172 us -> 12.2 us
  other arithmetic: 138 us -> 1.84 us
  Pallas kernels: 0 us -> 40.9 us
  loops' own time: 28.5 us -> 0 us
  blocking collectives: 98.4 us -> 74.6 us
  matrix products: 13.7 us -> 0 us
  between operations: 14.9 us -> 1.69 us
  starting transfers between devices: 23.9 us -> 35.5 us
    psum x1 -> x0, waiting for transfers between devices: 277 us -> none  [on_device(): summed = lax.psum(control, ('gx', 'gy', 'gz'))]
    psum x1 -> x0, blocking collectives: 98.4 us -> none  [on_device(): volume = lax.psum(jnp.sum(volumes), ('gx', 'gy', 'gz'))]
    squeeze x51 -> x2, local copies, waits for them, and re-layouts: 81.2 us -> 0.01 us  [the longest x1 0.01 us: on_device(): terms[3 * window]]
    all_to_all x0 -> x5, blocking collectives: none -> 74.6 us  [the longest x3 34.7 us: on_device(): owned = lax.all_to_all(owned, axes, 0, 0, tiled=True)]
    reduce_sum x28 -> x4, other arithmetic: 45.4 us -> 1.39 us  [the longest x1 0.75 us: on_device(): terms = jnp.sum(lax.all_to_all(terms, WIDTH, 0, 0, tiled=True), axis=0)]
    pallas_call x0 -> x3, Pallas kernels: none -> 40.9 us  [the longest x1 24.3 us: on_device(): pl.pallas_call(element_kernel, out_shape=jax.ShapeDtypeStruct((half * str...]
    dynamic_slice x27 -> x1, local copies, waits for them, and re-layouts: 30.2 us -> 0.63 us  [on_device(): start = lax.dynamic_slice_in_dim(span_x, lax.axis_index(LENGTH) * nx, 1)[0]]
    another operation x1 -> x0, loops' own time: 28.5 us -> none  [on_device(): lax.map(one_layer, (extended[:-1], extended[1:], jnp.arange(layers, dtype...]
  transfers between devices with their start and end apart: 7 -> 9, of which waited for: 5 -> 2; matrix products, arithmetic and copies ran while one was open for 1% -> 2% of each run, Pallas kernels for 0% -> 9%
where the time goes in v1:
time: 176 us; the launch traced here: 175 us
  blocking collectives  74.6 us (42%)
  Pallas kernels  40.9 us (23%)
  starting transfers between devices  35.5 us (20%)
  local copies, waits for them, and re-layouts  12.2 us (7%)
  waiting for transfers between devices  8.79 us (5%)
  other arithmetic  1.84 us (1%)
    all_to_all x3, blocking collectives, on_device(): owned = lax.all_to_all(owned, axes, 0, 0, tiled=True)  34.7 us
    pallas_call x1, Pallas kernels, on_device(): pl.pallas_call(element_kernel, out_shape=jax.ShapeDtypeStruct((half * str...  24.3 us
    all_to_all x1, blocking collectives, on_device(): terms = jnp.sum(lax.all_to_all(terms, WIDTH, 0, 0, tiled=True), axis=0)  21.3 us
    all_to_all x1, blocking collectives, on_device(): summed = jnp.sum(lax.all_to_all(spread, LENGTH, 0, 0, tiled=True), axis=0)  18.6 us
    ppermute x7, starting transfers between devices, shifted(): return lax.ppermute(value, names, pairs)  16.7 us
    pallas_call x1, Pallas kernels, on_device(): pl.pallas_call(net_kernel, out_shape=(jax.ShapeDtypeStruct((window + 1, 9...  16 us
    all_to_all x1, starting transfers between devices, on_device(): terms = jnp.sum(lax.all_to_all(terms, DEPTH, 0, 0, tiled=True), axis=0)  9.75 us
    ppermute x1, starting transfers between devices, on_device(): other = lax.ppermute(owned, 'c', [(0, 1), (1, 0)])  9.07 us
  transfers between devices with their start and end apart: 9, of which 2 were waited for; matrix products, arithmetic and copies ran while one was open for 2% of the time, Pallas kernels for 9%

profile of v1, /device:TPU:1, one launch (start us, length us, event | category | flops | bytes accessed | tf_op | source)
XLA Modules:
  0.0 175.5 jit_solution(7180502206912572626)
XLA Ops:
  0.0 1.3 copy-done
  1.3 1.3 copy-done.2
  2.5 0.7 faces.1
  3.2 1.3 collective-permute-start.5
  4.5 0.0 copy-start.4
  4.5 0.0 copy-start.5
  4.6 0.0 copy-start.6
  4.6 1.4 collective-permute-start.2
  6.0 8.8 %collective-permute-start.1 = (f32[24,8,128]{2,1,0:T(8,128)S(1)}, f32[24,8,128]{2,1,0:T(8,128)S(1)}, u32[]{:S(2)}, u32[]{:S(2)}) collective-permute-start(f32[24,8,128]{2,1,0:T(8,128)S(1)} %get-tuple-element.15), channel_id=1, source_target_pairs={{4,0},{8,4},{12,8},{16,12},{20,16},{24,20},{28,24},{5,1},{9,5},{13... | collective-permute-start | bytes 294920 | tf_op jit(solution)/shard_map/ppermute | solution.py:407
  14.8 1.3 collective-permute-start.3
  16.1 1.3 collective-permute-start.4
  17.4 3.5 %reshape.36.o_ref = bf16[3,48,64,64]{3,2,1,0:T(8,128)(2,1)S(1)} reshape(bf16[3,48,4096]{2,1,0:T(8,128)(2,1)} %param.6) | data formatting | bytes 2359296 | tf_op jit(solution)/shard_map/reshape | solution.py:456
  20.9 0.0 copy-done.4
  20.9 0.0 collective-permute-done.2.yxf_ref
  20.9 1.3 collective-permute-start.6
  22.2 0.0 collective-permute-done.5.zyf_ref
  22.3 1.3 collective-permute-start
  23.6 0.0 copy-done.5
  23.6 0.0 copy-done.6
  23.6 0.0 copy-start.1
  23.6 0.0 copy-start.3
  23.6 16.0 %net.1 = (f32[29,9,32,128]{3,2,1,0:T(8,128)S(1)}, f32[13,24,128]{2,1,0:T(8,128)S(1)}, f32[6,32,128]{2,1,0:T(8,128)S(1)}, bf16[64,192]{1,0:T(8,128)(2,1)S(1)}, bf16[2,512,128]{2,1,0:T(8,128)(2,1)S(1)}) custom-call(s32[384]{0:T(512)S(1)} %copy-done.4, bf16[3,48,64,64]{3,2,1,0:T(8,128)(2,1)S(1)} %reshape.36.o_ref, s32[1,384]{1,0:T(1,128)S(1)} %reshape.37.sx_ref, ...), custom_call_target="tpu_custom_call" | custom-call | flops 2000000000 | bytes 6291456 | tf_op jit(solution)/shard_map/net/pallas_call | solution.py:438
  39.6 0.0 copy-start.7
  39.6 2.0 %copy-done.7 = f32[29,9,32,128]{3,2,1,0:T(8,128)} copy-done((f32[29,9,32,128]{3,2,1,0:T(8,128)}, f32[29,9,32,128]{3,2,1,0:T(8,128)S(1)}, u32[]{:S(2)}) %copy-start.7) | copy-done | bytes 4276248
  41.5 0.0 collective-permute-done.6.zxyf_ref
  41.5 0.0 collective-permute-done.xf_ref
  41.5 0.0 collective-permute-done.1.yf_ref
  41.5 0.0 collective-permute-done.3.zf_ref
  41.6 0.0 collective-permute-done.4.zxf_ref
  41.6 24.3 %elements.1 = f32[2816,128]{1,0:T(8,128)S(1)} custom-call(s32[384]{0:T(512)S(1)} %copy-done.4, f32[13,24,128]{2,1,0:T(8,128)S(1)} %get-tuple-element.13.coef_ref, f32[24,3,32,128]{3,2,1,0:T(8,128)S(1)} %copy-done.1, f32[24,3,32,128]{3,2,1,0:T(8,128)S(1)} %copy-done.3, f32[6,32,128]{2,1,0:T(8,128)S(1)} %collective-permute-done.xf_ref, ...), custom_call_target="tpu_custom_call" | custom-call | flops 10000000000 | bytes 10485760 | tf_op jit(solution)/shard_map/elements/pallas_call | solution.py:460
  65.9 21.3 %all_to_all.30 = f32[8,352,128]{2,1,0:T(8,128)S(1)} all-to-all(f32[8,352,128]{2,1,0:T(8,128)S(1)} %bitcast.14), channel_id=1, replica_groups=mesh['zl'=2,'y'=8,'x'=4,'c'=2,'zh'=4] {'x','c'}, dimensions={0} | all-to-all | bytes 2883584 | tf_op jit(solution)/shard_map/all_to_all | solution.py:485
  87.1 0.8 reduce_sum.36
  87.9 9.7 %all-to-all-start.1 = ((f32[4,88,128]{2,1,0:T(8,128)}), f32[4,88,128]{2,1,0:T(8,128)S(1)}, u32[]{:S(2)}, u32[]{:S(2)}) async-start(f32[4,88,128]{2,1,0:T(8,128)} %bitcast.4), calls=%async_computation.1 | async-start | bytes 360448 | tf_op jit(solution)/shard_map/all_to_all | solution.py:487
  97.6 0.6 dynamic_slice.3
  98.9 6.3 %all-to-all-done.1 = f32[4,88,128]{2,1,0:T(8,128)S(1)} async-done(((f32[4,88,128]{2,1,0:T(8,128)}), f32[4,88,128]{2,1,0:T(8,128)S(1)}, u32[]{:S(2)}, u32[]{:S(2)}) %all-to-all-start.1) | async-done | bytes 180256 | tf_op jit(solution)/shard_map/all_to_all | solution.py:487
  105.3 0.4 dynamic_update_slice.3
  105.7 18.6 %all_to_all.31 = f32[16,10,128]{2,1,0:T(8,128)S(1)} all-to-all(f32[16,10,128]{2,1,0:T(8,128)S(1)} %pad_maximum_fusion), channel_id=1, replica_groups=mesh['zl'=2,'y'=8,'x'=4,'c'=2,'zh'=4] {'zl','y'}, dimensions={0} | all-to-all | bytes 163840 | tf_op jit(solution)/shard_map/all_to_all | solution.py:502
  124.3 0.6 slice_reduce_fusion
  125.7 10.5 %all_to_all.32 = f32[16,9,128]{2,1,0:T(8,128)S(1)} all-to-all(f32[16,9,128]{2,1,0:T(8,128)S(1)} %broadcast_in_dim.12), channel_id=1, replica_groups=mesh['zl'=2,'y'=8,'x'=4,'c'=2,'zh'=4] {'zl','y'}, dimensions={0} | all-to-all | bytes 147456 | tf_op jit(solution)/shard_map/all_to_all | solution.py:508
  136.2 11.3 %all_to_all.33 = f32[4,16,9,128]{3,1,2,0:T(8,128)S(1)} all-to-all(f32[4,16,9,128]{3,1,2,0:T(8,128)S(1)} %broadcast_in_dim.13), channel_id=1, replica_groups=mesh['zl'=2,'y'=8,'x'=4,'c'=2,'zh'=4] {'zh'}, dimensions={0} | all-to-all | bytes 589824 | tf_op jit(solution)/shard_map/all_to_all | solution.py:508
  147.6 0.1 broadcast_in_dim.28
  147.7 12.9 %all_to_all.34 = f32[4,4,16,9,128]{4,2,3,1,0:T(8,128)S(1)} all-to-all(f32[4,4,16,9,128]{4,2,3,1,0:T(8,128)S(1)} %broadcast_in_dim.28), channel_id=1, replica_groups=mesh['zl'=2,'y'=8,'x'=4,'c'=2,'zh'=4] {'x'}, dimensions={0} | all-to-all | bytes 2359296 | tf_op jit(solution)/shard_map/all_to_all | solution.py:508
  160.6 9.1 %collective-permute-start.7 = (f32[4,4,16,9,128]{4,2,3,1,0:T(8,128)S(1)}, f32[4,4,16,9,128]{4,2,3,1,0:T(8,128)S(1)}, u32[]{:S(2)}, u32[]{:S(2)}) collective-permute-start(f32[4,4,16,9,128]{4,2,3,1,0:T(8,128)S(1)} %all_to_all.34), channel_id=1, source_target_pairs={{0,4},{4,0},{1,5},{5,1},{2,6},{6,2},{3,7},{7,3},{8,12},{12,8},{9,1... | collective-permute-start | bytes 3538952 | tf_op jit(solution)/shard_map/ppermute | solution.py:509
  169.6 2.4 %collective-permute-done.7 = f32[4,4,16,9,128]{4,2,3,1,0:T(8,128)S(1)} collective-permute-done((f32[4,4,16,9,128]{4,2,3,1,0:T(8,128)S(1)}, f32[4,4,16,9,128]{4,2,3,1,0:T(8,128)S(1)}, u32[]{:S(2)}, u32[]{:S(2)}) %collective-permute-start.7) | collective-permute-done | bytes 1179680 | tf_op jit(solution)/shard_map/ppermute | solution.py:509
  172.1 0.2 broadcast_select_fusion.1
  172.3 0.2 maximum_bitcast_fusion
  172.5 0.9 copy.11
  173.5 2.0 %reshape.43 = f32[3,48,4096]{2,1,0:T(8,128)} reshape(f32[3,16,3,4,2,4,128]{6,5,4,3,2,1,0:T(4,128)S(1)} %copy.11) | data formatting | bytes 4718592 | tf_op jit(solution)/shard_map/reshape | solution.py:513
  (18 shorter events, 0.2 us)
Async XLA Ops:
  0.0 1.3 copy-start
  1.3 1.3 copy-start.2
  3.2 19.0 %collective-permute-start.5 = (f32[6,8,128]{2,1,0:T(8,128)S(1)}, f32[6,8,128]{2,1,0:T(8,128)S(1)}, u32[]{:S(2)}, u32[]{:S(2)}) collective-permute-start(f32[6,8,128]{2,1,0:T(8,128)S(1)} %slice.20), channel_id=1, source_target_pairs={{5,0},{6,1},{7,2},{9,4},{10,5},{11,6},{13,8},{14,9},{15,10},{17,12... | collective-permute-start | bytes 73736 | tf_op jit(solution)/shard_map/ppermute | solution.py:407
  4.5 16.4 %copy-start.4 = (s32[384]{0:T(512)S(1)}, s32[384]{0:T(512)}, u32[]{:S(2)}) copy-start(s32[384]{0:T(512)} %sx_smem.3) | copy-start | bytes 4612
  4.5 19.0 %copy-start.5 = (s32[512]{0:T(512)S(1)}, s32[512]{0:T(512)}, u32[]{:S(2)}) copy-start(s32[512]{0:T(512)} %param.11) | copy-start | bytes 6148
  4.6 19.0 %copy-start.6 = (s32[256]{0:T(256)S(1)}, s32[256]{0:T(256)}, u32[]{:S(2)}) copy-start(s32[256]{0:T(256)} %param.10) | copy-start | bytes 3076
  4.6 16.4 %collective-permute-start.2 = (f32[8,128]{1,0:T(8,128)S(1)}, f32[8,128]{1,0:T(8,128)S(1)}, u32[]{:S(2)}, u32[]{:S(2)}) collective-permute-start(f32[8,128]{1,0:T(8,128)S(1)} %slice_bitcast_fusion), channel_id=1, source_target_pairs={{36,0},{40,4},{44,8},{48,12},{52,16},{56,20},{60,24},{68,32},{72,3... | collective-permute-start | bytes 12296 | tf_op jit(solution)/shard_map/ppermute | solution.py:407
  6.0 35.6 %collective-permute-start.1 = (f32[24,8,128]{2,1,0:T(8,128)S(1)}, f32[24,8,128]{2,1,0:T(8,128)S(1)}, u32[]{:S(2)}, u32[]{:S(2)}) collective-permute-start(f32[24,8,128]{2,1,0:T(8,128)S(1)} %get-tuple-element.15), channel_id=1, source_target_pairs={{4,0},{8,4},{12,8},{16,12},{20,16},{24,20},{28,24},{5,1},{9,5},{13... | collective-permute-start | bytes 294920 | tf_op jit(solution)/shard_map/ppermute | solution.py:407
  14.8 26.8 %collective-permute-start.3 = (f32[6,32,128]{2,1,0:T(8,128)S(1)}, f32[6,32,128]{2,1,0:T(8,128)S(1)}, u32[]{:S(2)}, u32[]{:S(2)}) collective-permute-start(f32[6,32,128]{2,1,0:T(8,128)S(1)} %get-tuple-element.16), channel_id=1, source_target_pairs={{1,0},{2,1},{3,2},{5,4},{6,5},{7,6},{9,8},{10,9},{11,10},{13,12},{... | collective-permute-start | bytes 294920 | tf_op jit(solution)/shard_map/ppermute | solution.py:407
  16.1 25.5 %collective-permute-start.4 = (f32[6,32,128]{2,1,0:T(8,128)S(1)}, f32[6,32,128]{2,1,0:T(8,128)S(1)}, u32[]{:S(2)}, u32[]{:S(2)}) collective-permute-start(f32[6,32,128]{2,1,0:T(8,128)S(1)} %get-tuple-element.16), channel_id=1, source_target_pairs={{33,0},{34,1},{35,2},{65,32},{66,33},{67,34},{97,64},{98,65},{99,6... | collective-permute-start | bytes 294920 | tf_op jit(solution)/shard_map/ppermute | solution.py:407
  20.9 20.6 %collective-permute-start.6 = (f32[6,8,128]{2,1,0:T(8,128)S(1)}, f32[6,8,128]{2,1,0:T(8,128)S(1)}, u32[]{:S(2)}, u32[]{:S(2)}) collective-permute-start(f32[6,8,128]{2,1,0:T(8,128)S(1)} %slice.20), channel_id=1, source_target_pairs={{37,0},{38,1},{39,2},{41,4},{42,5},{43,6},{45,8},{46,9},{47,10},{4... | collective-permute-start | bytes 73736 | tf_op jit(solution)/shard_map/ppermute | solution.py:407
  22.3 19.3 %collective-permute-start = (f32[6,32,128]{2,1,0:T(8,128)S(1)}, f32[6,32,128]{2,1,0:T(8,128)S(1)}, u32[]{:S(2)}, u32[]{:S(2)}) collective-permute-start(f32[6,32,128]{2,1,0:T(8,128)S(1)} %get-tuple-element.14), channel_id=1, source_target_pairs={{32,0},{64,32},{96,64},{128,96},{160,128},{192,160},{224,192},{256... | collective-permute-start | bytes 294920 | tf_op jit(solution)/shard_map/ppermute | solution.py:407
  23.6 18.0 %copy-start.1 = (f32[24,3,32,128]{3,2,1,0:T(8,128)S(1)}, f32[24,3,32,128]{3,2,1,0:T(8,128)}, u32[]{:S(2)}) copy-start(f32[24,3,32,128]{3,2,1,0:T(8,128)} %u_ref.3) | copy-start | bytes 3538948
  23.6 18.0 %copy-start.3 = (f32[24,3,32,128]{3,2,1,0:T(8,128)S(1)}, f32[24,3,32,128]{3,2,1,0:T(8,128)}, u32[]{:S(2)}) copy-start(f32[24,3,32,128]{3,2,1,0:T(8,128)} %w_ref.3) | copy-start | bytes 3538948
  39.6 2.0 %copy-start.7 = (f32[29,9,32,128]{3,2,1,0:T(8,128)}, f32[29,9,32,128]{3,2,1,0:T(8,128)S(1)}, u32[]{:S(2)}) copy-start(f32[29,9,32,128]{3,2,1,0:T(8,128)S(1)} %get-tuple-element.18.q_ref) | copy-start | bytes 12828676
  87.9 17.3 %all-to-all-start.1 = ((f32[4,88,128]{2,1,0:T(8,128)}), f32[4,88,128]{2,1,0:T(8,128)S(1)}, u32[]{:S(2)}, u32[]{:S(2)}) async-start(f32[4,88,128]{2,1,0:T(8,128)} %bitcast.4), calls=%async_computation.1 | async-start | bytes 360448 | tf_op jit(solution)/shard_map/all_to_all | solution.py:487
  160.6 11.5 %collective-permute-start.7 = (f32[4,4,16,9,128]{4,2,3,1,0:T(8,128)S(1)}, f32[4,4,16,9,128]{4,2,3,1,0:T(8,128)S(1)}, u32[]{:S(2)}, u32[]{:S(2)}) collective-permute-start(f32[4,4,16,9,128]{4,2,3,1,0:T(8,128)S(1)} %all_to_all.34), channel_id=1, source_target_pairs={{0,4},{4,0},{1,5},{5,1},{2,6},{6,2},{3,7},{7,3},{8,12},{12,8},{9,1... | collective-permute-start | bytes 3538952 | tf_op jit(solution)/shard_map/ppermute | solution.py:509

commit v2 on v1

--- a/solution.py
+++ b/solution.py
@@ -21,6 +21,9 @@
 F32 = jnp.float32
 BF16 = jnp.bfloat16
 MIB = 1 << 20
+FOLD = 1
+DEPTH_SIZE = 4
+PITCH = NCY + 1
 
 
 def spline_weights(t):
@@ -71,14 +74,13 @@
     return lax.dot_general(a, b, (((1,), (0,)), ((), ())), preferred_element_type=F32)
 
 
-def face_kernel(u_ref, w_ref, x_ref, y_ref, z_ref):
+def face_kernel(u_ref, w_ref, y_ref, z_ref):
     layers = u_ref.shape[0]
     rows, lanes = u_ref.shape[2], u_ref.shape[3]
     lane = lax.broadcasted_iota(jnp.int32, (rows, lanes), 1)
     for f in range(6):
         source = (u_ref, w_ref)[f // 3]
         c = f % 3
-        x_ref[f] = source[0, c]
         packed = jnp.zeros((rows, lanes), F32)
         for i in range(layers):
             y_ref[i, pl.ds(f, 1)] = source[i, c, pl.ds(0, 1)]
@@ -89,12 +91,32 @@
         y_ref[i, pl.ds(6, 2)] = jnp.zeros((2, lanes), F32)
 
 
-def net_kernel(
-    sx_smem, o_ref, sx_ref, sy_ref, sz_ref, q_ref, coef_ref, lin_ref, yb_ref, zb_ref, zf_ref, yf_ref
+def widen_kernel(y_ref, xf_ref, out_ref):
+    layers = y_ref.shape[0]
+    out_ref[pl.ds(0, layers)] = y_ref[...]
+    for f in range(6):
+        out_ref[layers, pl.ds(f, 1)] = xf_ref[f, pl.ds(0, 1)]
+    out_ref[layers, pl.ds(6, 2)] = jnp.zeros((2, out_ref.shape[2]), F32)
+
+
+def deepen_kernel(z_ref, xf_ref, yf_ref, out_ref):
+    layers = yf_ref.shape[0] - 1
+    rows, lanes = z_ref.shape[1:]
+    lane = lax.broadcasted_iota(jnp.int32, (rows, lanes), 1)
+    edge = jnp.zeros((8, lanes), F32)
+    for i in range(layers + 1):
+        value = yf_ref[i]
+        edge = jnp.where(lane[:8] == i, value if i == 0 else pltpu.roll(value, i, 1), edge)
+    for f in range(6):
+        far = pltpu.roll(xf_ref[f], layers, 1)
+        out_ref[f, pl.ds(0, rows)] = jnp.where(lane == layers, far, z_ref[f])
+        out_ref[f, pl.ds(rows, 8)] = jnp.broadcast_to(edge[f : f + 1], (8, lanes))
+
+
+def table_kernel(
+    nx, sx_ref, sy_ref, sz_ref, coef_ref, lin_ref, yb_ref, zb_ref, zf_ref, yf_ref
 ):
-    window = q_ref.shape[0] - 1
-    ny, nz = q_ref.shape[2:]
-    nx = window - 4
+    ny, nz = lin_ref.shape[1:]
     nodes_x, nodes_y, nodes_z = sx_ref.shape[1], sy_ref.shape[1], sz_ref.shape[1]
     step_x = 2.0 * nodes_x / (NCX - 3)
     step_y = 2.0 * nodes_y / (NCY - 3)
@@ -129,8 +151,19 @@
     y_rows = element_rows(lower, upper, (lane % NCY).astype(F32), live_y)
     for r, step in enumerate((step_x, step_y, step_z)):
         hi, lo = split(step * y_rows)
-        yf_ref[r] = jnp.concatenate([hi, lo[:, :NCY]], axis=1)
-    paired = 2 * (lane % half) + (lane % NCY) // half
+        some = jnp.concatenate([hi, lo[:, :NCY]], axis=1)
+        none = jnp.zeros_like(some)
+        yf_ref[r] = jnp.concatenate(
+            [
+                jnp.concatenate([some if g == h else none for h in range(FOLD)], axis=1)
+                for g in range(FOLD)
+            ],
+            axis=0,
+        )
+    place = lane % half
+    core = (lax.axis_index("c") + 2 * place // half) % 2
+    owner = (place % (half // 2)) // DEPTH_SIZE * 2 + core
+    paired = 2 * (owner * DEPTH_SIZE + place % DEPTH_SIZE) + (lane % NCY) // half
     y_rows = element_rows(lower, upper, paired.astype(F32), live_y)
     turned = jnp.transpose(jnp.concatenate([y_rows, y_rows], axis=0))[:NCY]
     hi, lo = split(turned)
@@ -155,11 +188,13 @@
             [jnp.where(wide < NCZ, z_rows, 0.0), jnp.where(wide < NCZ, 0.0, z_rows)], axis=0
         )
     )
-    zb_ref[0] = hi
-    zb_ref[1] = lo
-    hi, lo = split(jnp.transpose(z_rows)[:NCZ])
-    zf_ref[0] = hi
-    zf_ref[1] = lo
+    zb_ref[...] = jnp.concatenate([hi, lo], axis=1)
+    turned = jnp.transpose(z_rows)
+    tall = lax.broadcasted_iota(jnp.int32, turned.shape, 0) < NCZ
+    hi, lo = split(
+        jnp.concatenate([jnp.where(tall, turned, 0.0), jnp.where(tall, 0.0, turned)], axis=1)
+    )
+    zf_ref[...] = jnp.concatenate([hi, lo], axis=0)
     place = (upper[0] + lower[0]) + (upper[1] + lower[1]) + (2.0 - (NCZ - 1))
     rise = (upper[0] - lower[0]) + (upper[1] - lower[1])
     place = jnp.transpose(jnp.broadcast_to(step_z * place, (nz, lanes)))[:ny]
@@ -167,20 +202,52 @@
     lin_ref[2] = jnp.where(live, place, 0.0)
     lin_ref[3] = jnp.where(live, rise, 0.0)
 
+
+def net_kernel(sx_smem, o_ref, zf_ref, yf_ref, q_ref, plain_ref, slope_ref):
+    window = q_ref.shape[0] - 1
+    ny, nz = q_ref.shape[2:]
+    lanes = 2 * NCZ
+    half = NCY // 2
+    start_x = lax.axis_index(LENGTH) * (window - 4)
+    group = 8
+
+    def along_z(step, carry):
+        r = step // (half // group)
+        pair = lax.rem(step, half // group) * group
+        wide = [
+            o_ref[r, :, pl.ds(pl.multiple_of((pair + g) * lanes, lanes), lanes)]
+            for g in range(group)
+        ]
+        wide = jnp.concatenate(wide, axis=0)
+        full = dot(jnp.concatenate([wide, wide], axis=1), zf_ref[...])
+        for g in range(group):
+            part = full[g * NCX : (g + 1) * NCX]
+            for p in range(2):
+                rows = pl.ds(r * NCX * PITCH + 2 * (pair + g) + p, NCX, stride=PITCH)
+                plain_ref[rows] = part[:, 2 * p * nz : (2 * p + 1) * nz]
+                slope_ref[rows] = part[:, (2 * p + 1) * nz : (2 * p + 2) * nz]
+        return carry
+
+    lax.fori_loop(0, 3 * half // group, along_z, 0)
+
     start = jnp.minimum(sx_smem[start_x], NCX - window)
 
-    def step(t, carry):
+    def along_y(step, carry):
         for r in range(3):
-            o = o_ref[r, start + t]
-            along_z = dot(o, zf_ref[0]) + dot(o, zf_ref[1])
-            high, low = split(along_z)
-            full = dot(yf_ref[r], jnp.concatenate([high, low, high], axis=0))
-            q_ref[t, 3 * r] = full[:ny, :nz]
-            q_ref[t, 3 * r + 1] = full[ny:, :nz]
-            q_ref[t, 3 * r + 2] = full[:ny, nz:]
+            both = []
+            for g in range(FOLD):
+                rows = pl.ds((r * NCX + start + step * FOLD + g) * PITCH, NCY)
+                hi, lo = split(jnp.concatenate([plain_ref[rows], slope_ref[rows]], axis=1))
+                both += [hi, lo, hi]
+            full = dot(yf_ref[r], jnp.concatenate(both, axis=0))
+            for g in range(FOLD):
+                part = full[g * 2 * ny : (g + 1) * 2 * ny]
+                q_ref[step * FOLD + g, 3 * r] = part[:ny, :nz]
+                q_ref[step * FOLD + g, 3 * r + 1] = part[ny:, :nz]
+                q_ref[step * FOLD + g, 3 * r + 2] = part[:ny, nz:]
         return carry
 
-    lax.fori_loop(0, window, step, 0)
+    lax.fori_loop(0, window // FOLD, along_y, 0, unroll=4)
     q_ref[window] = jnp.zeros(q_ref.shape[1:], F32)
 
 
@@ -248,8 +315,8 @@
 
 
 def element_kernel(
-    sx_smem, coef_ref, u_ref, w_ref, xf_ref, yf_ref, yxf_ref, zf_ref, zxf_ref, zyf_ref, zxyf_ref,
-    lin_ref, q_ref, yb_ref, zb_ref, out_ref, raw, side, sums, diffs, planes, acc, left_hi, left_lo,
+    sx_smem, coef_ref, u_ref, w_ref, xf_ref, yf_ref, zf_ref, lin_ref, q_ref, yb_ref, zb_ref,
+    keep_ref, send_ref, raw, sums, diffs, planes, acc, left_hi, left_lo, stage,
 ):
     layers, _, ny, nz = u_ref.shape
     window = q_ref.shape[0] - 1
@@ -259,32 +326,28 @@
     rows = ny + 8
     lane = lax.broadcasted_iota(jnp.int32, (rows, nz), 1)
 
-    for f in range(6):
-        far = pltpu.roll(zxf_ref[f], layers, 1)
-        side[f, pl.ds(0, ny)] = jnp.where(lane[:ny] == layers, far, zf_ref[f])
-        far = pltpu.roll(zxyf_ref[f], layers, 1)
-        side[f, pl.ds(ny, 8)] = jnp.where(lane[:8] == layers, far, zyf_ref[f])
     acc[...] = jnp.zeros(acc.shape, F32)
 
     def make_planes(i):
         slot = lax.rem(i, 2)
 
+        edge = yf_ref[i]
+        for f in range(6):
+            raw[f, pl.ds(ny, 1)] = edge[f : f + 1]
+
         @pl.when(i < layers)
         def _():
-            edge = yf_ref[i]
             for f in range(6):
                 raw[f, pl.ds(0, ny)] = (u_ref, w_ref)[f // 3][i, f % 3]
-                raw[f, pl.ds(ny, 1)] = edge[f : f + 1]
 
         @pl.when(i >= layers)
         def _():
             for f in range(6):
                 raw[f, pl.ds(0, ny)] = xf_ref[f]
-                raw[f, pl.ds(ny, 1)] = yxf_ref[pl.ds(f, 1)]
 
         for f in range(6):
             here = raw[f]
-            beyond = pltpu.roll(side[f], nz - 1 - i, 1)
+            beyond = pltpu.roll(zf_ref[f], nz - 1 - i, 1)
             there = jnp.where(lane == nz - 1, beyond, pltpu.roll(here, nz - 1, 1))
             sums[f] = here + there
             diffs[f] = there - here
@@ -368,102 +431,183 @@
 
     lax.fori_loop(0, window, along_width, 0)
 
-    stride = out_ref.shape[0] // half
+    kept = half // 2
+    rows_out = keep_ref.shape[0] // kept
+    pitch = rows_out + 1
     batch = 12
 
     def along_depth(step, carry):
         at = pl.ds(pl.multiple_of(step * batch * half, half), batch * half)
-        hi, lo = left_hi[at], left_lo[at]
-        full = dot(hi, zb_ref[0]) + dot(lo, zb_ref[0]) + dot(hi, zb_ref[1])
+        full = dot(left_hi[at], zb_ref[...])
+        full = full[:, : 2 * NCZ] + full[:, 2 * NCZ :] + dot(left_lo[at], zb_ref[:, : 2 * NCZ])
         for b in range(batch):
-            out_ref[pl.ds(step * batch + b, half, stride=stride)] = full[b * half : (b + 1) * half]
+            stage[pl.ds(step * batch + b, half, stride=pitch)] = full[b * half : (b + 1) * half]
         return carry
 
     lax.fori_loop(0, 3 * window // batch, along_depth, 0)
 
     total = jnp.sum(volume, axis=0, keepdims=True)
-    out_ref[pl.ds(3 * window, half, stride=stride)] = jnp.broadcast_to(total, (half, nz))
-    for spare in range(3 * window + 1, stride):
-        out_ref[pl.ds(spare, half, stride=stride)] = jnp.zeros((half, nz), F32)
+    spare = lax.broadcasted_iota(jnp.int32, (rows_out - 3 * window, nz), 0)
+    last = jnp.where(spare == 0, jnp.broadcast_to(total, spare.shape), 0.0)
+    for q in range(half):
+        out_ref = keep_ref if q < kept else send_ref
+        base = (q % kept) * rows_out
+        out_ref[pl.ds(base, 3 * window)] = stage[pl.ds(q * pitch, 3 * window)]
+        out_ref[pl.ds(base + 3 * window, rows_out - 3 * window)] = last
+
+
+def spread_kernel(sx_smem, in_ref, out_ref, dense):
+    parts, depth, rows, lanes = in_ref.shape
+    blocks, each = out_ref.shape[0] // depth, out_ref.shape[1] - 8
+    owners = lax.axis_size(LENGTH)
+    nx = sx_smem.shape[0] // owners
+    window = nx + 4
+    start = jnp.minimum(sx_smem[lax.axis_index(LENGTH) * nx], NCX - window)
+    dense[...] = jnp.zeros(dense.shape, F32)
+    row = lax.broadcasted_iota(jnp.int32, (8, lanes), 0)
+    for d in range(depth):
+        total = in_ref[0, d]
+        for p in range(1, parts):
+            total = total + in_ref[p, d]
+        dense[pl.ds(3 * start, 3 * window)] = total[: 3 * window]
+        last = jnp.where(row == 0, total[3 * window : 3 * window + 1], 0.0)
+        for block in range(blocks):
+            at = block * depth + d
+            out_ref[at, pl.ds(0, each)] = dense[pl.ds(block * each, each)]
+            out_ref[at, pl.ds(each, 8)] = last
+
+
+def divide_kernel(in_ref, out_ref, total):
+    value = in_ref[0]
+    for p in range(1, in_ref.shape[0]):
+        value = value + in_ref[p]
+    total[...] = value
+    owners = out_ref.shape[0]
+    rows = in_ref.shape[1] - 8
+    each = rows // owners
+    for owner in range(owners):
+        out_ref[owner, pl.ds(0, each)] = total[pl.ds(owner * each, each)]
+        out_ref[owner, pl.ds(each, 16 - each)] = total[pl.ds(rows, 16 - each)]
+
+
+def scale_kernel(elements, part, in_ref, out_ref):
+    total = in_ref[0]
+    for p in range(1, in_ref.shape[0]):
+        total = total + in_ref[p]
+    volume = jnp.sum(total[part : part + 1], axis=1, keepdims=True)
+    total = total * (elements * MU_SHEAR / volume)
+    for p in range(in_ref.shape[0]):
+        out_ref[p] = total
+
+
+def pack_kernel(in_ref, out_ref):
+    owners = in_ref.shape[0]
+    each = out_ref.shape[1] // owners
+    for copy in range(out_ref.shape[0]):
+        for owner in range(owners):
+            out_ref[copy, pl.ds(owner * each, each)] = in_ref[owner, pl.ds(0, each)]
+
+
+def repack_kernel(in_ref, out_ref, plane):
+    copies, blocks, rows, lanes = out_ref.shape
+    depth = blocks // 3
+    parts = in_ref.shape[0] // depth
+    each = rows // parts
+    for r in range(3):
+        for d in range(depth):
+            for part in range(parts):
+                plane[pl.ds(part * each, each)] = in_ref[part * depth + d, pl.ds(r, each, stride=3)]
+            value = plane[...]
+            for copy in range(copies):
+                out_ref[copy, r * depth + d] = value
+
+
+def place_kernel(own_ref, other_ref, out_ref):
+    chips, blocks, rows, lanes = own_ref.shape
+    depth = blocks // 3
+    core = lax.axis_index("c")
+    for ref, c in ((own_ref, core), (other_ref, 1 - core)):
+        for x in range(chips):
+            for r in range(3):
+                for d in range(depth):
+                    at = ((2 * x + c) * depth + d) * lanes
+                    out_ref[r, :, pl.ds(pl.multiple_of(at, lanes), lanes)] = ref[x, r * depth + d]
 
 
 def shifted(value, axes, sizes):
-    names = sum(axes, ())
-    dims = [sizes[a] for a in axes]
-    pairs = []
-    count = 1
-    for d in dims:
-        count *= d
-    for flat in range(count):
-        rest, index = flat, []
-        for d in reversed(dims):
-            index.insert(0, rest % d)
-            rest //= d
-        if all(v > 0 for v in index):
-            target = 0
-            for v, d in zip(index, dims):
-                target = target * d + v - 1
-            pairs.append((flat, target))
-    return lax.ppermute(value, names, pairs)
-
-
-def on_device(sizes, offsets, displacement, adjoint, span_x, span_y, span_z):
+    return lax.ppermute(value, axes, [(i, i - 1) for i in range(1, sizes[axes])])
+
+
+VMEM = pl.BlockSpec(memory_space=pltpu.VMEM)
+SMEM = pl.BlockSpec(memory_space=pltpu.SMEM)
+
+
+def call(kernel, out_shape, *operands, scratch=(), limit=16, flops=10**6):
+    return pl.pallas_call(
+        kernel,
+        out_shape=out_shape,
+        in_specs=[SMEM if o.ndim == 1 else VMEM for o in operands],
+        out_specs=jax.tree.map(lambda _: VMEM, out_shape),
+        scratch_shapes=[pltpu.VMEM(shape, dtype) for shape, dtype in scratch],
+        name=getattr(kernel, "func", kernel).__name__.removesuffix("_kernel"),
+        compiler_params=pltpu.CompilerParams(vmem_limit_bytes=limit * MIB),
+        cost_estimate=pl.CostEstimate(flops=flops, bytes_accessed=MIB, transcendentals=0),
+    )(*operands)
+
+
+def array(*shape, dtype=F32):
+    return jax.ShapeDtypeStruct(shape, dtype)
+
+
+def brick_faces(displacement, adjoint):
     nx, _, ny, nz = displacement.shape
-    nodes_x, nodes_y, nodes_z = span_x.shape[0], span_y.shape[0], span_z.shape[0]
-    vmem = pl.BlockSpec(memory_space=pltpu.VMEM)
-    smem = pl.BlockSpec(memory_space=pltpu.SMEM)
-
-    x_face, y_face, z_face = pl.pallas_call(
-        face_kernel,
-        out_shape=(
-            jax.ShapeDtypeStruct((6, ny, nz), F32),
-            jax.ShapeDtypeStruct((nx, 8, nz), F32),
-            jax.ShapeDtypeStruct((6, ny, nz), F32),
+    return call(face_kernel, (array(nx, 8, nz), array(6, ny, nz)), displacement, adjoint)
+
+
+def brick_tables(shape, span_x, span_y, span_z):
+    nx, _, ny, nz = shape
+    return call(
+        functools.partial(table_kernel, nx),
+        (
+            array(13, -(-nx // 8) * 8, nz),
+            array(6, ny, nz),
+            array(NCY, 6 * ny, dtype=BF16),
+            array(4 * nz, 4 * NCZ, dtype=BF16),
+            array(4 * NCZ, 4 * nz, dtype=BF16),
+            array(3, FOLD * 2 * ny, FOLD * 3 * NCY, dtype=BF16),
         ),
-        in_specs=[vmem] * 2,
-        out_specs=(vmem,) * 3,
-        name="faces",
-        compiler_params=pltpu.CompilerParams(vmem_limit_bytes=16 * MIB),
-    )(displacement, adjoint)
-    xf = shifted(x_face, (LENGTH,), sizes)
-    yf = shifted(y_face, (WIDTH,), sizes)
-    zf = shifted(z_face, (DEPTH,), sizes)
-    yxf = shifted(y_face[0], (LENGTH, WIDTH), sizes)
-    zxf = shifted(z_face, (LENGTH, DEPTH), sizes)
-    zyf = shifted(z_face[:, :8], (WIDTH, DEPTH), sizes)
-    zxyf = shifted(z_face[:, :8], (LENGTH, WIDTH, DEPTH), sizes)
-
+        *[s.reshape(1, s.shape[0]) for s in (span_x, span_y, span_z)],
+        flops=10**7,
+    )
+
+
+def brick_net(shape, offsets, span_x, z_front, y_front):
+    nx, _, ny, nz = shape
+    return call(
+        net_kernel,
+        array(nx + 5, 9, ny, nz),
+        span_x,
+        offsets,
+        z_front,
+        y_front,
+        scratch=[((3 * NCX * PITCH, nz), F32)] * 2,
+        limit=20,
+        flops=2 * 10**9,
+    )
+
+
+def brick_terms(span_x, tables, net, displacement, adjoint, halos):
+    nx, _, ny, nz = displacement.shape
+    coef, linear, y_back, z_back = tables[:4]
     window = nx + 4
-    spans = [s.reshape(1, s.shape[0]) for s in (span_x, span_y, span_z)]
-    net, coef, linear, y_back, z_back = pl.pallas_call(
-        net_kernel,
-        out_shape=(
-            jax.ShapeDtypeStruct((window + 1, 9, ny, nz), F32),
-            jax.ShapeDtypeStruct((13, -(-nx // 8) * 8, nz), F32),
-            jax.ShapeDtypeStruct((6, ny, nz), F32),
-            jax.ShapeDtypeStruct((NCY, 6 * ny), BF16),
-            jax.ShapeDtypeStruct((2, 4 * nz, 2 * NCZ), BF16),
-        ),
-        in_specs=[smem] + [vmem] * 4,
-        out_specs=(vmem,) * 5,
-        scratch_shapes=[
-            pltpu.VMEM((2, NCZ, 2 * nz), BF16),
-            pltpu.VMEM((3, 2 * ny, 3 * NCY), BF16),
-        ],
-        name="net",
-        compiler_params=pltpu.CompilerParams(vmem_limit_bytes=24 * MIB),
-        cost_estimate=pl.CostEstimate(flops=2 * 10**9, bytes_accessed=6 * MIB, transcendentals=0),
-    )(span_x, offsets.reshape(3, NCX, NCY, NCZ), *spans)
-
     half = NCY // 2
     stride = -(-(3 * window + 1) // 8) * 8
-    terms = pl.pallas_call(
+    return pl.pallas_call(
         element_kernel,
-        out_shape=jax.ShapeDtypeStruct((half * stride, 2 * NCZ), F32),
-        in_specs=[smem] + [vmem] * 14,
-        out_specs=vmem,
+        out_shape=(jax.ShapeDtypeStruct((half // 2 * stride, 2 * NCZ), F32),) * 2,
+        in_specs=[SMEM] + [VMEM] * 10,
+        out_specs=(VMEM,) * 2,
         scratch_shapes=[
-            pltpu.VMEM((6, ny + 8, nz), F32),
             pltpu.VMEM((6, ny + 8, nz), F32),
             pltpu.VMEM((6, ny + 8, nz), F32),
             pltpu.VMEM((6, ny + 8, nz), F32),
@@ -471,46 +615,66 @@
             pltpu.VMEM((window + 1, 9, ny, nz), F32),
             pltpu.VMEM((3 * window * half, 4 * nz), BF16),
             pltpu.VMEM((3 * window * half, 4 * nz), BF16),
+            pltpu.VMEM((half * (stride + 1), 2 * NCZ), F32),
         ],
         name="elements",
-        compiler_params=pltpu.CompilerParams(vmem_limit_bytes=48 * MIB),
+        compiler_params=pltpu.CompilerParams(vmem_limit_bytes=24 * MIB),
         cost_estimate=pl.CostEstimate(flops=10**10, bytes_accessed=10 * MIB, transcendentals=0),
-    )(
-        span_x, coef, displacement, adjoint, xf, yf, yxf, zf, zxf, zyf, zxyf,
-        linear, net, y_back, z_back,
-    )
-
-    size_w, size_d = sizes[WIDTH], sizes[DEPTH]
-    terms = terms.reshape(size_w, size_d * stride, 2 * NCZ)
-    terms = jnp.sum(lax.all_to_all(terms, WIDTH, 0, 0, tiled=True), axis=0)
-    terms = terms.reshape(size_d, stride, 2 * NCZ)
-    terms = jnp.sum(lax.all_to_all(terms, DEPTH, 0, 0, tiled=True), axis=0)
-    size_l = sizes[LENGTH]
-    part = 3 * NCX // size_l
-    start = lax.dynamic_slice_in_dim(span_x, lax.axis_index(LENGTH) * nx, 1)[0]
-    first_row = jnp.minimum(start, NCX - window)
-    spread = lax.dynamic_update_slice(
-        jnp.zeros((3 * NCX, 2 * NCZ), F32), terms[: 3 * window], (3 * first_row, 0)
-    )
-    spread = jnp.concatenate(
-        [
-            spread.reshape(size_l, part, 2 * NCZ),
-            jnp.broadcast_to(terms[3 * window], (size_l, 1, 2 * NCZ)),
-        ],
-        axis=1,
-    )
-    summed = jnp.sum(lax.all_to_all(spread, LENGTH, 0, 0, tiled=True), axis=0)
+    )(span_x, coef, displacement, adjoint, *halos, linear, net, y_back, z_back)
+
+
+def on_device(sizes, offsets, displacement, adjoint, span_x, span_y, span_z):
+    nodes_x, nodes_y, nodes_z = span_x.shape[0], span_y.shape[0], span_z.shape[0]
+    nx, _, ny, nz = shape = displacement.shape
+    swap = [(0, 1), (1, 0)]
+
+    xf = shifted(jnp.concatenate([displacement[0], adjoint[0]], axis=0), LENGTH, sizes)
+    y_face, z_face = brick_faces(displacement, adjoint)
+    tables = brick_tables(shape, span_x, span_y, span_z)
+    yf = shifted(call(widen_kernel, array(nx + 1, 8, nz), y_face, xf), WIDTH, sizes)
+    net = brick_net(shape, offsets, span_x, *tables[4:])
+    zf = shifted(call(deepen_kernel, array(6, ny + 8, nz), z_face, xf, yf), DEPTH, sizes)
+    keep, send = brick_terms(span_x, tables, net, displacement, adjoint, (xf, yf, zf))
+
+    size_l, size_w, size_d = sizes[LENGTH], sizes[WIDTH], sizes[DEPTH]
+    size_x, size_zl = size_w // 2, 2
+    lanes = 2 * NCZ
+    stride = keep.shape[0] // (size_x * size_d)
+    size_y = size_l // size_zl
+    blocks, part = size_zl * size_d, 3 * NCX // size_l
+    terms = keep + lax.ppermute(send, "c", swap)
+    terms = lax.all_to_all(terms.reshape(size_x, size_d * stride, lanes), "x", 0, 0, tiled=True)
+    terms = call(
+        spread_kernel,
+        array(blocks, part * size_y + 8, lanes),
+        span_x,
+        terms.reshape(size_x, size_d, stride, lanes),
+        scratch=[((3 * NCX, lanes), F32)],
+    )
+    terms = lax.all_to_all(terms, ("zl", "zh"), 0, 0, tiled=True)
+    terms = call(
+        divide_kernel,
+        array(size_y, 16, lanes),
+        terms,
+        scratch=[((part * size_y + 8, lanes), F32)],
+    )
+    terms = lax.all_to_all(terms, "y", 0, 0, tiled=True)
     elements = (nodes_x - 1) * (nodes_y - 1) * (nodes_z - 1)
-    owned = summed[:part] * (elements * MU_SHEAR / jnp.sum(summed[part]))
-    size_x, size_c = size_w // 2, 2
-    for axes, size in ((LENGTH, size_l), (DEPTH, size_d), (("x",), size_x)):
-        owned = jnp.broadcast_to(owned[None], (size,) + owned.shape)
-        owned = lax.all_to_all(owned, axes, 0, 0, tiled=True)
-    other = lax.ppermute(owned, "c", [(0, 1), (1, 0)])
-    core = lax.axis_index("c")
-    both = jnp.stack([jnp.where(core == 0, owned, other), jnp.where(core == 0, other, owned)])
-    both = both.reshape(size_c, size_x, size_d, size_l, part // 3, 3, 2 * NCZ)
-    return both.transpose(5, 3, 4, 1, 0, 2, 6).reshape(3, NCX, NCY * NCZ)
+    rows = call(
+        functools.partial(scale_kernel, elements, part), array(size_y, 16, lanes), terms
+    )
+    rows = lax.all_to_all(rows, "y", 0, 0, tiled=True)
+    rows = call(pack_kernel, array(blocks, part * size_y, lanes), rows)
+    rows = lax.all_to_all(rows, ("zl", "zh"), 0, 0, tiled=True)
+    rows = call(
+        repack_kernel,
+        array(size_x, 3 * size_d, NCX, lanes),
+        rows,
+        scratch=[((NCX, lanes), F32)],
+    )
+    rows = lax.all_to_all(rows, "x", 0, 0, tiled=True)
+    other = lax.ppermute(rows, "c", swap)
+    return call(place_kernel, array(3, NCX, NCY * NCZ), rows, other)
 
 
 def solution(mesh):

time: 176 us -> 150 us (0.85)
  starting transfers between devices: 35.5 us -> 23.5 us
  local copies, waits for them, and re-layouts: 12.2 us -> 3.4 us
  Pallas kernels: 40.9 us -> 32.2 us
  blocking collectives: 74.6 us -> 81.3 us
  other arithmetic: 1.84 us -> 0.08 us
    all_to_all x1 -> x0, starting transfers between devices: 9.75 us -> none  [on_device(): terms = jnp.sum(lax.all_to_all(terms, DEPTH, 0, 0, tiled=True), axis=0)]
    pallas_call x3 -> x12, Pallas kernels: 40.9 us -> 32.2 us  [the longest x1 22.2 us: brick_terms(): pl.pallas_call(element_kernel, out_shape=(jax.ShapeDtypeStruct((half // 2...]
    all_to_all x5 -> x6, blocking collectives: 74.6 us -> 81.3 us  [the longest x1 18.3 us: on_device(): terms = lax.all_to_all(terms, ('zl', 'zh'), 0, 0, tiled=True)]
    all_to_all x1 -> x0, waiting for transfers between devices: 6.33 us -> none  [on_device(): terms = jnp.sum(lax.all_to_all(terms, DEPTH, 0, 0, tiled=True), axis=0)]
    ppermute x8 -> x5, waiting for transfers between devices: 2.46 us -> 8.36 us  [the longest x3 4.11 us: shifted(): lax.ppermute(value, axes, [(i, i - 1) for i in range(1, sizes[axes])])]
    reshape x4 -> x1, local copies, waits for them, and re-layouts: 5.53 us -> 0.01 us  [brick_tables(): s.reshape(1, s.shape[0])]
    ppermute x8 -> x5, starting transfers between devices: 25.7 us -> 23.5 us  [the longest x3 11.8 us: shifted(): lax.ppermute(value, axes, [(i, i - 1) for i in range(1, sizes[axes])])]
    unnamed x16, local copies, waits for them, and re-layouts: 4.54 us -> 2.56 us
  transfers between devices with their start and end apart: 9 -> 5, of which waited for: 2 -> 5; matrix products, arithmetic and copies ran while one was open for 2% -> 0% of each run, Pallas kernels for 9% -> 5%
where the time goes in v2:
time: 150 us; the launch traced here: 149 us
  blocking collectives  81.3 us (54%)
  Pallas kernels  32.2 us (21%)
  starting transfers between devices  23.5 us (16%)
  waiting for transfers between devices  8.36 us (6%)
  local copies, waits for them, and re-layouts  3.4 us (2%)
    pallas_call x1, Pallas kernels, brick_terms(): pl.pallas_call(element_kernel, out_shape=(jax.ShapeDtypeStruct((half // 2...  22.2 us
    all_to_all x1, blocking collectives, on_device(): terms = lax.all_to_all(terms, ('zl', 'zh'), 0, 0, tiled=True)  18.3 us
    all_to_all x1, blocking collectives, on_device(): terms = lax.all_to_all(terms, 'y', 0, 0, tiled=True)  14.6 us
    all_to_all x1, blocking collectives, on_device(): lax.all_to_all(terms.reshape(size_x, size_d * stride, lanes), 'x', 0, 0,...  13.4 us
    all_to_all x1, blocking collectives, on_device(): rows = lax.all_to_all(rows, 'x', 0, 0, tiled=True)  12.9 us
    all_to_all x1, blocking collectives, on_device(): rows = lax.all_to_all(rows, ('zl', 'zh'), 0, 0, tiled=True)  12.6 us
    ppermute x3, starting transfers between devices, shifted(): lax.ppermute(value, axes, [(i, i - 1) for i in range(1, sizes[axes])])  11.8 us
    pallas_call x11, Pallas kernels, call(): pl.pallas_call(kernel, out_shape=out_shape, in_specs=[SMEM if o.ndim == 1...  10 us
  transfers between devices with their start and end apart: 5, of which 5 were waited for; matrix products, arithmetic and copies ran while one was open for 0% of the time, Pallas kernels for 5%

profile of v2, /device:TPU:1, one launch (start us, length us, event | category | flops | bytes accessed | tf_op | source)
XLA Modules:
  0.0 149.0 jit_solution(8738368038261530868)
XLA Ops:
  0.0 0.8 slice_bitcast_fusion
  0.8 1.3 collective-permute-start
  2.1 0.0 copy-start
  2.2 1.3 copy-done
  3.4 0.0 copy-start.2
  3.4 1.3 copy-done.2
  4.7 0.0 copy-start.4
  4.7 0.0 copy-start.6
  4.7 0.0 copy-start.7
  4.7 0.0 copy-start.5
  4.7 0.7 face.1
  5.4 1.5 %collective-permute-done.xf_ref = f32[6,32,128]{2,1,0:T(8,128)S(1)} collective-permute-done((f32[6,32,128]{2,1,0:T(8,128)S(1)}, f32[6,32,128]{2,1,0:T(8,128)S(1)}, u32[]{:S(2)}, u32[]{:S(2)}) %collective-permute-start) | collective-permute-done | bytes 98336 | tf_op jit(solution)/shard_map/ppermute | solution.py:538
  6.9 9.3 %collective-permute-start.1 = (f32[25,8,128]{2,1,0:T(8,128)S(1)}, f32[25,8,128]{2,1,0:T(8,128)S(1)}, u32[]{:S(2)}, u32[]{:S(2)}) collective-permute-start(f32[25,8,128]{2,1,0:T(8,128)S(1)} %widen.1), channel_id=1, source_target_pairs={{4,0},{8,4},{12,8},{16,12},{20,16},{24,20},{28,24},{5,1},{9,5},{13... | collective-permute-start | bytes 307208 | tf_op jit(solution)/shard_map/ppermute | solution.py:538
  16.2 0.0 copy-done.4
  16.2 0.0 copy-done.6
  16.2 0.0 copy-done.7
  16.2 0.6 table.1
  16.8 0.2 collective-permute-done.1.yf_ref
  17.1 0.1 deepen.1
  17.2 1.3 collective-permute-start.2
  18.5 0.0 copy-done.5
  18.5 0.0 copy-start.1
  18.5 0.0 copy-start.3
  18.5 6.1 %net.1.q_ref = f32[29,9,32,128]{3,2,1,0:T(8,128)S(1)} custom-call(s32[384]{0:T(512)S(1)} %copy-done.4, bf16[3,48,4096]{2,1,0:T(8,128)(2,1)S(1)} %copy-done.5, bf16[256,512]{1,0:T(8,128)(2,1)S(1)} %get-tuple-element.19.zf_ref, bf16[3,64,192]{2,1,0:T(8,128)(2,1)S(1)} %get-tuple-element.20.yf_ref), custom_call_target="tpu_custom_call" | custom-call | flops 2000000000 | bytes 1048576 | tf_op jit(solution)/shard_map/net/pallas_call | solution.py:546
  24.7 2.4 %collective-permute-done.2.zf_ref = f32[6,40,128]{2,1,0:T(8,128)S(1)} collective-permute-done((f32[6,40,128]{2,1,0:T(8,128)S(1)}, f32[6,40,128]{2,1,0:T(8,128)S(1)}, u32[]{:S(2)}, u32[]{:S(2)}) %collective-permute-start.2) | collective-permute-done | bytes 122912 | tf_op jit(solution)/shard_map/ppermute | solution.py:538
  27.1 0.0 copy-done.1
  27.1 0.0 copy-done.3
  27.1 22.2 %elements.1 = (f32[1408,128]{1,0:T(8,128)S(1)}, f32[1408,128]{1,0:T(8,128)S(1)}) custom-call(s32[384]{0:T(512)S(1)} %copy-done.4, f32[13,24,128]{2,1,0:T(8,128)S(1)} %get-tuple-element.15.coef_ref, f32[24,3,32,128]{3,2,1,0:T(8,128)S(1)} %copy-done.1, f32[24,3,32,128]{3,2,1,0:T(8,128)S(1)} %copy-done.3, f32[6,32,128]{2,1,0:T(8,128)S(1)} %collective-permute-done.xf_ref, ...), custom_call_target="tpu_custom_call" | custom-call | flops 10000000000 | bytes 10485760 | tf_op jit(solution)/shard_map/elements/pallas_call | solution.py:605
  49.2 2.4 %collective-permute-start.3 = (f32[1408,128]{1,0:T(8,128)S(1)}, f32[1408,128]{1,0:T(8,128)S(1)}, u32[]{:S(2)}, u32[]{:S(2)}) collective-permute-start(f32[1408,128]{1,0:T(8,128)S(1)} %get-tuple-element.24), channel_id=1, source_target_pairs={{0,4},{4,0},{1,5},{5,1},{2,6},{6,2},{3,7},{7,3},{8,12},{12,8},{9,1... | collective-permute-start | bytes 2162696 | tf_op jit(solution)/shard_map/ppermute | solution.py:645
  51.6 1.8 %collective-permute-done.3 = f32[1408,128]{1,0:T(8,128)S(1)} collective-permute-done((f32[1408,128]{1,0:T(8,128)S(1)}, f32[1408,128]{1,0:T(8,128)S(1)}, u32[]{:S(2)}, u32[]{:S(2)}) %collective-permute-start.3) | collective-permute-done | bytes 720928 | tf_op jit(solution)/shard_map/ppermute | solution.py:645
  53.4 0.1 add.3
  53.5 13.4 %all_to_all.30 = f32[4,352,128]{2,1,0:T(8,128)S(1)} all-to-all(f32[4,352,128]{2,1,0:T(8,128)S(1)} %bitcast.11), channel_id=1, replica_groups=mesh['zl'=2,'y'=8,'x'=4,'c'=2,'zh'=4] {'x'}, dimensions={0} | all-to-all | bytes 1441792 | tf_op jit(solution)/shard_map/all_to_all | solution.py:646
  66.9 0.6 spread.1
  67.5 18.3 %all_to_all.31.in_ref = f32[8,80,128]{2,1,0:T(8,128)S(1)} all-to-all(f32[8,80,128]{2,1,0:T(8,128)S(1)} %spread.1), channel_id=1, replica_groups=mesh['zl'=2,'y'=8,'x'=4,'c'=2,'zh'=4] {'zl','zh'}, dimensions={0} | all-to-all | bytes 655360 | tf_op jit(solution)/shard_map/all_to_all | solution.py:654
  85.8 14.6 %all_to_all.32.in_ref = f32[8,16,128]{2,1,0:T(8,128)S(1)} all-to-all(f32[8,16,128]{2,1,0:T(8,128)S(1)} %divide.1), channel_id=1, replica_groups=mesh['zl'=2,'y'=8,'x'=4,'c'=2,'zh'=4] {'y'}, dimensions={0} | all-to-all | bytes 131072 | tf_op jit(solution)/shard_map/all_to_all | solution.py:661
  100.4 0.1 scale.1
  100.5 9.6 %all_to_all.33.in_ref = f32[8,16,128]{2,1,0:T(8,128)S(1)} all-to-all(f32[8,16,128]{2,1,0:T(8,128)S(1)} %scale.1), channel_id=1, replica_groups=mesh['zl'=2,'y'=8,'x'=4,'c'=2,'zh'=4] {'y'}, dimensions={0} | all-to-all | bytes 131072 | tf_op jit(solution)/shard_map/all_to_all | solution.py:666
  110.1 12.6 %all_to_all.34.in_ref = f32[8,72,128]{2,1,0:T(8,128)S(1)} all-to-all(f32[8,72,128]{2,1,0:T(8,128)S(1)} %pack.1), channel_id=1, replica_groups=mesh['zl'=2,'y'=8,'x'=4,'c'=2,'zh'=4] {'zl','zh'}, dimensions={0} | all-to-all | bytes 589824 | tf_op jit(solution)/shard_map/all_to_all | solution.py:668
  122.7 0.1 repack.1
  122.8 12.9 %all_to_all.35.own_ref = f32[4,12,48,128]{3,2,1,0:T(8,128)S(1)} all-to-all(f32[4,12,48,128]{3,2,1,0:T(8,128)S(1)} %repack.1), channel_id=1, replica_groups=mesh['zl'=2,'y'=8,'x'=4,'c'=2,'zh'=4] {'x'}, dimensions={0} | all-to-all | bytes 2359296 | tf_op jit(solution)/shard_map/all_to_all | solution.py:675
  135.7 9.3 %collective-permute-start.4 = (f32[4,12,48,128]{3,2,1,0:T(8,128)S(1)}, f32[4,12,48,128]{3,2,1,0:T(8,128)S(1)}, u32[]{:S(2)}, u32[]{:S(2)}) collective-permute-start(f32[4,12,48,128]{3,2,1,0:T(8,128)S(1)} %all_to_all.35.own_ref), channel_id=1, source_target_pairs={{0,4},{4,0},{1,5},{5,1},{2,6},{6,2},{3,7},{7,3},{8,12},{12,8},{9,1... | collective-permute-start | bytes 3538952 | tf_op jit(solution)/shard_map/ppermute | solution.py:676
  144.9 2.5 %collective-permute-done.4.other_ref = f32[4,12,48,128]{3,2,1,0:T(8,128)S(1)} collective-permute-done((f32[4,12,48,128]{3,2,1,0:T(8,128)S(1)}, f32[4,12,48,128]{3,2,1,0:T(8,128)S(1)}, u32[]{:S(2)}, u32[]{:S(2)}) %collective-permute-start.4) | collective-permute-done | bytes 1179680 | tf_op jit(solution)/shard_map/ppermute | solution.py:676
  147.4 1.6 %place.1 = f32[3,48,4096]{2,1,0:T(8,128)} custom-call(f32[4,12,48,128]{3,2,1,0:T(8,128)S(1)} %all_to_all.35.own_ref, f32[4,12,48,128]{3,2,1,0:T(8,128)S(1)} %collective-permute-done.4.other_ref), custom_call_target="tpu_custom_call" | custom-call | flops 1000000 | bytes 1048576 | tf_op jit(solution)/shard_map/place/pallas_call | solution.py:546
  (5 shorter events, 0.1 us)
Async XLA Ops:
  0.8 6.0 %collective-permute-start = (f32[6,32,128]{2,1,0:T(8,128)S(1)}, f32[6,32,128]{2,1,0:T(8,128)S(1)}, u32[]{:S(2)}, u32[]{:S(2)}) collective-permute-start(f32[6,32,128]{2,1,0:T(8,128)S(1)} %pad_maximum_fusion), channel_id=1, source_target_pairs={{32,0},{64,32},{96,64},{128,96},{160,128},{192,160},{224,192},{256... | collective-permute-start | bytes 294920 | tf_op jit(solution)/shard_map/ppermute | solution.py:538
  2.1 1.3 copy-start
  3.4 1.3 copy-start.2
  4.7 11.5 %copy-start.4 = (s32[384]{0:T(512)S(1)}, s32[384]{0:T(512)}, u32[]{:S(2)}) copy-start(s32[384]{0:T(512)} %sx_smem.5) | copy-start | bytes 4612
  4.7 11.5 %copy-start.6 = (s32[512]{0:T(512)S(1)}, s32[512]{0:T(512)}, u32[]{:S(2)}) copy-start(s32[512]{0:T(512)} %param.11) | copy-start | bytes 6148
  4.7 11.5 %copy-start.7 = (s32[256]{0:T(256)S(1)}, s32[256]{0:T(256)}, u32[]{:S(2)}) copy-start(s32[256]{0:T(256)} %param.10) | copy-start | bytes 3076
  4.7 13.8 %copy-start.5 = (bf16[3,48,4096]{2,1,0:T(8,128)(2,1)S(1)}, bf16[3,48,4096]{2,1,0:T(8,128)(2,1)}, u32[]{:S(2)}) copy-start(bf16[3,48,4096]{2,1,0:T(8,128)(2,1)} %o_ref.1) | copy-start | bytes 3538948
  6.9 10.2 %collective-permute-start.1 = (f32[25,8,128]{2,1,0:T(8,128)S(1)}, f32[25,8,128]{2,1,0:T(8,128)S(1)}, u32[]{:S(2)}, u32[]{:S(2)}) collective-permute-start(f32[25,8,128]{2,1,0:T(8,128)S(1)} %widen.1), channel_id=1, source_target_pairs={{4,0},{8,4},{12,8},{16,12},{20,16},{24,20},{28,24},{5,1},{9,5},{13... | collective-permute-start | bytes 307208 | tf_op jit(solution)/shard_map/ppermute | solution.py:538
  17.2 9.8 %collective-permute-start.2 = (f32[6,40,128]{2,1,0:T(8,128)S(1)}, f32[6,40,128]{2,1,0:T(8,128)S(1)}, u32[]{:S(2)}, u32[]{:S(2)}) collective-permute-start(f32[6,40,128]{2,1,0:T(8,128)S(1)} %deepen.1), channel_id=1, source_target_pairs={{1,0},{2,1},{3,2},{5,4},{6,5},{7,6},{9,8},{10,9},{11,10},{13,12},{... | collective-permute-start | bytes 368648 | tf_op jit(solution)/shard_map/ppermute | solution.py:538
  18.5 8.5 %copy-start.1 = (f32[24,3,32,128]{3,2,1,0:T(8,128)S(1)}, f32[24,3,32,128]{3,2,1,0:T(8,128)}, u32[]{:S(2)}) copy-start(f32[24,3,32,128]{3,2,1,0:T(8,128)} %u_ref.3) | copy-start | bytes 3538948
  18.5 8.5 %copy-start.3 = (f32[24,3,32,128]{3,2,1,0:T(8,128)S(1)}, f32[24,3,32,128]{3,2,1,0:T(8,128)}, u32[]{:S(2)}) copy-start(f32[24,3,32,128]{3,2,1,0:T(8,128)} %w_ref.3) | copy-start | bytes 3538948
  49.2 4.2 %collective-permute-start.3 = (f32[1408,128]{1,0:T(8,128)S(1)}, f32[1408,128]{1,0:T(8,128)S(1)}, u32[]{:S(2)}, u32[]{:S(2)}) collective-permute-start(f32[1408,128]{1,0:T(8,128)S(1)} %get-tuple-element.24), channel_id=1, source_target_pairs={{0,4},{4,0},{1,5},{5,1},{2,6},{6,2},{3,7},{7,3},{8,12},{12,8},{9,1... | collective-permute-start | bytes 2162696 | tf_op jit(solution)/shard_map/ppermute | solution.py:645
  135.7 11.7 %collective-permute-start.4 = (f32[4,12,48,128]{3,2,1,0:T(8,128)S(1)}, f32[4,12,48,128]{3,2,1,0:T(8,128)S(1)}, u32[]{:S(2)}, u32[]{:S(2)}) collective-permute-start(f32[4,12,48,128]{3,2,1,0:T(8,128)S(1)} %all_to_all.35.own_ref), channel_id=1, source_target_pairs={{0,4},{4,0},{1,5},{5,1},{2,6},{6,2},{3,7},{7,3},{8,12},{12,8},{9,1... | collective-permute-start | bytes 3538952 | tf_op jit(solution)/shard_map/ppermute | solution.py:676

commit v3 on v2

--- a/solution.py
+++ b/solution.py
@@ -72,23 +72,6 @@
 
 def dot(a, b):
     return lax.dot_general(a, b, (((1,), (0,)), ((), ())), preferred_element_type=F32)
-
-
-def face_kernel(u_ref, w_ref, y_ref, z_ref):
-    layers = u_ref.shape[0]
-    rows, lanes = u_ref.shape[2], u_ref.shape[3]
-    lane = lax.broadcasted_iota(jnp.int32, (rows, lanes), 1)
-    for f in range(6):
-        source = (u_ref, w_ref)[f // 3]
-        c = f % 3
-        packed = jnp.zeros((rows, lanes), F32)
-        for i in range(layers):
-            y_ref[i, pl.ds(f, 1)] = source[i, c, pl.ds(0, 1)]
-            value = source[i, c]
-            packed = jnp.where(lane == i, value if i == 0 else pltpu.roll(value, i, 1), packed)
-        z_ref[f] = packed
-    for i in range(layers):
-        y_ref[i, pl.ds(6, 2)] = jnp.zeros((2, lanes), F32)
 
 
 def widen_kernel(y_ref, xf_ref, out_ref):
@@ -113,9 +96,35 @@
         out_ref[f, pl.ds(rows, 8)] = jnp.broadcast_to(edge[f : f + 1], (8, lanes))
 
 
+def pack_faces(bricks, y_ref, z_ref):
+    _, layers, _, rows, lanes = bricks.shape
+    lane = lax.broadcasted_iota(jnp.int32, (rows, lanes), 1)
+    for f in range(6):
+        packed = jnp.zeros((rows, lanes), F32)
+        for i in range(layers):
+            value = bricks[f // 3, i, f % 3]
+            y_ref[i, pl.ds(f, 1)] = value[:1]
+            packed = jnp.where(lane == i, value if i == 0 else pltpu.roll(value, i, 1), packed)
+        z_ref[f] = packed
+    for i in range(layers):
+        y_ref[i, pl.ds(6, 2)] = jnp.zeros((2, lanes), F32)
+
+
 def table_kernel(
-    nx, sx_ref, sy_ref, sz_ref, coef_ref, lin_ref, yb_ref, zb_ref, zf_ref, yf_ref
+    u_ref, w_ref, sx_ref, sy_ref, sz_ref,
+    y_ref, z_ref, coef_ref, lin_ref, yb_ref, zb_ref, zf_ref, yf_ref, bricks, sems,
 ):
+    nx = u_ref.shape[0]
+    halves = ((0, nx // 2), (nx // 2, nx - nx // 2))
+    copies = [
+        pltpu.make_async_copy(
+            ref.at[pl.ds(at, size)], bricks.at[b, pl.ds(at, size)], sems.at[2 * b + h]
+        )
+        for b, ref in enumerate((u_ref, w_ref))
+        for h, (at, size) in enumerate(halves)
+    ]
+    for copy in copies:
+        copy.start()
     ny, nz = lin_ref.shape[1:]
     nodes_x, nodes_y, nodes_z = sx_ref.shape[1], sy_ref.shape[1], sz_ref.shape[1]
     step_x = 2.0 * nodes_x / (NCX - 3)
@@ -201,6 +210,9 @@
     rise = jnp.transpose(jnp.broadcast_to(step_z * rise, (nz, lanes)))[:ny]
     lin_ref[2] = jnp.where(live, place, 0.0)
     lin_ref[3] = jnp.where(live, rise, 0.0)
+    for copy in copies:
+        copy.wait()
+    pack_faces(bricks, y_ref, z_ref)
 
 
 def net_kernel(sx_smem, o_ref, zf_ref, yf_ref, q_ref, plain_ref, slope_ref):
@@ -209,7 +221,7 @@
     lanes = 2 * NCZ
     half = NCY // 2
     start_x = lax.axis_index(LENGTH) * (window - 4)
-    group = 8
+    group = 16
 
     def along_z(step, carry):
         r = step // (half // group)
@@ -247,7 +259,7 @@
                 q_ref[step * FOLD + g, 3 * r + 2] = part[:ny, nz:]
         return carry
 
-    lax.fori_loop(0, window // FOLD, along_y, 0, unroll=4)
+    lax.fori_loop(0, window // FOLD, along_y, 0, unroll=7)
     q_ref[window] = jnp.zeros(q_ref.shape[1:], F32)
 
 
@@ -366,8 +378,8 @@
         first = sx_smem[start_x + i] - start
         coef = [coef_ref[k, pl.ds(i, 1)] for k in range(13)]
         total, delta = coef[:5], coef[5:10]
-        for block in range(ny // 8):
-            at = pl.ds(8 * block, 8)
+        for block in range(ny // 16):
+            at = pl.ds(16 * block, 16)
             jac = [[None] * 3 for _ in range(3)]
             for r in range(3):
                 for s in range(3):
@@ -391,7 +403,7 @@
                     ]
                 )
             det, gradient = element_gradient(jac, grads[:3], grads[3:], lin_ref[4, at])
-            volume = volume + det
+            volume = volume + det[:8] + det[8:]
             for r in range(3):
                 for s in range(3):
                     weight = delta if s == 0 else total
@@ -429,7 +441,7 @@
             left_lo[at, pl.ds(2 * nz, 2 * nz)] = low[half:]
         return carry
 
-    lax.fori_loop(0, window, along_width, 0)
+    lax.fori_loop(0, window, along_width, 0, unroll=7)
 
     kept = half // 2
     rows_out = keep_ref.shape[0] // kept
@@ -444,7 +456,7 @@
             stage[pl.ds(step * batch + b, half, stride=pitch)] = full[b * half : (b + 1) * half]
         return carry
 
-    lax.fori_loop(0, 3 * window // batch, along_depth, 0)
+    lax.fori_loop(0, 3 * window // batch, along_depth, 0, unroll=7)
 
     total = jnp.sum(volume, axis=0, keepdims=True)
     spare = lax.broadcasted_iota(jnp.int32, (rows_out - 3 * window, nz), 0)
@@ -477,35 +489,23 @@
             out_ref[at, pl.ds(each, 8)] = last
 
 
-def divide_kernel(in_ref, out_ref, total):
-    value = in_ref[0]
-    for p in range(1, in_ref.shape[0]):
-        value = value + in_ref[p]
-    total[...] = value
-    owners = out_ref.shape[0]
-    rows = in_ref.shape[1] - 8
-    each = rows // owners
-    for owner in range(owners):
-        out_ref[owner, pl.ds(0, each)] = total[pl.ds(owner * each, each)]
-        out_ref[owner, pl.ds(each, 16 - each)] = total[pl.ds(rows, 16 - each)]
-
-
-def scale_kernel(elements, part, in_ref, out_ref):
+def collect_kernel(in_ref, out_ref):
     total = in_ref[0]
     for p in range(1, in_ref.shape[0]):
         total = total + in_ref[p]
-    volume = jnp.sum(total[part : part + 1], axis=1, keepdims=True)
-    total = total * (elements * MU_SHEAR / volume)
-    for p in range(in_ref.shape[0]):
+    for p in range(out_ref.shape[0]):
         out_ref[p] = total
 
 
-def pack_kernel(in_ref, out_ref):
-    owners = in_ref.shape[0]
-    each = out_ref.shape[1] // owners
-    for copy in range(out_ref.shape[0]):
-        for owner in range(owners):
-            out_ref[copy, pl.ds(owner * each, each)] = in_ref[owner, pl.ds(0, each)]
+def scale_kernel(elements, in_ref, out_ref):
+    rows = out_ref.shape[1]
+    total = in_ref[0]
+    for p in range(1, in_ref.shape[0]):
+        total = total + in_ref[p]
+    volume = jnp.sum(total[rows : rows + 1], axis=1, keepdims=True)
+    total = total[:rows] * (elements * MU_SHEAR / volume)
+    for p in range(out_ref.shape[0]):
+        out_ref[p] = total
 
 
 def repack_kernel(in_ref, out_ref, plane):
@@ -559,26 +559,31 @@
     return jax.ShapeDtypeStruct(shape, dtype)
 
 
-def brick_faces(displacement, adjoint):
+def brick_tables(displacement, adjoint, span_x, span_y, span_z):
     nx, _, ny, nz = displacement.shape
-    return call(face_kernel, (array(nx, 8, nz), array(6, ny, nz)), displacement, adjoint)
-
-
-def brick_tables(shape, span_x, span_y, span_z):
-    nx, _, ny, nz = shape
-    return call(
-        functools.partial(table_kernel, nx),
-        (
-            array(13, -(-nx // 8) * 8, nz),
-            array(6, ny, nz),
-            array(NCY, 6 * ny, dtype=BF16),
-            array(4 * nz, 4 * NCZ, dtype=BF16),
-            array(4 * NCZ, 4 * nz, dtype=BF16),
-            array(3, FOLD * 2 * ny, FOLD * 3 * NCY, dtype=BF16),
-        ),
-        *[s.reshape(1, s.shape[0]) for s in (span_x, span_y, span_z)],
-        flops=10**7,
-    )
+    out_shape = (
+        array(nx, 8, nz),
+        array(6, ny, nz),
+        array(13, -(-nx // 8) * 8, nz),
+        array(6, ny, nz),
+        array(NCY, 6 * ny, dtype=BF16),
+        array(4 * nz, 4 * NCZ, dtype=BF16),
+        array(4 * NCZ, 4 * nz, dtype=BF16),
+        array(3, FOLD * 2 * ny, FOLD * 3 * NCY, dtype=BF16),
+    )
+    return pl.pallas_call(
+        table_kernel,
+        out_shape=out_shape,
+        in_specs=[pl.BlockSpec(memory_space=pl.ANY)] * 2 + [VMEM] * 3,
+        out_specs=(VMEM,) * len(out_shape),
+        scratch_shapes=[
+            pltpu.VMEM((2,) + displacement.shape, F32),
+            pltpu.SemaphoreType.DMA((4,)),
+        ],
+        name="table",
+        compiler_params=pltpu.CompilerParams(vmem_limit_bytes=16 * MIB),
+        cost_estimate=pl.CostEstimate(flops=10**7, bytes_accessed=4 * MIB, transcendentals=0),
+    )(displacement, adjoint, *[s.reshape(1, s.shape[0]) for s in (span_x, span_y, span_z)])
 
 
 def brick_net(shape, offsets, span_x, z_front, y_front):
@@ -629,8 +634,7 @@
     swap = [(0, 1), (1, 0)]
 
     xf = shifted(jnp.concatenate([displacement[0], adjoint[0]], axis=0), LENGTH, sizes)
-    y_face, z_face = brick_faces(displacement, adjoint)
-    tables = brick_tables(shape, span_x, span_y, span_z)
+    y_face, z_face, *tables = brick_tables(displacement, adjoint, span_x, span_y, span_z)
     yf = shifted(call(widen_kernel, array(nx + 1, 8, nz), y_face, xf), WIDTH, sizes)
     net = brick_net(shape, offsets, span_x, *tables[4:])
     zf = shifted(call(deepen_kernel, array(6, ny + 8, nz), z_face, xf, yf), DEPTH, sizes)
@@ -644,27 +648,21 @@
     blocks, part = size_zl * size_d, 3 * NCX // size_l
     terms = keep + lax.ppermute(send, "c", swap)
     terms = lax.all_to_all(terms.reshape(size_x, size_d * stride, lanes), "x", 0, 0, tiled=True)
+    rows = part * size_y
     terms = call(
         spread_kernel,
-        array(blocks, part * size_y + 8, lanes),
+        array(blocks, rows + 8, lanes),
         span_x,
         terms.reshape(size_x, size_d, stride, lanes),
         scratch=[((3 * NCX, lanes), F32)],
     )
     terms = lax.all_to_all(terms, ("zl", "zh"), 0, 0, tiled=True)
-    terms = call(
-        divide_kernel,
-        array(size_y, 16, lanes),
-        terms,
-        scratch=[((part * size_y + 8, lanes), F32)],
-    )
+    terms = call(collect_kernel, array(size_y, rows + 8, lanes), terms)
     terms = lax.all_to_all(terms, "y", 0, 0, tiled=True)
     elements = (nodes_x - 1) * (nodes_y - 1) * (nodes_z - 1)
     rows = call(
-        functools.partial(scale_kernel, elements, part), array(size_y, 16, lanes), terms
-    )
-    rows = lax.all_to_all(rows, "y", 0, 0, tiled=True)
-    rows = call(pack_kernel, array(blocks, part * size_y, lanes), rows)
+        functools.partial(scale_kernel, elements), array(blocks, rows, lanes), terms
+    )
     rows = lax.all_to_all(rows, ("zl", "zh"), 0, 0, tiled=True)
     rows = call(
         repack_kernel,

time: 150 us -> 140 us (0.933)
  Pallas kernels: 32.2 us -> 26.4 us
  blocking collectives: 81.3 us -> 79 us
  waiting for transfers between devices: 8.36 us -> 6.28 us
  local copies, waits for them, and re-layouts: 3.4 us -> 5.43 us
    all_to_all x1 -> x0, blocking collectives: 9.59 us -> none  [on_device(): rows = lax.all_to_all(rows, 'y', 0, 0, tiled=True)]
    pallas_call x1, Pallas kernels: 22.2 us -> 17.2 us  [brick_terms(): pl.pallas_call(element_kernel, out_shape=(jax.ShapeDtypeStruct((half // 2...]
    all_to_all x1, blocking collectives: 18.3 us -> 22.1 us  [on_device(): terms = lax.all_to_all(terms, ('zl', 'zh'), 0, 0, tiled=True)]
    pallas_call x11 -> x8, Pallas kernels: 10 us -> 7.44 us  [call(): pl.pallas_call(kernel, out_shape=out_shape, in_specs=[SMEM if o.ndim == 1...]
    ppermute x3, waiting for transfers between devices: 4.11 us -> 2.03 us  [shifted(): lax.ppermute(value, axes, [(i, i - 1) for i in range(1, sizes[axes])])]
    all_to_all x1, blocking collectives: 14.6 us -> 16.4 us  [on_device(): terms = lax.all_to_all(terms, 'y', 0, 0, tiled=True)]
    pallas_call x0 -> x1, Pallas kernels: none -> 1.82 us  [brick_tables(): pl.pallas_call(table_kernel, out_shape=out_shape, in_specs=[pl.BlockSpec(...]
  transfers between devices with their start and end apart: 5 -> 5, of which waited for: 5 -> 4; matrix products, arithmetic and copies ran while one was open for 0% -> 0% of each run, Pallas kernels for 5% -> 5%
where the time goes in v3:
time: 140 us
  blocking collectives  79 us (56%)
  Pallas kernels  26.4 us (19%)
  starting transfers between devices  22.6 us (16%)
  waiting for transfers between devices  6.28 us (4%)
  local copies, waits for them, and re-layouts  5.43 us (4%)
    all_to_all x1, blocking collectives, on_device(): terms = lax.all_to_all(terms, ('zl', 'zh'), 0, 0, tiled=True)  22.1 us
    pallas_call x1, Pallas kernels, brick_terms(): pl.pallas_call(element_kernel, out_shape=(jax.ShapeDtypeStruct((half // 2...  17.2 us
    all_to_all x1, blocking collectives, on_device(): terms = lax.all_to_all(terms, 'y', 0, 0, tiled=True)  16.4 us
    all_to_all x1, blocking collectives, on_device(): rows = lax.all_to_all(rows, 'x', 0, 0, tiled=True)  13.8 us
    all_to_all x1, blocking collectives, on_device(): lax.all_to_all(terms.reshape(size_x, size_d * stride, lanes), 'x', 0, 0,...  13.4 us
    all_to_all x1, blocking collectives, on_device(): rows = lax.all_to_all(rows, ('zl', 'zh'), 0, 0, tiled=True)  13.2 us
    ppermute x3, starting transfers between devices, shifted(): lax.ppermute(value, axes, [(i, i - 1) for i in range(1, sizes[axes])])  11.4 us
    ppermute x1, starting transfers between devices, on_device(): other = lax.ppermute(rows, 'c', swap)  7.99 us
  transfers between devices with their start and end apart: 5, of which 4 were waited for; matrix products, arithmetic and copies ran while one was open for 0% of the time, Pallas kernels for 5%

profile of v3, /device:TPU:1, one launch (start us, length us, event | category | flops | bytes accessed | tf_op | source)
XLA Modules:
  0.0 139.9 jit_solution(15638157647622165560)
XLA Ops:
  0.0 0.8 slice_bitcast_fusion
  0.8 1.3 collective-permute-start
  2.1 0.7 reshape.15.sx_ref
  2.8 0.0 copy-start
  2.8 1.3 copy-done
  4.1 0.0 copy-start.2
  4.1 1.3 copy-done.2
  5.4 0.0 copy-start.5
  5.4 0.7 copy-done.5
  6.1 0.0 copy-start.6
  6.1 0.7 copy-done.6
  6.7 0.0 copy-start.4
  6.7 0.0 copy-start.7
  6.7 1.8 %table.1 = (f32[24,8,128]{2,1,0:T(8,128)S(1)}, f32[6,32,128]{2,1,0:T(8,128)S(1)}, f32[13,24,128]{2,1,0:T(8,128)S(1)}, f32[6,32,128]{2,1,0:T(8,128)S(1)}, bf16[64...) custom-call(f32[24,3,32,128]{3,2,1,0:T(8,128)S(1)} %copy-done, ...), custom_call_target="tpu_custom_call" | custom-call | flops 10000000 | bytes 4194304 | tf_op jit(solution)/shard_map/table/pallas_call | solution.py:574
  8.6 0.0 collective-permute-done.xf_ref
  8.6 8.8 %collective-permute-start.1 = (f32[25,8,128]{2,1,0:T(8,128)S(1)}, f32[25,8,128]{2,1,0:T(8,128)S(1)}, u32[]{:S(2)}, u32[]{:S(2)}) collective-permute-start(f32[25,8,128]{2,1,0:T(8,128)S(1)} %widen.1), channel_id=1, source_target_pairs={{4,0},{8,4},{12,8},{16,12},{20,16},{24,20},{28,24},{5,1},{9,5},{13... | collective-permute-start | bytes 307208 | tf_op jit(solution)/shard_map/ppermute | solution.py:538
  17.4 0.9 collective-permute-done.1.yf_ref
  18.3 0.1 deepen.1
  18.4 1.3 collective-permute-start.2
  19.7 0.0 copy-done.4
  19.7 0.0 copy-done.7
  19.8 0.0 copy-start.1
  19.8 0.0 copy-start.3
  19.8 4.9 %net.1.q_ref = f32[29,9,32,128]{3,2,1,0:T(8,128)S(1)} custom-call(s32[384]{0:T(512)S(1)} %copy-done.4, bf16[3,48,4096]{2,1,0:T(8,128)(2,1)S(1)} %copy-done.7, bf16[256,512]{1,0:T(8,128)(2,1)S(1)} %get-tuple-element.19.zf_ref, bf16[3,64,192]{2,1,0:T(8,128)(2,1)S(1)} %get-tuple-element.20.yf_ref), custom_call_target="tpu_custom_call" | custom-call | flops 2000000000 | bytes 1048576 | tf_op jit(solution)/shard_map/net/pallas_call | solution.py:546
  24.7 1.1 collective-permute-done.2.zf_ref
  25.8 0.0 copy-done.1
  25.8 0.0 copy-done.3
  25.8 17.2 %elements.1 = (f32[1408,128]{1,0:T(8,128)S(1)}, f32[1408,128]{1,0:T(8,128)S(1)}) custom-call(s32[384]{0:T(512)S(1)} %copy-done.4, f32[13,24,128]{2,1,0:T(8,128)S(1)} %get-tuple-element.15.coef_ref, f32[24,3,32,128]{3,2,1,0:T(8,128)S(1)} %copy-done.1, f32[24,3,32,128]{3,2,1,0:T(8,128)S(1)} %copy-done.3, f32[6,32,128]{2,1,0:T(8,128)S(1)} %collective-permute-done.xf_ref, ...), custom_call_target="tpu_custom_call" | custom-call | flops 10000000000 | bytes 10485760 | tf_op jit(solution)/shard_map/elements/pallas_call | solution.py:610
  42.9 3.2 %collective-permute-start.3 = (f32[1408,128]{1,0:T(8,128)S(1)}, f32[1408,128]{1,0:T(8,128)S(1)}, u32[]{:S(2)}, u32[]{:S(2)}) collective-permute-start(f32[1408,128]{1,0:T(8,128)S(1)} %get-tuple-element.24), channel_id=1, source_target_pairs={{0,4},{4,0},{1,5},{5,1},{2,6},{6,2},{3,7},{7,3},{8,12},{12,8},{9,1... | collective-permute-start | bytes 2162696 | tf_op jit(solution)/shard_map/ppermute | solution.py:649
  46.1 1.8 %collective-permute-done.3 = f32[1408,128]{1,0:T(8,128)S(1)} collective-permute-done((f32[1408,128]{1,0:T(8,128)S(1)}, f32[1408,128]{1,0:T(8,128)S(1)}, u32[]{:S(2)}, u32[]{:S(2)}) %collective-permute-start.3) | collective-permute-done | bytes 720928 | tf_op jit(solution)/shard_map/ppermute | solution.py:649
  47.9 0.1 add.3
  48.0 13.4 %all_to_all.25 = f32[4,352,128]{2,1,0:T(8,128)S(1)} all-to-all(f32[4,352,128]{2,1,0:T(8,128)S(1)} %bitcast.11), channel_id=1, replica_groups=mesh['zl'=2,'y'=8,'x'=4,'c'=2,'zh'=4] {'x'}, dimensions={0} | all-to-all | bytes 1441792 | tf_op jit(solution)/shard_map/all_to_all | solution.py:650
  61.5 0.6 spread.1
  62.1 22.1 %all_to_all.26.in_ref = f32[8,80,128]{2,1,0:T(8,128)S(1)} all-to-all(f32[8,80,128]{2,1,0:T(8,128)S(1)} %spread.1), channel_id=1, replica_groups=mesh['zl'=2,'y'=8,'x'=4,'c'=2,'zh'=4] {'zl','zh'}, dimensions={0} | all-to-all | bytes 655360 | tf_op jit(solution)/shard_map/all_to_all | solution.py:659
  84.3 16.4 %all_to_all.27.in_ref = f32[8,80,128]{2,1,0:T(8,128)S(1)} all-to-all(f32[8,80,128]{2,1,0:T(8,128)S(1)} %collect.1), channel_id=1, replica_groups=mesh['zl'=2,'y'=8,'x'=4,'c'=2,'zh'=4] {'y'}, dimensions={0} | all-to-all | bytes 655360 | tf_op jit(solution)/shard_map/all_to_all | solution.py:661
  100.7 0.1 scale.1
  100.8 13.2 %all_to_all.28.in_ref = f32[8,72,128]{2,1,0:T(8,128)S(1)} all-to-all(f32[8,72,128]{2,1,0:T(8,128)S(1)} %scale.1), channel_id=1, replica_groups=mesh['zl'=2,'y'=8,'x'=4,'c'=2,'zh'=4] {'zl','zh'}, dimensions={0} | all-to-all | bytes 589824 | tf_op jit(solution)/shard_map/all_to_all | solution.py:666
  114.0 0.1 repack.1
  114.1 13.8 %all_to_all.29.own_ref = f32[4,12,48,128]{3,2,1,0:T(8,128)S(1)} all-to-all(f32[4,12,48,128]{3,2,1,0:T(8,128)S(1)} %repack.1), channel_id=1, replica_groups=mesh['zl'=2,'y'=8,'x'=4,'c'=2,'zh'=4] {'x'}, dimensions={0} | all-to-all | bytes 2359296 | tf_op jit(solution)/shard_map/all_to_all | solution.py:673
  127.9 8.0 %collective-permute-start.4 = (f32[4,12,48,128]{3,2,1,0:T(8,128)S(1)}, f32[4,12,48,128]{3,2,1,0:T(8,128)S(1)}, u32[]{:S(2)}, u32[]{:S(2)}) collective-permute-start(f32[4,12,48,128]{3,2,1,0:T(8,128)S(1)} %all_to_all.29.own_ref), channel_id=1, source_target_pairs={{0,4},{4,0},{1,5},{5,1},{2,6},{6,2},{3,7},{7,3},{8,12},{12,8},{9,1... | collective-permute-start | bytes 3538952 | tf_op jit(solution)/shard_map/ppermute | solution.py:674
  135.9 2.5 %collective-permute-done.4.other_ref = f32[4,12,48,128]{3,2,1,0:T(8,128)S(1)} collective-permute-done((f32[4,12,48,128]{3,2,1,0:T(8,128)S(1)}, f32[4,12,48,128]{3,2,1,0:T(8,128)S(1)}, u32[]{:S(2)}, u32[]{:S(2)}) %collective-permute-start.4) | collective-permute-done | bytes 1179680 | tf_op jit(solution)/shard_map/ppermute | solution.py:674
  138.3 1.6 %place.1 = f32[3,48,4096]{2,1,0:T(8,128)} custom-call(f32[4,12,48,128]{3,2,1,0:T(8,128)S(1)} %all_to_all.29.own_ref, f32[4,12,48,128]{3,2,1,0:T(8,128)S(1)} %collective-permute-done.4.other_ref), custom_call_target="tpu_custom_call" | custom-call | flops 1000000 | bytes 1048576 | tf_op jit(solution)/shard_map/place/pallas_call | solution.py:546
  (3 shorter events, 0.0 us)
Async XLA Ops:
  0.8 7.7 %collective-permute-start = (f32[6,32,128]{2,1,0:T(8,128)S(1)}, f32[6,32,128]{2,1,0:T(8,128)S(1)}, u32[]{:S(2)}, u32[]{:S(2)}) collective-permute-start(f32[6,32,128]{2,1,0:T(8,128)S(1)} %pad_maximum_fusion), channel_id=1, source_target_pairs={{32,0},{64,32},{96,64},{128,96},{160,128},{192,160},{224,192},{256... | collective-permute-start | bytes 294920 | tf_op jit(solution)/shard_map/ppermute | solution.py:538
  2.8 1.3 copy-start
  4.1 1.3 copy-start.2
  5.4 0.7 copy-start.5
  6.1 0.7 copy-start.6
  6.7 13.0 %copy-start.4 = (s32[384]{0:T(512)S(1)}, s32[384]{0:T(512)}, u32[]{:S(2)}) copy-start(s32[384]{0:T(512)} %sx_smem.5) | copy-start | bytes 4612
  6.7 13.0 %copy-start.7 = (bf16[3,48,4096]{2,1,0:T(8,128)(2,1)S(1)}, bf16[3,48,4096]{2,1,0:T(8,128)(2,1)}, u32[]{:S(2)}) copy-start(bf16[3,48,4096]{2,1,0:T(8,128)(2,1)} %o_ref.1) | copy-start | bytes 3538948
  8.6 9.7 %collective-permute-start.1 = (f32[25,8,128]{2,1,0:T(8,128)S(1)}, f32[25,8,128]{2,1,0:T(8,128)S(1)}, u32[]{:S(2)}, u32[]{:S(2)}) collective-permute-start(f32[25,8,128]{2,1,0:T(8,128)S(1)} %widen.1), channel_id=1, source_target_pairs={{4,0},{8,4},{12,8},{16,12},{20,16},{24,20},{28,24},{5,1},{9,5},{13... | collective-permute-start | bytes 307208 | tf_op jit(solution)/shard_map/ppermute | solution.py:538
  18.4 7.3 %collective-permute-start.2 = (f32[6,40,128]{2,1,0:T(8,128)S(1)}, f32[6,40,128]{2,1,0:T(8,128)S(1)}, u32[]{:S(2)}, u32[]{:S(2)}) collective-permute-start(f32[6,40,128]{2,1,0:T(8,128)S(1)} %deepen.1), channel_id=1, source_target_pairs={{1,0},{2,1},{3,2},{5,4},{6,5},{7,6},{9,8},{10,9},{11,10},{13,12},{... | collective-permute-start | bytes 368648 | tf_op jit(solution)/shard_map/ppermute | solution.py:538
  19.8 6.0 %copy-start.1 = (f32[24,3,32,128]{3,2,1,0:T(8,128)S(1)}, f32[24,3,32,128]{3,2,1,0:T(8,128)}, u32[]{:S(2)}) copy-start(f32[24,3,32,128]{3,2,1,0:T(8,128)} %u_ref.3) | copy-start | bytes 3538948
  19.8 6.0 %copy-start.3 = (f32[24,3,32,128]{3,2,1,0:T(8,128)S(1)}, f32[24,3,32,128]{3,2,1,0:T(8,128)}, u32[]{:S(2)}) copy-start(f32[24,3,32,128]{3,2,1,0:T(8,128)} %w_ref.3) | copy-start | bytes 3538948
  42.9 5.0 %collective-permute-start.3 = (f32[1408,128]{1,0:T(8,128)S(1)}, f32[1408,128]{1,0:T(8,128)S(1)}, u32[]{:S(2)}, u32[]{:S(2)}) collective-permute-start(f32[1408,128]{1,0:T(8,128)S(1)} %get-tuple-element.24), channel_id=1, source_target_pairs={{0,4},{4,0},{1,5},{5,1},{2,6},{6,2},{3,7},{7,3},{8,12},{12,8},{9,1... | collective-permute-start | bytes 2162696 | tf_op jit(solution)/shard_map/ppermute | solution.py:649
  127.9 10.5 %collective-permute-start.4 = (f32[4,12,48,128]{3,2,1,0:T(8,128)S(1)}, f32[4,12,48,128]{3,2,1,0:T(8,128)S(1)}, u32[]{:S(2)}, u32[]{:S(2)}) collective-permute-start(f32[4,12,48,128]{3,2,1,0:T(8,128)S(1)} %all_to_all.29.own_ref), channel_id=1, source_target_pairs={{0,4},{4,0},{1,5},{5,1},{2,6},{6,2},{3,7},{7,3},{8,12},{12,8},{9,1... | collective-permute-start | bytes 3538952 | tf_op jit(solution)/shard_map/ppermute | solution.py:674

commit v4 on v2

--- a/solution.py
+++ b/solution.py
@@ -209,7 +209,7 @@
     lanes = 2 * NCZ
     half = NCY // 2
     start_x = lax.axis_index(LENGTH) * (window - 4)
-    group = 8
+    group = 16
 
     def along_z(step, carry):
         r = step // (half // group)
@@ -247,7 +247,7 @@
                 q_ref[step * FOLD + g, 3 * r + 2] = part[:ny, nz:]
         return carry
 
-    lax.fori_loop(0, window // FOLD, along_y, 0, unroll=4)
+    lax.fori_loop(0, window // FOLD, along_y, 0, unroll=7)
     q_ref[window] = jnp.zeros(q_ref.shape[1:], F32)
 
 
@@ -366,8 +366,8 @@
         first = sx_smem[start_x + i] - start
         coef = [coef_ref[k, pl.ds(i, 1)] for k in range(13)]
         total, delta = coef[:5], coef[5:10]
-        for block in range(ny // 8):
-            at = pl.ds(8 * block, 8)
+        for block in range(ny // 16):
+            at = pl.ds(16 * block, 16)
             jac = [[None] * 3 for _ in range(3)]
             for r in range(3):
                 for s in range(3):
@@ -391,7 +391,7 @@
                     ]
                 )
             det, gradient = element_gradient(jac, grads[:3], grads[3:], lin_ref[4, at])
-            volume = volume + det
+            volume = volume + det[:8] + det[8:]
             for r in range(3):
                 for s in range(3):
                     weight = delta if s == 0 else total
@@ -429,7 +429,7 @@
             left_lo[at, pl.ds(2 * nz, 2 * nz)] = low[half:]
         return carry
 
-    lax.fori_loop(0, window, along_width, 0)
+    lax.fori_loop(0, window, along_width, 0, unroll=7)
 
     kept = half // 2
     rows_out = keep_ref.shape[0] // kept
@@ -444,7 +444,7 @@
             stage[pl.ds(step * batch + b, half, stride=pitch)] = full[b * half : (b + 1) * half]
         return carry
 
-    lax.fori_loop(0, 3 * window // batch, along_depth, 0)
+    lax.fori_loop(0, 3 * window // batch, along_depth, 0, unroll=7)
 
     total = jnp.sum(volume, axis=0, keepdims=True)
     spare = lax.broadcasted_iota(jnp.int32, (rows_out - 3 * window, nz), 0)
@@ -477,35 +477,23 @@
             out_ref[at, pl.ds(each, 8)] = last
 
 
-def divide_kernel(in_ref, out_ref, total):
-    value = in_ref[0]
-    for p in range(1, in_ref.shape[0]):
-        value = value + in_ref[p]
-    total[...] = value
-    owners = out_ref.shape[0]
-    rows = in_ref.shape[1] - 8
-    each = rows // owners
-    for owner in range(owners):
-        out_ref[owner, pl.ds(0, each)] = total[pl.ds(owner * each, each)]
-        out_ref[owner, pl.ds(each, 16 - each)] = total[pl.ds(rows, 16 - each)]
-
-
-def scale_kernel(elements, part, in_ref, out_ref):
+def collect_kernel(in_ref, out_ref):
     total = in_ref[0]
     for p in range(1, in_ref.shape[0]):
         total = total + in_ref[p]
-    volume = jnp.sum(total[part : part + 1], axis=1, keepdims=True)
-    total = total * (elements * MU_SHEAR / volume)
-    for p in range(in_ref.shape[0]):
+    for p in range(out_ref.shape[0]):
         out_ref[p] = total
 
 
-def pack_kernel(in_ref, out_ref):
-    owners = in_ref.shape[0]
-    each = out_ref.shape[1] // owners
-    for copy in range(out_ref.shape[0]):
-        for owner in range(owners):
-            out_ref[copy, pl.ds(owner * each, each)] = in_ref[owner, pl.ds(0, each)]
+def scale_kernel(elements, in_ref, out_ref):
+    rows = out_ref.shape[1]
+    total = in_ref[0]
+    for p in range(1, in_ref.shape[0]):
+        total = total + in_ref[p]
+    volume = jnp.sum(total[rows : rows + 1], axis=1, keepdims=True)
+    total = total[:rows] * (elements * MU_SHEAR / volume)
+    for p in range(out_ref.shape[0]):
+        out_ref[p] = total
 
 
 def repack_kernel(in_ref, out_ref, plane):
@@ -644,27 +632,21 @@
     blocks, part = size_zl * size_d, 3 * NCX // size_l
     terms = keep + lax.ppermute(send, "c", swap)
     terms = lax.all_to_all(terms.reshape(size_x, size_d * stride, lanes), "x", 0, 0, tiled=True)
+    rows = part * size_y
     terms = call(
         spread_kernel,
-        array(blocks, part * size_y + 8, lanes),
+        array(blocks, rows + 8, lanes),
         span_x,
         terms.reshape(size_x, size_d, stride, lanes),
         scratch=[((3 * NCX, lanes), F32)],
     )
     terms = lax.all_to_all(terms, ("zl", "zh"), 0, 0, tiled=True)
-    terms = call(
-        divide_kernel,
-        array(size_y, 16, lanes),
-        terms,
-        scratch=[((part * size_y + 8, lanes), F32)],
-    )
+    terms = call(collect_kernel, array(size_y, rows + 8, lanes), terms)
     terms = lax.all_to_all(terms, "y", 0, 0, tiled=True)
     elements = (nodes_x - 1) * (nodes_y - 1) * (nodes_z - 1)
     rows = call(
-        functools.partial(scale_kernel, elements, part), array(size_y, 16, lanes), terms
-    )
-    rows = lax.all_to_all(rows, "y", 0, 0, tiled=True)
-    rows = call(pack_kernel, array(blocks, part * size_y, lanes), rows)
+        functools.partial(scale_kernel, elements), array(blocks, rows, lanes), terms
+    )
     rows = lax.all_to_all(rows, ("zl", "zh"), 0, 0, tiled=True)
     rows = call(
         repack_kernel,

time: 150 us -> 138 us (0.920)
  Pallas kernels: 32.2 us -> 25.9 us
  blocking collectives: 81.3 us -> 76 us
    all_to_all x1 -> x0, blocking collectives: 9.59 us -> none  [on_device(): rows = lax.all_to_all(rows, 'y', 0, 0, tiled=True)]
    pallas_call x1, Pallas kernels: 22.2 us -> 17.1 us  [brick_terms(): pl.pallas_call(element_kernel, out_shape=(jax.ShapeDtypeStruct((half // 2...]
    all_to_all x1, blocking collectives: 14.6 us -> 17.5 us  [on_device(): terms = lax.all_to_all(terms, 'y', 0, 0, tiled=True)]
    pallas_call x11 -> x10, Pallas kernels: 10 us -> 8.72 us  [call(): pl.pallas_call(kernel, out_shape=out_shape, in_specs=[SMEM if o.ndim == 1...]
  transfers between devices with their start and end apart: 5 -> 5, of which waited for: 5 -> 5; matrix products, arithmetic and copies ran while one was open for 0% -> 0% of each run, Pallas kernels for 5% -> 4%
where the time goes in v4:
time: 138 us; the launch traced here: 137 us
  blocking collectives  76 us (55%)
  Pallas kernels  25.9 us (19%)
  starting transfers between devices  22.3 us (16%)
  waiting for transfers between devices  9.62 us (7%)
  local copies, waits for them, and re-layouts  3.4 us (2%)
    all_to_all x1, blocking collectives, on_device(): terms = lax.all_to_all(terms, ('zl', 'zh'), 0, 0, tiled=True)  18.2 us
    all_to_all x1, blocking collectives, on_device(): terms = lax.all_to_all(terms, 'y', 0, 0, tiled=True)  17.5 us
    pallas_call x1, Pallas kernels, brick_terms(): pl.pallas_call(element_kernel, out_shape=(jax.ShapeDtypeStruct((half // 2...  17.1 us
    all_to_all x1, blocking collectives, on_device(): rows = lax.all_to_all(rows, 'x', 0, 0, tiled=True)  13.8 us
    all_to_all x1, blocking collectives, on_device(): lax.all_to_all(terms.reshape(size_x, size_d * stride, lanes), 'x', 0, 0,...  13.4 us
    all_to_all x1, blocking collectives, on_device(): rows = lax.all_to_all(rows, ('zl', 'zh'), 0, 0, tiled=True)  13.2 us
    ppermute x3, starting transfers between devices, shifted(): lax.ppermute(value, axes, [(i, i - 1) for i in range(1, sizes[axes])])  11.8 us
    pallas_call x10, Pallas kernels, call(): pl.pallas_call(kernel, out_shape=out_shape, in_specs=[SMEM if o.ndim == 1...  8.72 us
  transfers between devices with their start and end apart: 5, of which 5 were waited for; matrix products, arithmetic and copies ran while one was open for 0% of the time, Pallas kernels for 4%

profile of v4, /device:TPU:1, one launch (start us, length us, event | category | flops | bytes accessed | tf_op | source)
XLA Modules:
  0.0 137.4 jit_solution(6458022766311038363)
XLA Ops:
  0.0 0.8 slice_bitcast_fusion
  0.8 1.3 collective-permute-start
  2.1 0.0 copy-start
  2.2 1.3 copy-done
  3.4 0.0 copy-start.2
  3.4 1.3 copy-done.2
  4.7 0.0 copy-start.4
  4.7 0.0 copy-start.6
  4.7 0.0 copy-start.7
  4.7 0.0 copy-start.5
  4.7 0.7 face.1
  5.4 1.5 %collective-permute-done.xf_ref = f32[6,32,128]{2,1,0:T(8,128)S(1)} collective-permute-done((f32[6,32,128]{2,1,0:T(8,128)S(1)}, f32[6,32,128]{2,1,0:T(8,128)S(1)}, u32[]{:S(2)}, u32[]{:S(2)}) %collective-permute-start) | collective-permute-done | bytes 98336 | tf_op jit(solution)/shard_map/ppermute | solution.py:526
  6.9 9.3 %collective-permute-start.1 = (f32[25,8,128]{2,1,0:T(8,128)S(1)}, f32[25,8,128]{2,1,0:T(8,128)S(1)}, u32[]{:S(2)}, u32[]{:S(2)}) collective-permute-start(f32[25,8,128]{2,1,0:T(8,128)S(1)} %widen.1), channel_id=1, source_target_pairs={{4,0},{8,4},{12,8},{16,12},{20,16},{24,20},{28,24},{5,1},{9,5},{13... | collective-permute-start | bytes 307208 | tf_op jit(solution)/shard_map/ppermute | solution.py:526
  16.2 0.0 copy-done.4
  16.2 0.0 copy-done.6
  16.2 0.0 copy-done.7
  16.2 0.6 table.1
  16.8 0.2 collective-permute-done.1.yf_ref
  17.1 0.1 deepen.1
  17.2 1.3 collective-permute-start.2
  18.5 0.0 copy-done.5
  18.5 0.0 copy-start.1
  18.5 0.0 copy-start.3
  18.5 4.9 %net.1.q_ref = f32[29,9,32,128]{3,2,1,0:T(8,128)S(1)} custom-call(s32[384]{0:T(512)S(1)} %copy-done.4, bf16[3,48,4096]{2,1,0:T(8,128)(2,1)S(1)} %copy-done.5, bf16[256,512]{1,0:T(8,128)(2,1)S(1)} %get-tuple-element.19.zf_ref, bf16[3,64,192]{2,1,0:T(8,128)(2,1)S(1)} %get-tuple-element.20.yf_ref), custom_call_target="tpu_custom_call" | custom-call | flops 2000000000 | bytes 1048576 | tf_op jit(solution)/shard_map/net/pallas_call | solution.py:534
  23.4 3.6 %collective-permute-done.2.zf_ref = f32[6,40,128]{2,1,0:T(8,128)S(1)} collective-permute-done((f32[6,40,128]{2,1,0:T(8,128)S(1)}, f32[6,40,128]{2,1,0:T(8,128)S(1)}, u32[]{:S(2)}, u32[]{:S(2)}) %collective-permute-start.2) | collective-permute-done | bytes 122912 | tf_op jit(solution)/shard_map/ppermute | solution.py:526
  27.1 0.0 copy-done.1
  27.1 0.0 copy-done.3
  27.1 17.1 %elements.1 = (f32[1408,128]{1,0:T(8,128)S(1)}, f32[1408,128]{1,0:T(8,128)S(1)}) custom-call(s32[384]{0:T(512)S(1)} %copy-done.4, f32[13,24,128]{2,1,0:T(8,128)S(1)} %get-tuple-element.15.coef_ref, f32[24,3,32,128]{3,2,1,0:T(8,128)S(1)} %copy-done.1, f32[24,3,32,128]{3,2,1,0:T(8,128)S(1)} %copy-done.3, f32[6,32,128]{2,1,0:T(8,128)S(1)} %collective-permute-done.xf_ref, ...), custom_call_target="tpu_custom_call" | custom-call | flops 10000000000 | bytes 10485760 | tf_op jit(solution)/shard_map/elements/pallas_call | solution.py:593
  44.2 2.4 %collective-permute-start.3 = (f32[1408,128]{1,0:T(8,128)S(1)}, f32[1408,128]{1,0:T(8,128)S(1)}, u32[]{:S(2)}, u32[]{:S(2)}) collective-permute-start(f32[1408,128]{1,0:T(8,128)S(1)} %get-tuple-element.24), channel_id=1, source_target_pairs={{0,4},{4,0},{1,5},{5,1},{2,6},{6,2},{3,7},{7,3},{8,12},{12,8},{9,1... | collective-permute-start | bytes 2162696 | tf_op jit(solution)/shard_map/ppermute | solution.py:633
  46.6 1.8 %collective-permute-done.3 = f32[1408,128]{1,0:T(8,128)S(1)} collective-permute-done((f32[1408,128]{1,0:T(8,128)S(1)}, f32[1408,128]{1,0:T(8,128)S(1)}, u32[]{:S(2)}, u32[]{:S(2)}) %collective-permute-start.3) | collective-permute-done | bytes 720928 | tf_op jit(solution)/shard_map/ppermute | solution.py:633
  48.4 0.1 add.3
  48.5 13.4 %all_to_all.25 = f32[4,352,128]{2,1,0:T(8,128)S(1)} all-to-all(f32[4,352,128]{2,1,0:T(8,128)S(1)} %bitcast.11), channel_id=1, replica_groups=mesh['zl'=2,'y'=8,'x'=4,'c'=2,'zh'=4] {'x'}, dimensions={0} | all-to-all | bytes 1441792 | tf_op jit(solution)/shard_map/all_to_all | solution.py:634
  61.9 0.6 spread.1
  62.5 18.2 %all_to_all.26.in_ref = f32[8,80,128]{2,1,0:T(8,128)S(1)} all-to-all(f32[8,80,128]{2,1,0:T(8,128)S(1)} %spread.1), channel_id=1, replica_groups=mesh['zl'=2,'y'=8,'x'=4,'c'=2,'zh'=4] {'zl','zh'}, dimensions={0} | all-to-all | bytes 655360 | tf_op jit(solution)/shard_map/all_to_all | solution.py:643
  80.7 17.5 %all_to_all.27.in_ref = f32[8,80,128]{2,1,0:T(8,128)S(1)} all-to-all(f32[8,80,128]{2,1,0:T(8,128)S(1)} %collect.1), channel_id=1, replica_groups=mesh['zl'=2,'y'=8,'x'=4,'c'=2,'zh'=4] {'y'}, dimensions={0} | all-to-all | bytes 655360 | tf_op jit(solution)/shard_map/all_to_all | solution.py:645
  98.2 0.1 scale.1
  98.3 13.2 %all_to_all.28.in_ref = f32[8,72,128]{2,1,0:T(8,128)S(1)} all-to-all(f32[8,72,128]{2,1,0:T(8,128)S(1)} %scale.1), channel_id=1, replica_groups=mesh['zl'=2,'y'=8,'x'=4,'c'=2,'zh'=4] {'zl','zh'}, dimensions={0} | all-to-all | bytes 589824 | tf_op jit(solution)/shard_map/all_to_all | solution.py:650
  111.5 0.1 repack.1
  111.6 13.8 %all_to_all.29.own_ref = f32[4,12,48,128]{3,2,1,0:T(8,128)S(1)} all-to-all(f32[4,12,48,128]{3,2,1,0:T(8,128)S(1)} %repack.1), channel_id=1, replica_groups=mesh['zl'=2,'y'=8,'x'=4,'c'=2,'zh'=4] {'x'}, dimensions={0} | all-to-all | bytes 2359296 | tf_op jit(solution)/shard_map/all_to_all | solution.py:657
  125.4 8.0 %collective-permute-start.4 = (f32[4,12,48,128]{3,2,1,0:T(8,128)S(1)}, f32[4,12,48,128]{3,2,1,0:T(8,128)S(1)}, u32[]{:S(2)}, u32[]{:S(2)}) collective-permute-start(f32[4,12,48,128]{3,2,1,0:T(8,128)S(1)} %all_to_all.29.own_ref), channel_id=1, source_target_pairs={{0,4},{4,0},{1,5},{5,1},{2,6},{6,2},{3,7},{7,3},{8,12},{12,8},{9,1... | collective-permute-start | bytes 3538952 | tf_op jit(solution)/shard_map/ppermute | solution.py:658
  133.4 2.5 %collective-permute-done.4.other_ref = f32[4,12,48,128]{3,2,1,0:T(8,128)S(1)} collective-permute-done((f32[4,12,48,128]{3,2,1,0:T(8,128)S(1)}, f32[4,12,48,128]{3,2,1,0:T(8,128)S(1)}, u32[]{:S(2)}, u32[]{:S(2)}) %collective-permute-start.4) | collective-permute-done | bytes 1179680 | tf_op jit(solution)/shard_map/ppermute | solution.py:658
  135.8 1.6 %place.1 = f32[3,48,4096]{2,1,0:T(8,128)} custom-call(f32[4,12,48,128]{3,2,1,0:T(8,128)S(1)} %all_to_all.29.own_ref, f32[4,12,48,128]{3,2,1,0:T(8,128)S(1)} %collective-permute-done.4.other_ref), custom_call_target="tpu_custom_call" | custom-call | flops 1000000 | bytes 1048576 | tf_op jit(solution)/shard_map/place/pallas_call | solution.py:534
  (4 shorter events, 0.1 us)
Async XLA Ops:
  0.8 6.0 %collective-permute-start = (f32[6,32,128]{2,1,0:T(8,128)S(1)}, f32[6,32,128]{2,1,0:T(8,128)S(1)}, u32[]{:S(2)}, u32[]{:S(2)}) collective-permute-start(f32[6,32,128]{2,1,0:T(8,128)S(1)} %pad_maximum_fusion), channel_id=1, source_target_pairs={{32,0},{64,32},{96,64},{128,96},{160,128},{192,160},{224,192},{256... | collective-permute-start | bytes 294920 | tf_op jit(solution)/shard_map/ppermute | solution.py:526
  2.1 1.3 copy-start
  3.4 1.3 copy-start.2
  4.7 11.5 %copy-start.4 = (s32[384]{0:T(512)S(1)}, s32[384]{0:T(512)}, u32[]{:S(2)}) copy-start(s32[384]{0:T(512)} %sx_smem.5) | copy-start | bytes 4612
  4.7 11.5 %copy-start.6 = (s32[512]{0:T(512)S(1)}, s32[512]{0:T(512)}, u32[]{:S(2)}) copy-start(s32[512]{0:T(512)} %param.11) | copy-start | bytes 6148
  4.7 11.5 %copy-start.7 = (s32[256]{0:T(256)S(1)}, s32[256]{0:T(256)}, u32[]{:S(2)}) copy-start(s32[256]{0:T(256)} %param.10) | copy-start | bytes 3076
  4.7 13.8 %copy-start.5 = (bf16[3,48,4096]{2,1,0:T(8,128)(2,1)S(1)}, bf16[3,48,4096]{2,1,0:T(8,128)(2,1)}, u32[]{:S(2)}) copy-start(bf16[3,48,4096]{2,1,0:T(8,128)(2,1)} %o_ref.1) | copy-start | bytes 3538948
  6.9 10.2 %collective-permute-start.1 = (f32[25,8,128]{2,1,0:T(8,128)S(1)}, f32[25,8,128]{2,1,0:T(8,128)S(1)}, u32[]{:S(2)}, u32[]{:S(2)}) collective-permute-start(f32[25,8,128]{2,1,0:T(8,128)S(1)} %widen.1), channel_id=1, source_target_pairs={{4,0},{8,4},{12,8},{16,12},{20,16},{24,20},{28,24},{5,1},{9,5},{13... | collective-permute-start | bytes 307208 | tf_op jit(solution)/shard_map/ppermute | solution.py:526
  17.2 9.8 %collective-permute-start.2 = (f32[6,40,128]{2,1,0:T(8,128)S(1)}, f32[6,40,128]{2,1,0:T(8,128)S(1)}, u32[]{:S(2)}, u32[]{:S(2)}) collective-permute-start(f32[6,40,128]{2,1,0:T(8,128)S(1)} %deepen.1), channel_id=1, source_target_pairs={{1,0},{2,1},{3,2},{5,4},{6,5},{7,6},{9,8},{10,9},{11,10},{13,12},{... | collective-permute-start | bytes 368648 | tf_op jit(solution)/shard_map/ppermute | solution.py:526
  18.5 8.5 %copy-start.1 = (f32[24,3,32,128]{3,2,1,0:T(8,128)S(1)}, f32[24,3,32,128]{3,2,1,0:T(8,128)}, u32[]{:S(2)}) copy-start(f32[24,3,32,128]{3,2,1,0:T(8,128)} %u_ref.3) | copy-start | bytes 3538948
  18.5 8.5 %copy-start.3 = (f32[24,3,32,128]{3,2,1,0:T(8,128)S(1)}, f32[24,3,32,128]{3,2,1,0:T(8,128)}, u32[]{:S(2)}) copy-start(f32[24,3,32,128]{3,2,1,0:T(8,128)} %w_ref.3) | copy-start | bytes 3538948
  44.2 4.2 %collective-permute-start.3 = (f32[1408,128]{1,0:T(8,128)S(1)}, f32[1408,128]{1,0:T(8,128)S(1)}, u32[]{:S(2)}, u32[]{:S(2)}) collective-permute-start(f32[1408,128]{1,0:T(8,128)S(1)} %get-tuple-element.24), channel_id=1, source_target_pairs={{0,4},{4,0},{1,5},{5,1},{2,6},{6,2},{3,7},{7,3},{8,12},{12,8},{9,1... | collective-permute-start | bytes 2162696 | tf_op jit(solution)/shard_map/ppermute | solution.py:633
  125.4 10.5 %collective-permute-start.4 = (f32[4,12,48,128]{3,2,1,0:T(8,128)S(1)}, f32[4,12,48,128]{3,2,1,0:T(8,128)S(1)}, u32[]{:S(2)}, u32[]{:S(2)}) collective-permute-start(f32[4,12,48,128]{3,2,1,0:T(8,128)S(1)} %all_to_all.29.own_ref), channel_id=1, source_target_pairs={{0,4},{4,0},{1,5},{5,1},{2,6},{6,2},{3,7},{7,3},{8,12},{12,8},{9,1... | collective-permute-start | bytes 3538952 | tf_op jit(solution)/shard_map/ppermute | solution.py:658

commit v5 on v4

--- a/solution.py
+++ b/solution.py
@@ -557,7 +557,7 @@
     return call(
         functools.partial(table_kernel, nx),
         (
-            array(13, -(-nx // 8) * 8, nz),
+            array(13, -(-nx // 8) * 8 + 8, nz),
             array(6, ny, nz),
             array(NCY, 6 * ny, dtype=BF16),
             array(4 * nz, 4 * NCZ, dtype=BF16),
@@ -578,7 +578,7 @@
         offsets,
         z_front,
         y_front,
-        scratch=[((3 * NCX * PITCH, nz), F32)] * 2,
+        scratch=[((3 * NCX * PITCH + 2 * NCY, nz), F32)] * 2,
         limit=20,
         flops=2 * 10**9,
     )
@@ -603,7 +603,7 @@
             pltpu.VMEM((window + 1, 9, ny, nz), F32),
             pltpu.VMEM((3 * window * half, 4 * nz), BF16),
             pltpu.VMEM((3 * window * half, 4 * nz), BF16),
-            pltpu.VMEM((half * (stride + 1), 2 * NCZ), F32),
+            pltpu.VMEM(((half + 1) * (stride + 1), 2 * NCZ), F32),
         ],
         name="elements",
         compiler_params=pltpu.CompilerParams(vmem_limit_bytes=24 * MIB),
@@ -638,7 +638,7 @@
         array(blocks, rows + 8, lanes),
         span_x,
         terms.reshape(size_x, size_d, stride, lanes),
-        scratch=[((3 * NCX, lanes), F32)],
+        scratch=[((3 * NCX + 8, lanes), F32)],
     )
     terms = lax.all_to_all(terms, ("zl", "zh"), 0, 0, tiled=True)
     terms = call(collect_kernel, array(size_y, rows + 8, lanes), terms)

time: 138 us -> 138 us (level)
  transfers between devices with their start and end apart: 5 -> 5, of which waited for: 5 -> 5; matrix products, arithmetic and copies ran while one was open for 0% -> 0% of each run, Pallas kernels for 4% -> 5%
where the time goes in v5:
time: 138 us; the launch traced here: 137 us
  blocking collectives  76 us (55%)
  Pallas kernels  25.9 us (19%)
  starting transfers between devices  22.3 us (16%)
  waiting for transfers between devices  9.61 us (7%)
  local copies, waits for them, and re-layouts  3.4 us (2%)
    all_to_all x1, blocking collectives, on_device(): terms = lax.all_to_all(terms, ('zl', 'zh'), 0, 0, tiled=True)  18.2 us
    all_to_all x1, blocking collectives, on_device(): terms = lax.all_to_all(terms, 'y', 0, 0, tiled=True)  17.5 us
    pallas_call x1, Pallas kernels, brick_terms(): pl.pallas_call(element_kernel, out_shape=(jax.ShapeDtypeStruct((half // 2...  17.1 us
    all_to_all x1, blocking collectives, on_device(): rows = lax.all_to_all(rows, 'x', 0, 0, tiled=True)  13.8 us
    all_to_all x1, blocking collectives, on_device(): lax.all_to_all(terms.reshape(size_x, size_d * stride, lanes), 'x', 0, 0,...  13.4 us
    all_to_all x1, blocking collectives, on_device(): rows = lax.all_to_all(rows, ('zl', 'zh'), 0, 0, tiled=True)  13.2 us
    ppermute x3, starting transfers between devices, shifted(): lax.ppermute(value, axes, [(i, i - 1) for i in range(1, sizes[axes])])  11.8 us
    pallas_call x10, Pallas kernels, call(): pl.pallas_call(kernel, out_shape=out_shape, in_specs=[SMEM if o.ndim == 1...  8.73 us
  transfers between devices with their start and end apart: 5, of which 5 were waited for; matrix products, arithmetic and copies ran while one was open for 0% of the time, Pallas kernels for 5%

profile of v5, /device:TPU:1, one launch (start us, length us, event | category | flops | bytes accessed | tf_op | source)
XLA Modules:
  0.0 137.4 jit_solution(15134891896621446460)
XLA Ops:
  0.0 0.8 slice_bitcast_fusion
  0.8 1.3 collective-permute-start
  2.1 0.0 copy-start
  2.2 1.3 copy-done
  3.4 0.0 copy-start.2
  3.4 1.3 copy-done.2
  4.7 0.0 copy-start.4
  4.7 0.0 copy-start.6
  4.7 0.0 copy-start.7
  4.7 0.0 copy-start.5
  4.7 0.7 face.1
  5.4 1.5 %collective-permute-done.xf_ref = f32[6,32,128]{2,1,0:T(8,128)S(1)} collective-permute-done((f32[6,32,128]{2,1,0:T(8,128)S(1)}, f32[6,32,128]{2,1,0:T(8,128)S(1)}, u32[]{:S(2)}, u32[]{:S(2)}) %collective-permute-start) | collective-permute-done | bytes 98336 | tf_op jit(solution)/shard_map/ppermute | solution.py:526
  6.9 9.3 %collective-permute-start.1 = (f32[25,8,128]{2,1,0:T(8,128)S(1)}, f32[25,8,128]{2,1,0:T(8,128)S(1)}, u32[]{:S(2)}, u32[]{:S(2)}) collective-permute-start(f32[25,8,128]{2,1,0:T(8,128)S(1)} %widen.1), channel_id=1, source_target_pairs={{4,0},{8,4},{12,8},{16,12},{20,16},{24,20},{28,24},{5,1},{9,5},{13... | collective-permute-start | bytes 307208 | tf_op jit(solution)/shard_map/ppermute | solution.py:526
  16.2 0.0 copy-done.4
  16.2 0.0 copy-done.6
  16.2 0.0 copy-done.7
  16.2 0.7 table.1
  16.9 0.2 collective-permute-done.1.yf_ref
  17.1 0.1 deepen.1
  17.2 1.3 collective-permute-start.2
  18.5 0.0 copy-done.5
  18.5 0.0 copy-start.1
  18.5 0.0 copy-start.3
  18.5 4.9 %net.1.q_ref = f32[29,9,32,128]{3,2,1,0:T(8,128)S(1)} custom-call(s32[384]{0:T(512)S(1)} %copy-done.4, bf16[3,48,4096]{2,1,0:T(8,128)(2,1)S(1)} %copy-done.5, bf16[256,512]{1,0:T(8,128)(2,1)S(1)} %get-tuple-element.19.zf_ref, bf16[3,64,192]{2,1,0:T(8,128)(2,1)S(1)} %get-tuple-element.20.yf_ref), custom_call_target="tpu_custom_call" | custom-call | flops 2000000000 | bytes 1048576 | tf_op jit(solution)/shard_map/net/pallas_call | solution.py:534
  23.4 3.6 %collective-permute-done.2.zf_ref = f32[6,40,128]{2,1,0:T(8,128)S(1)} collective-permute-done((f32[6,40,128]{2,1,0:T(8,128)S(1)}, f32[6,40,128]{2,1,0:T(8,128)S(1)}, u32[]{:S(2)}, u32[]{:S(2)}) %collective-permute-start.2) | collective-permute-done | bytes 122912 | tf_op jit(solution)/shard_map/ppermute | solution.py:526
  27.1 0.0 copy-done.1
  27.1 0.0 copy-done.3
  27.1 17.1 %elements.1 = (f32[1408,128]{1,0:T(8,128)S(1)}, f32[1408,128]{1,0:T(8,128)S(1)}) custom-call(s32[384]{0:T(512)S(1)} %copy-done.4, f32[13,32,128]{2,1,0:T(8,128)S(1)} %get-tuple-element.15.coef_ref, f32[24,3,32,128]{3,2,1,0:T(8,128)S(1)} %copy-done.1, f32[24,3,32,128]{3,2,1,0:T(8,128)S(1)} %copy-done.3, f32[6,32,128]{2,1,0:T(8,128)S(1)} %collective-permute-done.xf_ref, ...), custom_call_target="tpu_custom_call" | custom-call | flops 10000000000 | bytes 10485760 | tf_op jit(solution)/shard_map/elements/pallas_call | solution.py:593
  44.2 2.4 %collective-permute-start.3 = (f32[1408,128]{1,0:T(8,128)S(1)}, f32[1408,128]{1,0:T(8,128)S(1)}, u32[]{:S(2)}, u32[]{:S(2)}) collective-permute-start(f32[1408,128]{1,0:T(8,128)S(1)} %get-tuple-element.24), channel_id=1, source_target_pairs={{0,4},{4,0},{1,5},{5,1},{2,6},{6,2},{3,7},{7,3},{8,12},{12,8},{9,1... | collective-permute-start | bytes 2162696 | tf_op jit(solution)/shard_map/ppermute | solution.py:633
  46.6 1.8 %collective-permute-done.3 = f32[1408,128]{1,0:T(8,128)S(1)} collective-permute-done((f32[1408,128]{1,0:T(8,128)S(1)}, f32[1408,128]{1,0:T(8,128)S(1)}, u32[]{:S(2)}, u32[]{:S(2)}) %collective-permute-start.3) | collective-permute-done | bytes 720928 | tf_op jit(solution)/shard_map/ppermute | solution.py:633
  48.4 0.1 add.3
  48.5 13.4 %all_to_all.25 = f32[4,352,128]{2,1,0:T(8,128)S(1)} all-to-all(f32[4,352,128]{2,1,0:T(8,128)S(1)} %bitcast.11), channel_id=1, replica_groups=mesh['zl'=2,'y'=8,'x'=4,'c'=2,'zh'=4] {'x'}, dimensions={0} | all-to-all | bytes 1441792 | tf_op jit(solution)/shard_map/all_to_all | solution.py:634
  61.9 0.6 spread.1
  62.5 18.2 %all_to_all.26.in_ref = f32[8,80,128]{2,1,0:T(8,128)S(1)} all-to-all(f32[8,80,128]{2,1,0:T(8,128)S(1)} %spread.1), channel_id=1, replica_groups=mesh['zl'=2,'y'=8,'x'=4,'c'=2,'zh'=4] {'zl','zh'}, dimensions={0} | all-to-all | bytes 655360 | tf_op jit(solution)/shard_map/all_to_all | solution.py:643
  80.7 17.5 %all_to_all.27.in_ref = f32[8,80,128]{2,1,0:T(8,128)S(1)} all-to-all(f32[8,80,128]{2,1,0:T(8,128)S(1)} %collect.1), channel_id=1, replica_groups=mesh['zl'=2,'y'=8,'x'=4,'c'=2,'zh'=4] {'y'}, dimensions={0} | all-to-all | bytes 655360 | tf_op jit(solution)/shard_map/all_to_all | solution.py:645
  98.2 0.1 scale.1
  98.3 13.2 %all_to_all.28.in_ref = f32[8,72,128]{2,1,0:T(8,128)S(1)} all-to-all(f32[8,72,128]{2,1,0:T(8,128)S(1)} %scale.1), channel_id=1, replica_groups=mesh['zl'=2,'y'=8,'x'=4,'c'=2,'zh'=4] {'zl','zh'}, dimensions={0} | all-to-all | bytes 589824 | tf_op jit(solution)/shard_map/all_to_all | solution.py:650
  111.5 0.1 repack.1
  111.6 13.8 %all_to_all.29.own_ref = f32[4,12,48,128]{3,2,1,0:T(8,128)S(1)} all-to-all(f32[4,12,48,128]{3,2,1,0:T(8,128)S(1)} %repack.1), channel_id=1, replica_groups=mesh['zl'=2,'y'=8,'x'=4,'c'=2,'zh'=4] {'x'}, dimensions={0} | all-to-all | bytes 2359296 | tf_op jit(solution)/shard_map/all_to_all | solution.py:657
  125.4 8.0 %collective-permute-start.4 = (f32[4,12,48,128]{3,2,1,0:T(8,128)S(1)}, f32[4,12,48,128]{3,2,1,0:T(8,128)S(1)}, u32[]{:S(2)}, u32[]{:S(2)}) collective-permute-start(f32[4,12,48,128]{3,2,1,0:T(8,128)S(1)} %all_to_all.29.own_ref), channel_id=1, source_target_pairs={{0,4},{4,0},{1,5},{5,1},{2,6},{6,2},{3,7},{7,3},{8,12},{12,8},{9,1... | collective-permute-start | bytes 3538952 | tf_op jit(solution)/shard_map/ppermute | solution.py:658
  133.4 2.5 %collective-permute-done.4.other_ref = f32[4,12,48,128]{3,2,1,0:T(8,128)S(1)} collective-permute-done((f32[4,12,48,128]{3,2,1,0:T(8,128)S(1)}, f32[4,12,48,128]{3,2,1,0:T(8,128)S(1)}, u32[]{:S(2)}, u32[]{:S(2)}) %collective-permute-start.4) | collective-permute-done | bytes 1179680 | tf_op jit(solution)/shard_map/ppermute | solution.py:658
  135.8 1.6 %place.1 = f32[3,48,4096]{2,1,0:T(8,128)} custom-call(f32[4,12,48,128]{3,2,1,0:T(8,128)S(1)} %all_to_all.29.own_ref, f32[4,12,48,128]{3,2,1,0:T(8,128)S(1)} %collective-permute-done.4.other_ref), custom_call_target="tpu_custom_call" | custom-call | flops 1000000 | bytes 1048576 | tf_op jit(solution)/shard_map/place/pallas_call | solution.py:534
  (4 shorter events, 0.1 us)
Async XLA Ops:
  0.8 6.0 %collective-permute-start = (f32[6,32,128]{2,1,0:T(8,128)S(1)}, f32[6,32,128]{2,1,0:T(8,128)S(1)}, u32[]{:S(2)}, u32[]{:S(2)}) collective-permute-start(f32[6,32,128]{2,1,0:T(8,128)S(1)} %pad_maximum_fusion), channel_id=1, source_target_pairs={{32,0},{64,32},{96,64},{128,96},{160,128},{192,160},{224,192},{256... | collective-permute-start | bytes 294920 | tf_op jit(solution)/shard_map/ppermute | solution.py:526
  2.1 1.3 copy-start
  3.4 1.3 copy-start.2
  4.7 11.5 %copy-start.4 = (s32[384]{0:T(512)S(1)}, s32[384]{0:T(512)}, u32[]{:S(2)}) copy-start(s32[384]{0:T(512)} %sx_smem.5) | copy-start | bytes 4612
  4.7 11.5 %copy-start.6 = (s32[512]{0:T(512)S(1)}, s32[512]{0:T(512)}, u32[]{:S(2)}) copy-start(s32[512]{0:T(512)} %param.11) | copy-start | bytes 6148
  4.7 11.5 %copy-start.7 = (s32[256]{0:T(256)S(1)}, s32[256]{0:T(256)}, u32[]{:S(2)}) copy-start(s32[256]{0:T(256)} %param.10) | copy-start | bytes 3076
  4.7 13.8 %copy-start.5 = (bf16[3,48,4096]{2,1,0:T(8,128)(2,1)S(1)}, bf16[3,48,4096]{2,1,0:T(8,128)(2,1)}, u32[]{:S(2)}) copy-start(bf16[3,48,4096]{2,1,0:T(8,128)(2,1)} %o_ref.1) | copy-start | bytes 3538948
  6.9 10.2 %collective-permute-start.1 = (f32[25,8,128]{2,1,0:T(8,128)S(1)}, f32[25,8,128]{2,1,0:T(8,128)S(1)}, u32[]{:S(2)}, u32[]{:S(2)}) collective-permute-start(f32[25,8,128]{2,1,0:T(8,128)S(1)} %widen.1), channel_id=1, source_target_pairs={{4,0},{8,4},{12,8},{16,12},{20,16},{24,20},{28,24},{5,1},{9,5},{13... | collective-permute-start | bytes 307208 | tf_op jit(solution)/shard_map/ppermute | solution.py:526
  17.2 9.8 %collective-permute-start.2 = (f32[6,40,128]{2,1,0:T(8,128)S(1)}, f32[6,40,128]{2,1,0:T(8,128)S(1)}, u32[]{:S(2)}, u32[]{:S(2)}) collective-permute-start(f32[6,40,128]{2,1,0:T(8,128)S(1)} %deepen.1), channel_id=1, source_target_pairs={{1,0},{2,1},{3,2},{5,4},{6,5},{7,6},{9,8},{10,9},{11,10},{13,12},{... | collective-permute-start | bytes 368648 | tf_op jit(solution)/shard_map/ppermute | solution.py:526
  18.5 8.5 %copy-start.1 = (f32[24,3,32,128]{3,2,1,0:T(8,128)S(1)}, f32[24,3,32,128]{3,2,1,0:T(8,128)}, u32[]{:S(2)}) copy-start(f32[24,3,32,128]{3,2,1,0:T(8,128)} %u_ref.3) | copy-start | bytes 3538948
  18.5 8.5 %copy-start.3 = (f32[24,3,32,128]{3,2,1,0:T(8,128)S(1)}, f32[24,3,32,128]{3,2,1,0:T(8,128)}, u32[]{:S(2)}) copy-start(f32[24,3,32,128]{3,2,1,0:T(8,128)} %w_ref.3) | copy-start | bytes 3538948
  44.2 4.2 %collective-permute-start.3 = (f32[1408,128]{1,0:T(8,128)S(1)}, f32[1408,128]{1,0:T(8,128)S(1)}, u32[]{:S(2)}, u32[]{:S(2)}) collective-permute-start(f32[1408,128]{1,0:T(8,128)S(1)} %get-tuple-element.24), channel_id=1, source_target_pairs={{0,4},{4,0},{1,5},{5,1},{2,6},{6,2},{3,7},{7,3},{8,12},{12,8},{9,1... | collective-permute-start | bytes 2162696 | tf_op jit(solution)/shard_map/ppermute | solution.py:633
  125.4 10.5 %collective-permute-start.4 = (f32[4,12,48,128]{3,2,1,0:T(8,128)S(1)}, f32[4,12,48,128]{3,2,1,0:T(8,128)S(1)}, u32[]{:S(2)}, u32[]{:S(2)}) collective-permute-start(f32[4,12,48,128]{3,2,1,0:T(8,128)S(1)} %all_to_all.29.own_ref), channel_id=1, source_target_pairs={{0,4},{4,0},{1,5},{5,1},{2,6},{6,2},{3,7},{7,3},{8,12},{12,8},{9,1... | collective-permute-start | bytes 3538952 | tf_op jit(solution)/shard_map/ppermute | solution.py:658

commit v6 on v5

--- a/solution.py
+++ b/solution.py
@@ -510,16 +510,21 @@
                 out_ref[copy, r * depth + d] = value
 
 
-def place_kernel(own_ref, other_ref, out_ref):
+def place_kernel(own_ref, other_ref, out_hbm, result, sems):
     chips, blocks, rows, lanes = own_ref.shape
     depth = blocks // 3
     core = lax.axis_index("c")
-    for ref, c in ((own_ref, core), (other_ref, 1 - core)):
-        for x in range(chips):
-            for r in range(3):
+    copies = []
+    for r in range(3):
+        for ref, c in ((own_ref, core), (other_ref, 1 - core)):
+            for x in range(chips):
                 for d in range(depth):
-                    at = ((2 * x + c) * depth + d) * lanes
-                    out_ref[r, :, pl.ds(pl.multiple_of(at, lanes), lanes)] = ref[x, r * depth + d]
+                    at = pl.multiple_of(((2 * x + c) * depth + d) * lanes, lanes)
+                    result[r, :, pl.ds(at, lanes)] = ref[x, r * depth + d]
+        copies.append(pltpu.make_async_copy(result.at[r], out_hbm.at[r], sems.at[r]))
+        copies[-1].start()
+    for copy in copies:
+        copy.wait()
 
 
 def shifted(value, axes, sizes):
@@ -656,7 +661,18 @@
     )
     rows = lax.all_to_all(rows, "x", 0, 0, tiled=True)
     other = lax.ppermute(rows, "c", swap)
-    return call(place_kernel, array(3, NCX, NCY * NCZ), rows, other)
+    return pl.pallas_call(
+        place_kernel,
+        out_shape=array(3, NCX, NCY * NCZ),
+        in_specs=[VMEM] * 2,
+        out_specs=pl.BlockSpec(memory_space=pltpu.HBM),
+        scratch_shapes=[
+            pltpu.VMEM((3, NCX, NCY * NCZ), F32),
+            pltpu.SemaphoreType.DMA((3,)),
+        ],
+        name="place",
+        compiler_params=pltpu.CompilerParams(vmem_limit_bytes=16 * MIB),
+    )(rows, other)
 
 
 def solution(mesh):

time: 138 us -> 138 us (level)
    pallas_call x10 -> x9, Pallas kernels: 8.73 us -> 7.15 us  [call(): pl.pallas_call(kernel, out_shape=out_shape, in_specs=[SMEM if o.ndim == 1...]
    pallas_call x0 -> x1, Pallas kernels: none -> 1.48 us  [on_device(): pl.pallas_call(place_kernel, out_shape=array(3, NCX, NCY * NCZ), in_specs...]
where the time goes in v6:
time: 138 us; the launch traced here: 137 us
  blocking collectives  76 us (55%)
  Pallas kernels  25.8 us (19%)
  starting transfers between devices  22.3 us (16%)
  waiting for transfers between devices  9.61 us (7%)
  local copies, waits for them, and re-layouts  3.4 us (2%)
    all_to_all x1, blocking collectives, on_device(): terms = lax.all_to_all(terms, ('zl', 'zh'), 0, 0, tiled=True)  18.2 us
    all_to_all x1, blocking collectives, on_device(): terms = lax.all_to_all(terms, 'y', 0, 0, tiled=True)  17.5 us
    pallas_call x1, Pallas kernels, brick_terms(): pl.pallas_call(element_kernel, out_shape=(jax.ShapeDtypeStruct((half // 2...  17.1 us
    all_to_all x1, blocking collectives, on_device(): rows = lax.all_to_all(rows, 'x', 0, 0, tiled=True)  13.8 us
    all_to_all x1, blocking collectives, on_device(): lax.all_to_all(terms.reshape(size_x, size_d * stride, lanes), 'x', 0, 0,...  13.4 us
    all_to_all x1, blocking collectives, on_device(): rows = lax.all_to_all(rows, ('zl', 'zh'), 0, 0, tiled=True)  13.2 us
    ppermute x3, starting transfers between devices, shifted(): lax.ppermute(value, axes, [(i, i - 1) for i in range(1, sizes[axes])])  11.8 us
    ppermute x1, starting transfers between devices, on_device(): other = lax.ppermute(rows, 'c', swap)  8.02 us
  transfers between devices with their start and end apart: 5, of which 5 were waited for; matrix products, arithmetic and copies ran while one was open for 0% of the time, Pallas kernels for 5%

profile of v6, /device:TPU:1, one launch (start us, length us, event | category | flops | bytes accessed | tf_op | source)
XLA Modules:
  0.0 137.3 jit_solution(9634829644641842903)
XLA Ops:
  0.0 0.8 slice_bitcast_fusion
  0.8 1.3 collective-permute-start
  2.1 0.0 copy-start
  2.2 1.3 copy-done
  3.4 0.0 copy-start.2
  3.4 1.3 copy-done.2
  4.7 0.0 copy-start.4
  4.7 0.0 copy-start.6
  4.7 0.0 copy-start.7
  4.7 0.0 copy-start.5
  4.7 0.7 face.1
  5.4 1.5 %collective-permute-done.xf_ref = f32[6,32,128]{2,1,0:T(8,128)S(1)} collective-permute-done((f32[6,32,128]{2,1,0:T(8,128)S(1)}, f32[6,32,128]{2,1,0:T(8,128)S(1)}, u32[]{:S(2)}, u32[]{:S(2)}) %collective-permute-start) | collective-permute-done | bytes 98336 | tf_op jit(solution)/shard_map/ppermute | solution.py:531
  6.9 9.3 %collective-permute-start.1 = (f32[25,8,128]{2,1,0:T(8,128)S(1)}, f32[25,8,128]{2,1,0:T(8,128)S(1)}, u32[]{:S(2)}, u32[]{:S(2)}) collective-permute-start(f32[25,8,128]{2,1,0:T(8,128)S(1)} %widen.1), channel_id=1, source_target_pairs={{4,0},{8,4},{12,8},{16,12},{20,16},{24,20},{28,24},{5,1},{9,5},{13... | collective-permute-start | bytes 307208 | tf_op jit(solution)/shard_map/ppermute | solution.py:531
  16.2 0.0 copy-done.4
  16.2 0.0 copy-done.6
  16.2 0.0 copy-done.7
  16.2 0.7 table.1
  16.9 0.2 collective-permute-done.1.yf_ref
  17.1 0.1 deepen.1
  17.2 1.3 collective-permute-start.2
  18.5 0.0 copy-done.5
  18.5 0.0 copy-start.1
  18.5 0.0 copy-start.3
  18.5 4.9 %net.1.q_ref = f32[29,9,32,128]{3,2,1,0:T(8,128)S(1)} custom-call(s32[384]{0:T(512)S(1)} %copy-done.4, bf16[3,48,4096]{2,1,0:T(8,128)(2,1)S(1)} %copy-done.5, bf16[256,512]{1,0:T(8,128)(2,1)S(1)} %get-tuple-element.19.zf_ref, bf16[3,64,192]{2,1,0:T(8,128)(2,1)S(1)} %get-tuple-element.20.yf_ref), custom_call_target="tpu_custom_call" | custom-call | flops 2000000000 | bytes 1048576 | tf_op jit(solution)/shard_map/net/pallas_call | solution.py:539
  23.4 3.6 %collective-permute-done.2.zf_ref = f32[6,40,128]{2,1,0:T(8,128)S(1)} collective-permute-done((f32[6,40,128]{2,1,0:T(8,128)S(1)}, f32[6,40,128]{2,1,0:T(8,128)S(1)}, u32[]{:S(2)}, u32[]{:S(2)}) %collective-permute-start.2) | collective-permute-done | bytes 122912 | tf_op jit(solution)/shard_map/ppermute | solution.py:531
  27.1 0.0 copy-done.1
  27.1 0.0 copy-done.3
  27.1 17.1 %elements.1 = (f32[1408,128]{1,0:T(8,128)S(1)}, f32[1408,128]{1,0:T(8,128)S(1)}) custom-call(s32[384]{0:T(512)S(1)} %copy-done.4, f32[13,32,128]{2,1,0:T(8,128)S(1)} %get-tuple-element.15.coef_ref, f32[24,3,32,128]{3,2,1,0:T(8,128)S(1)} %copy-done.1, f32[24,3,32,128]{3,2,1,0:T(8,128)S(1)} %copy-done.3, f32[6,32,128]{2,1,0:T(8,128)S(1)} %collective-permute-done.xf_ref, ...), custom_call_target="tpu_custom_call" | custom-call | flops 10000000000 | bytes 10485760 | tf_op jit(solution)/shard_map/elements/pallas_call | solution.py:598
  44.2 2.4 %collective-permute-start.3 = (f32[1408,128]{1,0:T(8,128)S(1)}, f32[1408,128]{1,0:T(8,128)S(1)}, u32[]{:S(2)}, u32[]{:S(2)}) collective-permute-start(f32[1408,128]{1,0:T(8,128)S(1)} %get-tuple-element.24), channel_id=1, source_target_pairs={{0,4},{4,0},{1,5},{5,1},{2,6},{6,2},{3,7},{7,3},{8,12},{12,8},{9,1... | collective-permute-start | bytes 2162696 | tf_op jit(solution)/shard_map/ppermute | solution.py:638
  46.6 1.8 %collective-permute-done.3 = f32[1408,128]{1,0:T(8,128)S(1)} collective-permute-done((f32[1408,128]{1,0:T(8,128)S(1)}, f32[1408,128]{1,0:T(8,128)S(1)}, u32[]{:S(2)}, u32[]{:S(2)}) %collective-permute-start.3) | collective-permute-done | bytes 720928 | tf_op jit(solution)/shard_map/ppermute | solution.py:638
  48.4 0.1 add.3
  48.5 13.4 %all_to_all.25 = f32[4,352,128]{2,1,0:T(8,128)S(1)} all-to-all(f32[4,352,128]{2,1,0:T(8,128)S(1)} %bitcast.11), channel_id=1, replica_groups=mesh['zl'=2,'y'=8,'x'=4,'c'=2,'zh'=4] {'x'}, dimensions={0} | all-to-all | bytes 1441792 | tf_op jit(solution)/shard_map/all_to_all | solution.py:639
  61.9 0.6 spread.1
  62.5 18.2 %all_to_all.26.in_ref = f32[8,80,128]{2,1,0:T(8,128)S(1)} all-to-all(f32[8,80,128]{2,1,0:T(8,128)S(1)} %spread.1), channel_id=1, replica_groups=mesh['zl'=2,'y'=8,'x'=4,'c'=2,'zh'=4] {'zl','zh'}, dimensions={0} | all-to-all | bytes 655360 | tf_op jit(solution)/shard_map/all_to_all | solution.py:648
  80.7 17.5 %all_to_all.27.in_ref = f32[8,80,128]{2,1,0:T(8,128)S(1)} all-to-all(f32[8,80,128]{2,1,0:T(8,128)S(1)} %collect.1), channel_id=1, replica_groups=mesh['zl'=2,'y'=8,'x'=4,'c'=2,'zh'=4] {'y'}, dimensions={0} | all-to-all | bytes 655360 | tf_op jit(solution)/shard_map/all_to_all | solution.py:650
  98.2 0.1 scale.1
  98.3 13.2 %all_to_all.28.in_ref = f32[8,72,128]{2,1,0:T(8,128)S(1)} all-to-all(f32[8,72,128]{2,1,0:T(8,128)S(1)} %scale.1), channel_id=1, replica_groups=mesh['zl'=2,'y'=8,'x'=4,'c'=2,'zh'=4] {'zl','zh'}, dimensions={0} | all-to-all | bytes 589824 | tf_op jit(solution)/shard_map/all_to_all | solution.py:655
  111.5 0.1 repack.1
  111.6 13.8 %all_to_all.29.own_ref = f32[4,12,48,128]{3,2,1,0:T(8,128)S(1)} all-to-all(f32[4,12,48,128]{3,2,1,0:T(8,128)S(1)} %repack.1), channel_id=1, replica_groups=mesh['zl'=2,'y'=8,'x'=4,'c'=2,'zh'=4] {'x'}, dimensions={0} | all-to-all | bytes 2359296 | tf_op jit(solution)/shard_map/all_to_all | solution.py:662
  125.4 8.0 %collective-permute-start.4 = (f32[4,12,48,128]{3,2,1,0:T(8,128)S(1)}, f32[4,12,48,128]{3,2,1,0:T(8,128)S(1)}, u32[]{:S(2)}, u32[]{:S(2)}) collective-permute-start(f32[4,12,48,128]{3,2,1,0:T(8,128)S(1)} %all_to_all.29.own_ref), channel_id=1, source_target_pairs={{0,4},{4,0},{1,5},{5,1},{2,6},{6,2},{3,7},{7,3},{8,12},{12,8},{9,1... | collective-permute-start | bytes 3538952 | tf_op jit(solution)/shard_map/ppermute | solution.py:663
  133.4 2.5 %collective-permute-done.4.other_ref = f32[4,12,48,128]{3,2,1,0:T(8,128)S(1)} collective-permute-done((f32[4,12,48,128]{3,2,1,0:T(8,128)S(1)}, f32[4,12,48,128]{3,2,1,0:T(8,128)S(1)}, u32[]{:S(2)}, u32[]{:S(2)}) %collective-permute-start.4) | collective-permute-done | bytes 1179680 | tf_op jit(solution)/shard_map/ppermute | solution.py:663
  135.8 1.5 %place.1 = f32[3,48,4096]{2,1,0:T(8,128)} custom-call(f32[4,12,48,128]{3,2,1,0:T(8,128)S(1)} %all_to_all.29.own_ref, f32[4,12,48,128]{3,2,1,0:T(8,128)S(1)} %collective-permute-done.4.other_ref), custom_call_target="tpu_custom_call" | custom-call | tf_op jit(solution)/shard_map/place/pallas_call | solution.py:664
  (4 shorter events, 0.1 us)
Async XLA Ops:
  0.8 6.0 %collective-permute-start = (f32[6,32,128]{2,1,0:T(8,128)S(1)}, f32[6,32,128]{2,1,0:T(8,128)S(1)}, u32[]{:S(2)}, u32[]{:S(2)}) collective-permute-start(f32[6,32,128]{2,1,0:T(8,128)S(1)} %pad_maximum_fusion), channel_id=1, source_target_pairs={{32,0},{64,32},{96,64},{128,96},{160,128},{192,160},{224,192},{256... | collective-permute-start | bytes 294920 | tf_op jit(solution)/shard_map/ppermute | solution.py:531
  2.1 1.3 copy-start
  3.4 1.3 copy-start.2
  4.7 11.5 %copy-start.4 = (s32[384]{0:T(512)S(1)}, s32[384]{0:T(512)}, u32[]{:S(2)}) copy-start(s32[384]{0:T(512)} %sx_smem.5) | copy-start | bytes 4612
  4.7 11.5 %copy-start.6 = (s32[512]{0:T(512)S(1)}, s32[512]{0:T(512)}, u32[]{:S(2)}) copy-start(s32[512]{0:T(512)} %param.11) | copy-start | bytes 6148
  4.7 11.5 %copy-start.7 = (s32[256]{0:T(256)S(1)}, s32[256]{0:T(256)}, u32[]{:S(2)}) copy-start(s32[256]{0:T(256)} %param.10) | copy-start | bytes 3076
  4.7 13.8 %copy-start.5 = (bf16[3,48,4096]{2,1,0:T(8,128)(2,1)S(1)}, bf16[3,48,4096]{2,1,0:T(8,128)(2,1)}, u32[]{:S(2)}) copy-start(bf16[3,48,4096]{2,1,0:T(8,128)(2,1)} %o_ref.1) | copy-start | bytes 3538948
  6.9 10.2 %collective-permute-start.1 = (f32[25,8,128]{2,1,0:T(8,128)S(1)}, f32[25,8,128]{2,1,0:T(8,128)S(1)}, u32[]{:S(2)}, u32[]{:S(2)}) collective-permute-start(f32[25,8,128]{2,1,0:T(8,128)S(1)} %widen.1), channel_id=1, source_target_pairs={{4,0},{8,4},{12,8},{16,12},{20,16},{24,20},{28,24},{5,1},{9,5},{13... | collective-permute-start | bytes 307208 | tf_op jit(solution)/shard_map/ppermute | solution.py:531
  17.2 9.8 %collective-permute-start.2 = (f32[6,40,128]{2,1,0:T(8,128)S(1)}, f32[6,40,128]{2,1,0:T(8,128)S(1)}, u32[]{:S(2)}, u32[]{:S(2)}) collective-permute-start(f32[6,40,128]{2,1,0:T(8,128)S(1)} %deepen.1), channel_id=1, source_target_pairs={{1,0},{2,1},{3,2},{5,4},{6,5},{7,6},{9,8},{10,9},{11,10},{13,12},{... | collective-permute-start | bytes 368648 | tf_op jit(solution)/shard_map/ppermute | solution.py:531
  18.5 8.5 %copy-start.1 = (f32[24,3,32,128]{3,2,1,0:T(8,128)S(1)}, f32[24,3,32,128]{3,2,1,0:T(8,128)}, u32[]{:S(2)}) copy-start(f32[24,3,32,128]{3,2,1,0:T(8,128)} %u_ref.3) | copy-start | bytes 3538948
  18.5 8.5 %copy-start.3 = (f32[24,3,32,128]{3,2,1,0:T(8,128)S(1)}, f32[24,3,32,128]{3,2,1,0:T(8,128)}, u32[]{:S(2)}) copy-start(f32[24,3,32,128]{3,2,1,0:T(8,128)} %w_ref.3) | copy-start | bytes 3538948
  44.2 4.2 %collective-permute-start.3 = (f32[1408,128]{1,0:T(8,128)S(1)}, f32[1408,128]{1,0:T(8,128)S(1)}, u32[]{:S(2)}, u32[]{:S(2)}) collective-permute-start(f32[1408,128]{1,0:T(8,128)S(1)} %get-tuple-element.24), channel_id=1, source_target_pairs={{0,4},{4,0},{1,5},{5,1},{2,6},{6,2},{3,7},{7,3},{8,12},{12,8},{9,1... | collective-permute-start | bytes 2162696 | tf_op jit(solution)/shard_map/ppermute | solution.py:638
  125.4 10.5 %collective-permute-start.4 = (f32[4,12,48,128]{3,2,1,0:T(8,128)S(1)}, f32[4,12,48,128]{3,2,1,0:T(8,128)S(1)}, u32[]{:S(2)}, u32[]{:S(2)}) collective-permute-start(f32[4,12,48,128]{3,2,1,0:T(8,128)S(1)} %all_to_all.29.own_ref), channel_id=1, source_target_pairs={{0,4},{4,0},{1,5},{5,1},{2,6},{6,2},{3,7},{7,3},{8,12},{12,8},{9,1... | collective-permute-start | bytes 3538952 | tf_op jit(solution)/shard_map/ppermute | solution.py:663
